TPU v7x, 128 devices: a whole 4x4x4 slice. The times are simulated.
128 devices in a mesh: row: 16 (over x, z_hi, core), col: 8 (over z_lo, y).
Axes of the slice: x: 4, y: 4, z: 4 (z_hi: 2, z_lo: 2; z = z_hi * 2 + z_lo), core: 2. Of those that a mesh axis runs over, the one named last changes fastest.
Arguments:
- source_vectors: float32 [1024, 73728], P(('row', 'col')), may hold values from -6 to 6
- source_slot: int32 [1024], P('col'), may hold values from 0 to 1023, as said below
- reflectors: float32 [73728, 1024], P('row'), may hold values from -6 to 6
- panel_offsets: int32 [16], replicated, may hold values from 0 to 18432
Outputs:
- vectors: float32 [1024, 73728], P('col', 'row')
Inputs may be any that keep to these rules, and one draw needn't show every extreme that they name: `source_slot`: A permutation of 0 .. 1023; for each c, the entries c * 128 .. (c + 1) * 128 - 1 are exactly the values s with (s // 8) % 8 == c.
All inputs are finite; a program needn't handle non-finite values.
Results may differ from a plain program's by a relative error of at most 0.0003.
Values sent between devices are 32-bit elements; how exact they have to be, the bound alone decides.
No kernel may reach another device: no remote copies, remote signals or barrier semaphores. Data moves between devices by JAX's collectives and lax.ppermute only.
A program may use at most 128 MiB of HBM per device.

v0:
```python
import jax
import jax.numpy as jnp
from jax import lax
from jax.sharding import PartitionSpec as P


def reflector_block(reflectors, panel_offsets, row_start, width):
    count = reflectors.shape[0]
    total = reflectors.shape[1]
    panels = panel_offsets.shape[0]
    rows = row_start + jnp.arange(count, dtype=jnp.int32)[:, None]
    columns = jnp.arange(total, dtype=jnp.int32)
    owner = jnp.arange(panels, dtype=jnp.int32)[:, None] == (columns // width)[None, :]
    lead = jnp.sum(jnp.where(owner, panel_offsets[:, None], 0), axis=0) + columns % width
    lead = lead[None, :]
    return jnp.where(rows < lead, 0.0, jnp.where(rows == lead, 1.0, reflectors))


def invert_upper(blocks):
    width = blocks.shape[-1]
    half = jnp.diagonal(blocks, axis1=1, axis2=2) / 2.0
    strict = jnp.triu(blocks, 1)
    power = -strict / half[:, :, None]
    identity = jnp.eye(width, dtype=blocks.dtype)[None, :, :]
    inverse = identity + power
    for level in range(max(1, (width - 1).bit_length()) - 1):
        power = jnp.einsum("nab,nbc->nac", power, power, precision=lax.Precision.HIGHEST)
        inverse = jnp.einsum(
            "nab,nbc->nac", inverse, identity + power, precision=lax.Precision.HIGHEST
        )
    return inverse / half[:, None, :]


def apply_panel(vectors, summed, panel, factor):
    weighted = jnp.dot(summed, factor.T, precision=lax.Precision.HIGHEST)
    change = lax.dot_general(
        weighted, panel, (((1,), (1,)), ((), ())), precision=lax.Precision.HIGHEST
    )
    return vectors - change


def per_device(source_vectors, source_slot, reflectors, panel_offsets):
    row_count = lax.axis_size("row")
    col_count = lax.axis_size("col")
    src_block = source_vectors.shape[0]
    rows_dev = reflectors.shape[0]
    total = reflectors.shape[1]
    panels = panel_offsets.shape[0]
    width = total // panels
    reflect = reflector_block(reflectors, panel_offsets, lax.axis_index("row") * rows_dev, width)
    paired = reflect.reshape(rows_dev, panels // 2, 2 * width)
    inner_local = jnp.einsum("rpa,rpb->pab", paired, paired, precision=lax.Precision.HIGHEST)
    inner = lax.psum(inner_local, "row")
    leading = reflect[:, total - width :]
    shaped = source_vectors.reshape(src_block, row_count, rows_dev)
    received = lax.all_to_all(shaped, "row", split_axis=1, concat_axis=1, tiled=True)
    received = received.reshape(src_block * row_count, rows_dev)
    partial_value = jnp.dot(received, leading, precision=lax.Precision.HIGHEST)
    placing = source_slot % src_block * row_count + source_slot // (col_count * src_block)
    vectors = jnp.take(received, placing, axis=0)
    partial_value = jnp.take(partial_value, placing, axis=0)
    summed = lax.psum(partial_value, "row")
    diagonal_blocks = jnp.stack([inner[:, :width, :width], inner[:, width:, width:]], axis=1)
    factors = invert_upper(diagonal_blocks.reshape(panels, width, width))
    vectors = apply_panel(vectors, summed, leading, factors[panels - 1])

    def panel_step(step, current):
        index = panels - 2 - step
        panel = lax.dynamic_slice_in_dim(reflect, index * width, width, 1)
        factor = lax.dynamic_index_in_dim(factors, index, keepdims=False)
        local = jnp.dot(current, panel, precision=lax.Precision.HIGHEST)
        product = lax.psum(local, "row")
        return apply_panel(current, product, panel, factor)

    return lax.fori_loop(0, panels - 1, panel_step, vectors)


def solution(mesh):
    in_specs = (P(("row", "col"), None), P("col"), P("row", None), P())
    out_specs = P("col", "row")
    return jax.shard_map(
        per_device, mesh=mesh, in_specs=in_specs, out_specs=out_specs, check_vma=False
    )
```

profile of v0, /device:TPU:1, one launch (start us, length us, event | category | flops | bytes accessed | tf_op | source)
XLA Modules:
  0.0 1456.0 jit_solution(4660716329826489066)
XLA Ops:
  7.3 42.0 %fusion.12 = f32[8,128,128]{2,1,0:T(8,128)} fusion(f32[4608,1024]{1,0:T(8,128)} %param.8, s32[1024]{0:T(1024)S(1)} %fusion.43, s32[4608]{0:T(1024)S(1)} %iota_add_fusion), kind=kOutput, calls=%fused_computation.14 | convolution fusion | flops 7266631680 | bytes 19421184 | tf_op jit(solution)/shard_map/rpa,rpb->pab/dot_general | solution.py:52
  49.3 9.1 all-to-all-start
  58.5 15.6 %select_select_fusion = f32[4608,1024]{1,0:T(8,128)} fusion(f32[4608,1024]{1,0:T(8,128)} %param.8, s32[1024]{0:T(1024)S(1)} %fusion.43, s32[4608]{0:T(1024)S(1)} %iota_add_fusion), kind=kLoop, calls=%fused_computation.17 | loop fusion | flops 18874368 | bytes 37771264 | tf_op jit(solution)/shard_map/jit(_where)/select_n | solution.py:16
  74.1 129.3 %all-reduce.2.cloned.1.call-done = f32[8,128,128]{2,1,0:T(8,128)} async-done(((f32[8,128,128]{2,1,0:T(8,128)}), f32[8,128,128]{2,1,0:T(8,128)}) %all-reduce.2.cloned.1.call-update) | async-done | bytes 524304 | tf_op jit(solution)/shard_map/psum | solution.py:53
  216.2 6.5 fusion.18
  226.2 64.9 %psum.28 = f32[128,64]{1,0:T(8,128)S(1)} all-reduce(f32[128,64]{1,0:T(8,128)S(1)} %broadcast_select_fusion), channel_id=1, replica_groups=mesh['row'=16,'col'=8] {'row'}, use_global_device_ids=true, to_apply=%region_1.2 | all-reduce | flops 8192 | bytes 65536 | tf_op jit(solution)/shard_map/psum | solution.py:62
  296.8 1150.9 %while.15 = (s32[]{:T(128)}, f32[128,4608]{1,0:T(8,128)S(1)}, f32[4608,1024]{1,0:T(8,128)}, f32[16,64,64]{2,1,0:T(8,128)S(1)}, s32[]{:T(128)}, /*index=5*/s32[]{:T(128)}, s32[]{:T(128)}, s32[]{:T(128)}, s32[]{:T(128)}, s32[]{:T(128)}) while((s32[]{:T(128)}, f32[128,4608]{1,0:T(8,128)S(1)}, f32[4608,1024]{1,0:T(8,128)}, ...), condition=%wide.region_5.6_spmd, body=%wide.region_3.5_spmd.sunk | while | flops 912859136 | bytes 12026061 | solution.py:75
  296.9 6.3 fusion.86
  303.1 64.9 %psum.31 = f32[128,64]{0,1:T(8,128)S(1)} all-reduce(f32[128,64]{0,1:T(8,128)S(1)} %fusion.86), channel_id=1, replica_groups=mesh['row'=16,'col'=8] {'row'}, use_global_device_ids=true, to_apply=%region_4.4 | all-reduce | flops 8192 | bytes 65536 | tf_op jit(solution)/shard_map/while/body/eval_jaxpr/psum | solution.py:72
  373.6 6.3 fusion.86
  379.9 64.9 %psum.31 = f32[128,64]{0,1:T(8,128)S(1)} all-reduce(f32[128,64]{0,1:T(8,128)S(1)} %fusion.86), channel_id=1, replica_groups=mesh['row'=16,'col'=8] {'row'}, use_global_device_ids=true, to_apply=%region_4.4 | all-reduce | flops 8192 | bytes 65536 | tf_op jit(solution)/shard_map/while/body/eval_jaxpr/psum | solution.py:72
  450.3 6.3 fusion.86
  456.6 64.9 %psum.31 = f32[128,64]{0,1:T(8,128)S(1)} all-reduce(f32[128,64]{0,1:T(8,128)S(1)} %fusion.86), channel_id=1, replica_groups=mesh['row'=16,'col'=8] {'row'}, use_global_device_ids=true, to_apply=%region_4.4 | all-reduce | flops 8192 | bytes 65536 | tf_op jit(solution)/shard_map/while/body/eval_jaxpr/psum | solution.py:72
  527.0 6.3 fusion.86
  533.3 64.9 %psum.31 = f32[128,64]{0,1:T(8,128)S(1)} all-reduce(f32[128,64]{0,1:T(8,128)S(1)} %fusion.86), channel_id=1, replica_groups=mesh['row'=16,'col'=8] {'row'}, use_global_device_ids=true, to_apply=%region_4.4 | all-reduce | flops 8192 | bytes 65536 | tf_op jit(solution)/shard_map/while/body/eval_jaxpr/psum | solution.py:72
  603.8 6.3 fusion.86
  610.0 64.9 %psum.31 = f32[128,64]{0,1:T(8,128)S(1)} all-reduce(f32[128,64]{0,1:T(8,128)S(1)} %fusion.86), channel_id=1, replica_groups=mesh['row'=16,'col'=8] {'row'}, use_global_device_ids=true, to_apply=%region_4.4 | all-reduce | flops 8192 | bytes 65536 | tf_op jit(solution)/shard_map/while/body/eval_jaxpr/psum | solution.py:72
  686.8 64.9 %psum.31 = f32[128,64]{0,1:T(8,128)S(1)} all-reduce(f32[128,64]{0,1:T(8,128)S(1)} %fusion.86), channel_id=1, replica_groups=mesh['row'=16,'col'=8] {'row'}, use_global_device_ids=true, to_apply=%region_4.4 | all-reduce | flops 8192 | bytes 65536 | tf_op jit(solution)/shard_map/while/body/eval_jaxpr/psum | solution.py:72
  757.2 6.3 fusion.86
  763.5 64.9 %psum.31 = f32[128,64]{0,1:T(8,128)S(1)} all-reduce(f32[128,64]{0,1:T(8,128)S(1)} %fusion.86), channel_id=1, replica_groups=mesh['row'=16,'col'=8] {'row'}, use_global_device_ids=true, to_apply=%region_4.4 | all-reduce | flops 8192 | bytes 65536 | tf_op jit(solution)/shard_map/while/body/eval_jaxpr/psum | solution.py:72
  840.2 64.9 %psum.31 = f32[128,64]{0,1:T(8,128)S(1)} all-reduce(f32[128,64]{0,1:T(8,128)S(1)} %fusion.86), channel_id=1, replica_groups=mesh['row'=16,'col'=8] {'row'}, use_global_device_ids=true, to_apply=%region_4.4 | all-reduce | flops 8192 | bytes 65536 | tf_op jit(solution)/shard_map/while/body/eval_jaxpr/psum | solution.py:72
  910.6 6.3 fusion.86
  916.9 64.9 %psum.31 = f32[128,64]{0,1:T(8,128)S(1)} all-reduce(f32[128,64]{0,1:T(8,128)S(1)} %fusion.86), channel_id=1, replica_groups=mesh['row'=16,'col'=8] {'row'}, use_global_device_ids=true, to_apply=%region_4.4 | all-reduce | flops 8192 | bytes 65536 | tf_op jit(solution)/shard_map/while/body/eval_jaxpr/psum | solution.py:72
  993.7 64.9 %psum.31 = f32[128,64]{0,1:T(8,128)S(1)} all-reduce(f32[128,64]{0,1:T(8,128)S(1)} %fusion.86), channel_id=1, replica_groups=mesh['row'=16,'col'=8] {'row'}, use_global_device_ids=true, to_apply=%region_4.4 | all-reduce | flops 8192 | bytes 65536 | tf_op jit(solution)/shard_map/while/body/eval_jaxpr/psum | solution.py:72
  1064.1 6.3 fusion.86
  1070.4 64.9 %psum.31 = f32[128,64]{0,1:T(8,128)S(1)} all-reduce(f32[128,64]{0,1:T(8,128)S(1)} %fusion.86), channel_id=1, replica_groups=mesh['row'=16,'col'=8] {'row'}, use_global_device_ids=true, to_apply=%region_4.4 | all-reduce | flops 8192 | bytes 65536 | tf_op jit(solution)/shard_map/while/body/eval_jaxpr/psum | solution.py:72
  1147.1 64.9 %psum.31 = f32[128,64]{0,1:T(8,128)S(1)} all-reduce(f32[128,64]{0,1:T(8,128)S(1)} %fusion.86), channel_id=1, replica_groups=mesh['row'=16,'col'=8] {'row'}, use_global_device_ids=true, to_apply=%region_4.4 | all-reduce | flops 8192 | bytes 65536 | tf_op jit(solution)/shard_map/while/body/eval_jaxpr/psum | solution.py:72
  1217.5 6.3 fusion.86
  1223.8 64.9 %psum.31 = f32[128,64]{0,1:T(8,128)S(1)} all-reduce(f32[128,64]{0,1:T(8,128)S(1)} %fusion.86), channel_id=1, replica_groups=mesh['row'=16,'col'=8] {'row'}, use_global_device_ids=true, to_apply=%region_4.4 | all-reduce | flops 8192 | bytes 65536 | tf_op jit(solution)/shard_map/while/body/eval_jaxpr/psum | solution.py:72
  1300.6 64.9 %psum.31 = f32[128,64]{0,1:T(8,128)S(1)} all-reduce(f32[128,64]{0,1:T(8,128)S(1)} %fusion.86), channel_id=1, replica_groups=mesh['row'=16,'col'=8] {'row'}, use_global_device_ids=true, to_apply=%region_4.4 | all-reduce | flops 8192 | bytes 65536 | tf_op jit(solution)/shard_map/while/body/eval_jaxpr/psum | solution.py:72
  1371.0 6.3 fusion.86
  1377.3 64.9 %psum.31 = f32[128,64]{0,1:T(8,128)S(1)} all-reduce(f32[128,64]{0,1:T(8,128)S(1)} %fusion.86), channel_id=1, replica_groups=mesh['row'=16,'col'=8] {'row'}, use_global_device_ids=true, to_apply=%region_4.4 | all-reduce | flops 8192 | bytes 65536 | tf_op jit(solution)/shard_map/while/body/eval_jaxpr/psum | solution.py:72
  (74 shorter events, 137.3 us)
Async XLA Ops:
  6.5 196.9 %all-reduce.2.cloned.1.call-start = ((), (), s32[]{:S(2)}) async-start(), calls=%async_computation.1 | async-start | bytes 1048576 | tf_op jit(solution)/shard_map/psum | solution.py:53
  49.3 163.8 %all-to-all-start = ((f32[8,16,4608]{2,0,1:T(8,128)}), f32[8,16,4608]{2,0,1:T(8,128)}, u32[]{:S(2)}, u32[]{:S(2)}) async-start(f32[8,16,4608]{2,0,1:T(8,128)} %bitcast.2), calls=%async_computation | async-start | bytes 4718592 | tf_op jit(solution)/shard_map/all_to_all | solution.py:56
  58.5 15.6 %copy-start.1 = (s32[128]{0:T(128)S(1)}, s32[128]{0:T(128)}, u32[]{:S(2)}) copy-start(s32[128]{0:T(128)} %param.7) | copy-start | bytes 1540
  1447.7 1.4 copy-start
Sparse Core Ops, SparseCore 0:
  49.5 153.8 all-reduce.1
where the time goes:
time: 1460 us
  blocking collectives  1040 us (71%)
  matrix products  237 us (16%)
  waiting for transfers between devices  129 us (9%)
  other arithmetic  16.5 us (1%)
    psum x15, blocking collectives, panel_step(): product = lax.psum(local, 'row')  974 us
    psum x1, waiting for transfers between devices, per_device(): inner = lax.psum(inner_local, 'row')  129 us
    dot_general x15, matrix products, panel_step(): local = jnp.dot(current, panel, precision=lax.Precision.HIGHEST)  94.3 us
    dot_general x16, matrix products, apply_panel(): lax.dot_general(weighted, panel, (((1,), (1,)), ((), ())), precision=lax....  84.9 us
    psum x1, blocking collectives, per_device(): summed = lax.psum(partial_value, 'row')  64.9 us
    dot_general x1, matrix products, per_device(): jnp.einsum('rpa,rpb->pab', paired, paired, precision=lax.Precision.HIGHEST)  42 us
  transfers between devices with their start and end apart: 2, of which 1 were waited for; matrix products, arithmetic and copies ran while one was open for 2% of the time, Pallas kernels for 0%

commit v1 on v0

v1 whole, which is shorter than its diff:
```python
import functools

import jax
import jax.numpy as jnp
from jax import lax
from jax.experimental import pallas as pl
from jax.experimental.pallas import tpu as pltpu
from jax.sharding import PartitionSpec as P

F32 = jnp.float32
BF16 = jnp.bfloat16
TILE = 512
BLOCK = 128


def halves(x):
    high = x.astype(BF16)
    return high, (x - high.astype(F32)).astype(BF16)


def dot(a, b, ca=1, cb=0):
    return lax.dot_general(a, b, (((ca,), (cb,)), ((), ())), preferred_element_type=F32)


def dot3(a, b, ca=1, cb=0):
    ah, al = halves(a)
    bh, bl = halves(b)
    return dot(ah, bh, ca, cb) + (dot(ah, bl, ca, cb) + dot(al, bh, ca, cb))


def basis_halves(tile_ref, lead_ref, first_row):
    x = tile_ref[...]
    rows = first_row + lax.broadcasted_iota(jnp.int32, x.shape, 0)
    lead = lead_ref[...]
    return halves(jnp.where(rows < lead, 0.0, jnp.where(rows == lead, 1.0, x)))


def gram_kernel(place_ref, lead_ref, tile_ref, out_ref, high_ref, low_ref):
    step = pl.program_id(0)
    tile = tile_ref.shape[0]
    high, low = basis_halves(tile_ref, lead_ref, place_ref[0] + step * tile)
    high_ref[...] = high
    low_ref[...] = low
    mine = pl.ds(pl.multiple_of(place_ref[1] * BLOCK, BLOCK), BLOCK)
    left = jnp.concatenate([high_ref[:, mine], low_ref[:, mine]], axis=1)
    both = dot(left, high, 0, 0)
    total = both[:BLOCK] + (both[BLOCK:] + dot(left[:, :BLOCK], low, 0, 0))

    @pl.when(step == 0)
    def _():
        out_ref[...] = total

    @pl.when(step > 0)
    def _():
        out_ref[...] += total


def product_kernel(place_ref, lead_ref, vec_ref, tile_ref, out_ref):
    step = pl.program_id(0)
    tile = tile_ref.shape[0]
    high, low = basis_halves(tile_ref, lead_ref, place_ref[0] + step * tile)
    vh, vl = halves(vec_ref[...])
    count = vh.shape[0]
    both = dot(jnp.concatenate([vh, vl], axis=0), high)
    total = both[:count] + (both[count:] + dot(vh, low))

    @pl.when(step == 0)
    def _():
        out_ref[...] = total

    @pl.when(step > 0)
    def _():
        out_ref[...] += total


def inverse_kernel(gram_ref, out_ref, low_ref):
    total = out_ref.shape[0]
    blocks = total // BLOCK
    r = lax.broadcasted_iota(jnp.int32, (BLOCK, BLOCK), 0)
    c = lax.broadcasted_iota(jnp.int32, (BLOCK, BLOCK), 1)
    for q in range(blocks):
        low_ref[q * BLOCK : (q + 1) * BLOCK, :] = gram_ref[:, q].reshape(BLOCK, total)
    out_ref[...] = jnp.zeros_like(out_ref)
    lows, inverses = [], []
    for q in range(blocks):
        part = pl.ds(q * BLOCK, BLOCK)
        square = low_ref[part, part]
        lows.append(square)
        inverses.append(jnp.where(r == c, 2.0 / square, 0.0))
    size = 1
    while size < BLOCK:
        pair = (r // (2 * size) == c // (2 * size)) & (r // size > c // size)
        mids = [dot3(jnp.where(pair, lows[q], 0.0), inverses[q]) for q in range(blocks)]
        inverses = [inverses[q] - dot3(inverses[q], mids[q]) for q in range(blocks)]
        size *= 2
    for q in range(blocks):
        part = pl.ds(q * BLOCK, BLOCK)
        out_ref[part, part] = inverses[q]
    while size < total:
        for start in range(0, total, 2 * size):
            a, b = pl.ds(start, size), pl.ds(start + size, size)
            mid = dot3(low_ref[b, a], out_ref[a, a])
            out_ref[b, a] = -dot3(out_ref[b, b], mid)
        size *= 2


def change_kernel(
    place_ref, lead_ref, order_ref, summed_ref, inverse_ref, vec_ref, tile_ref, out_ref, wh_ref, wl_ref
):
    step = pl.program_id(0)
    tile = tile_ref.shape[0]
    count = vec_ref.shape[0]

    @pl.when(step == 0)
    def _():
        wh, wl = halves(dot3(summed_ref[...], inverse_ref[...]))
        wh_ref[...] = wh
        wl_ref[...] = wl

    high, low = basis_halves(tile_ref, lead_ref, place_ref[0] + step * tile)
    wh = wh_ref[...]
    both = dot(jnp.concatenate([wh, wl_ref[...]], axis=0), high, 1, 1)
    value = vec_ref[...] - (both[:count] + (both[count:] + dot(wh, low, 1, 1)))
    v1 = value.astype(BF16)
    rest = value - v1.astype(F32)
    v2 = rest.astype(BF16)
    v3 = (rest - v2.astype(F32)).astype(BF16)
    order = order_ref[...]
    out_ref[...] = dot(order, v1) + (dot(order, v2) + dot(order, v3))


def params(mib):
    return pltpu.CompilerParams(vmem_limit_bytes=mib << 20)


def per_device(source_vectors, source_slot, reflectors, panel_offsets):
    row_count = lax.axis_size("row")
    col_count = lax.axis_size("col")
    src_block = source_vectors.shape[0]
    rows_dev, total = reflectors.shape
    width = total // panel_offsets.shape[0]
    count = src_block * row_count
    steps = rows_dev // TILE

    place = jnp.stack([lax.axis_index("row") * rows_dev, lax.axis_index("col")]).astype(jnp.int32)
    lead = (panel_offsets[:, None] + jnp.arange(width, dtype=jnp.int32)[None, :]).reshape(1, total)
    placing = source_slot // (col_count * src_block) * src_block + source_slot % src_block
    order = (placing[:, None] == jnp.arange(count, dtype=jnp.int32)[None, :]).astype(BF16)

    smem = pl.BlockSpec(memory_space=pltpu.SMEM)
    lead_spec = pl.BlockSpec((1, total), lambda i: (0, 0))
    tile_spec = pl.BlockSpec((TILE, total), lambda i: (i, 0))
    vec_spec = pl.BlockSpec((count, TILE), lambda i: (0, i))

    def whole(shape):
        return pl.BlockSpec(shape, lambda i: tuple(0 for _ in shape))

    shaped = source_vectors.reshape(src_block, row_count, rows_dev).transpose(1, 0, 2)
    received = lax.all_to_all(shaped, "row", 0, 0, tiled=True).reshape(count, rows_dev)

    gram = pl.pallas_call(
        gram_kernel,
        grid=(steps,),
        in_specs=[smem, lead_spec, tile_spec],
        out_specs=whole((BLOCK, total)),
        out_shape=jax.ShapeDtypeStruct((BLOCK, total), F32),
        scratch_shapes=[pltpu.VMEM((TILE, total), BF16), pltpu.VMEM((TILE, total), BF16)],
        compiler_params=params(24),
        cost_estimate=pl.CostEstimate(
            flops=6 * rows_dev * BLOCK * total, bytes_accessed=4 * rows_dev * total, transcendentals=0
        ),
        name="gram",
    )(place, lead, reflectors)
    pieces = lax.all_to_all(gram.reshape(row_count, BLOCK // row_count, total), "row", 0, 0, tiled=True)
    piece = jnp.sum(pieces, axis=0)
    everyone = row_count * col_count
    spread = jnp.broadcast_to(piece[None], (everyone,) + piece.shape)
    grams = lax.all_to_all(spread, ("row", "col"), 0, 0, tiled=True)
    grams = grams.reshape(row_count, col_count, BLOCK // row_count, total)
    inverse = pl.pallas_call(
        inverse_kernel,
        out_shape=jax.ShapeDtypeStruct((total, total), F32),
        scratch_shapes=[pltpu.VMEM((total, total), F32)],
        compiler_params=params(32),
        cost_estimate=pl.CostEstimate(flops=2 * total**3, bytes_accessed=8 * total**2, transcendentals=0),
        name="inverse",
    )(grams)

    partial_value = pl.pallas_call(
        product_kernel,
        grid=(steps,),
        in_specs=[smem, lead_spec, vec_spec, tile_spec],
        out_specs=whole((count, total)),
        out_shape=jax.ShapeDtypeStruct((count, total), F32),
        compiler_params=params(24),
        cost_estimate=pl.CostEstimate(
            flops=6 * rows_dev * count * total, bytes_accessed=4 * rows_dev * (total + count), transcendentals=0
        ),
        name="product",
    )(place, lead, received, reflectors)
    parts = lax.all_to_all(partial_value.reshape(row_count, src_block, total), "row", 0, 0, tiled=True)
    mine = jnp.sum(parts, axis=0)
    spread = jnp.broadcast_to(mine[None], (row_count,) + mine.shape)
    summed = lax.all_to_all(spread, "row", 0, 0, tiled=True).reshape(count, total)

    return pl.pallas_call(
        change_kernel,
        grid=(steps,),
        in_specs=[smem, lead_spec, whole((count, count)), whole((count, total)), whole((total, total)), vec_spec, tile_spec],
        out_specs=vec_spec,
        out_shape=jax.ShapeDtypeStruct((count, rows_dev), F32),
        scratch_shapes=[pltpu.VMEM((count, total), BF16), pltpu.VMEM((count, total), BF16)],
        compiler_params=params(32),
        cost_estimate=pl.CostEstimate(
            flops=6 * rows_dev * count * total, bytes_accessed=4 * rows_dev * (total + 2 * count), transcendentals=0
        ),
        name="change",
    )(place, lead, order, summed, inverse, received, reflectors)


def solution(mesh):
    in_specs = (P(("row", "col"), None), P("col"), P("row", None), P())
    out_specs = P("col", "row")
    return jax.shard_map(per_device, mesh=mesh, in_specs=in_specs, out_specs=out_specs, check_vma=False)
```

time: 1460 us -> 182 us (0.12)
  blocking collectives: 1040 us -> 0 us
  matrix products: 237 us -> 0 us
  waiting for transfers between devices: 129 us -> 74.3 us
  Pallas kernels: 0 us -> 52.2 us
  starting transfers between devices: 9.14 us -> 33.5 us
  other arithmetic: 16.5 us -> 0.31 us
    psum x16 -> x0, blocking collectives: 1040 us -> none  [the longest x15 974 us: panel_step(): product = lax.psum(local, 'row')]
    dot_general x59 -> x0, matrix products: 237 us -> none  [the longest x15 94.3 us: panel_step(): local = jnp.dot(current, panel, precision=lax.Precision.HIGHEST)]
    psum x1 -> x0, waiting for transfers between devices: 129 us -> none  [per_device(): inner = lax.psum(inner_local, 'row')]
    all_to_all x1 -> x5, waiting for transfers between devices: 0.01 us -> 74.3 us  [the longest x1 54.4 us: per_device(): grams = lax.all_to_all(spread, ('row', 'col'), 0, 0, tiled=True)]
    pallas_call x0 -> x4, Pallas kernels: none -> 52.2 us  [the longest x1 17.1 us: per_device(): pl.pallas_call(change_kernel, grid=(steps,), in_specs=[smem, lead_spec, w...]
    all_to_all x1 -> x5, starting transfers between devices: 9.14 us -> 33.5 us  [the longest x1 9.26 us: per_device(): lax.all_to_all(shaped, 'row', 0, 0, tiled=True).reshape(count, rows_dev)]
    select_n x3 -> x0, other arithmetic: 15.6 us -> none  [the longest x1 15.6 us: reflector_block(): return jnp.where(rows < lead, 0.0, jnp.where(rows == lead, 1.0, reflectors))]
    unnamed x4 -> x12, local copies, waits for them, and re-layouts: 1.4 us -> 16.9 us
  transfers between devices with their start and end apart: 2 -> 5, of which waited for: 1 -> 4; matrix products, arithmetic and copies ran while one was open for 2% -> 0% of each run, Pallas kernels for 0% -> 19%
where the time goes in v1:
time: 182 us; the launch traced here: 181 us
  waiting for transfers between devices  74.3 us (41%)
  Pallas kernels  52.2 us (29%)
  starting transfers between devices  33.5 us (18%)
  local copies, waits for them, and re-layouts  20.3 us (11%)
    all_to_all x1, waiting for transfers between devices, per_device(): grams = lax.all_to_all(spread, ('row', 'col'), 0, 0, tiled=True)  54.4 us
    pallas_call x1, Pallas kernels, per_device(): pl.pallas_call(change_kernel, grid=(steps,), in_specs=[smem, lead_spec, w...  17.1 us
    unnamed x12, local copies, waits for them, and re-layouts  16.9 us
    pallas_call x1, Pallas kernels, per_device(): pl.pallas_call(gram_kernel, grid=(steps,), in_specs=[smem, lead_spec, til...  16.5 us
    all_to_all x1, waiting for transfers between devices, per_device(): lax.all_to_all(partial_value.reshape(row_count, src_block, total), 'row',...  11.1 us
    pallas_call x1, Pallas kernels, per_device(): pl.pallas_call(product_kernel, grid=(steps,), in_specs=[smem, lead_spec,...  10.2 us
    all_to_all x1, starting transfers between devices, per_device(): lax.all_to_all(shaped, 'row', 0, 0, tiled=True).reshape(count, rows_dev)  9.26 us
    pallas_call x1, Pallas kernels, per_device(): pl.pallas_call(inverse_kernel, out_shape=jax.ShapeDtypeStruct((total, tot...  8.36 us
  transfers between devices with their start and end apart: 5, of which 4 were waited for; matrix products, arithmetic and copies ran while one was open for 0% of the time, Pallas kernels for 19%

profile of v1, /device:TPU:1, one launch (start us, length us, event | category | flops | bytes accessed | tf_op | source)
XLA Modules:
  0.0 180.7 jit_solution(9346156254440576775)
XLA Ops:
  0.0 0.0 copy-start.4
  0.0 9.3 %all-to-all-start = ((f32[16,8,4608]{2,1,0:T(8,128)}), f32[16,8,4608]{2,1,0:T(8,128)S(1)}, u32[]{:S(2)}, u32[]{:S(2)}) async-start(f32[16,8,4608]{2,1,0:T(8,128)} %bitcast.13), calls=%async_computation | async-start | bytes 4718592 | tf_op jit(solution)/shard_map/all_to_all | solution.py:159
  9.3 0.0 copy-done.4
  9.3 0.1 iota_add_fusion
  9.3 0.1 add.36.lead_ref
  9.4 0.1 pad_add_fusion.place_ref
  9.5 0.0 copy-start
  9.5 6.4 %copy-done = f32[4608,1024]{1,0:T(8,128)S(1)} copy-done((f32[4608,1024]{1,0:T(8,128)S(1)}, f32[4608,1024]{1,0:T(8,128)}, u32[]{:S(2)}) %copy-start) | copy-done | bytes 18874392
  15.9 16.5 %gram.1 = f32[128,1024]{1,0:T(8,128)} custom-call(s32[2]{0:T(128)S(1)} %pad_add_fusion.place_ref, s32[1,1024]{1,0:T(1,128)S(1)} %add.36.lead_ref, f32[4608,1024]{1,0:T(8,128)S(1)} %copy-done), custom_call_target="tpu_custom_call" | custom-call | flops 3623878656 | bytes 18874368 | tf_op jit(solution)/shard_map/gram/pallas_call | solution.py:161
  32.4 8.2 %all-to-all-done = f32[16,8,4608]{2,1,0:T(8,128)S(1)} async-done(((f32[16,8,4608]{2,1,0:T(8,128)}), f32[16,8,4608]{2,1,0:T(8,128)S(1)}, u32[]{:S(2)}, u32[]{:S(2)}) %all-to-all-start) | async-done | bytes 2359328 | tf_op jit(solution)/shard_map/all_to_all | solution.py:159
  40.5 6.4 %all-to-all-start.3 = ((f32[16,8,1024]{2,1,0:T(8,128)}), f32[16,8,1024]{2,1,0:T(8,128)S(1)}, u32[]{:S(2)}, u32[]{:S(2)}) async-start(f32[16,8,1024]{2,1,0:T(8,128)} %bitcast.7), calls=%async_computation.3 | async-start | bytes 1048576 | tf_op jit(solution)/shard_map/all_to_all | solution.py:174
  46.9 0.0 copy-start.1
  46.9 6.4 %copy-done.1 = f32[4608,1024]{1,0:T(8,128)S(1)} copy-done((f32[4608,1024]{1,0:T(8,128)S(1)}, f32[4608,1024]{1,0:T(8,128)}, u32[]{:S(2)}) %copy-start.1) | copy-done | bytes 18874392
  53.2 10.2 %product.1 = f32[128,1024]{1,0:T(8,128)} custom-call(s32[2]{0:T(128)S(1)} %pad_add_fusion.place_ref, s32[1,1024]{1,0:T(1,128)S(1)} %add.36.lead_ref, f32[128,4608]{1,0:T(8,128)S(1)} %bitcast.10, f32[4608,1024]{1,0:T(8,128)S(1)} %copy-done.1), custom_call_target="tpu_custom_call" | custom-call | flops 3623878656 | bytes 21233664 | tf_op jit(solution)/shard_map/product/pallas_call | solution.py:189
  63.5 0.0 all-to-all-done.3
  63.5 7.2 %all-to-all-start.1 = ((f32[16,8,1024]{2,1,0:T(8,128)}), f32[16,8,1024]{2,1,0:T(8,128)S(1)}, u32[]{:S(2)}, u32[]{:S(2)}) async-start(f32[16,8,1024]{2,1,0:T(8,128)} %bitcast.5), calls=%async_computation.1 | async-start | bytes 1048576 | tf_op jit(solution)/shard_map/all_to_all | solution.py:201
  70.7 11.1 %all-to-all-done.1 = f32[16,8,1024]{2,1,0:T(8,128)S(1)} async-done(((f32[16,8,1024]{2,1,0:T(8,128)}), f32[16,8,1024]{2,1,0:T(8,128)S(1)}, u32[]{:S(2)}, u32[]{:S(2)}) %all-to-all-start.1) | async-done | bytes 524320 | tf_op jit(solution)/shard_map/all_to_all | solution.py:201
  81.8 2.5 %broadcast_in_dim.5 = f32[128,8,1024]{2,1,0:T(8,128)} broadcast(f32[8,1024]{1,0:T(8,128)S(1)} %reduce_sum.19), dimensions={1,2} | broadcast | bytes 4227072 | tf_op jit(solution)/shard_map/broadcast_in_dim | solution.py:177
  84.3 0.0 copy-start.5
  84.3 6.7 %all-to-all-start.4 = ((f32[128,8,1024]{2,1,0:T(8,128)}), f32[128,8,1024]{2,1,0:T(8,128)}, u32[]{:S(2)}, u32[]{:S(2)}) async-start(f32[128,8,1024]{2,1,0:T(8,128)} %broadcast_in_dim.5), calls=%async_computation.4 | async-start | bytes 8388608 | tf_op jit(solution)/shard_map/all_to_all | solution.py:178
  91.1 54.4 %all-to-all-done.4 = f32[128,8,1024]{2,1,0:T(8,128)} async-done(((f32[128,8,1024]{2,1,0:T(8,128)}), f32[128,8,1024]{2,1,0:T(8,128)}, u32[]{:S(2)}, u32[]{:S(2)}) %all-to-all-start.4) | async-done | bytes 4194336 | tf_op jit(solution)/shard_map/all_to_all | solution.py:178
  145.5 0.8 broadcast_in_dim.4
  146.3 3.9 %all-to-all-start.2 = ((f32[16,8,1024]{2,1,0:T(8,128)}), f32[16,8,1024]{2,1,0:T(8,128)S(1)}, u32[]{:S(2)}, u32[]{:S(2)}) async-start(f32[16,8,1024]{2,1,0:T(8,128)} %broadcast_in_dim.4), calls=%async_computation.2 | async-start | bytes 1048576 | tf_op jit(solution)/shard_map/all_to_all | solution.py:204
  150.2 0.0 copy-done.5
  150.3 0.1 fusion.order_ref
  150.3 8.4 %inverse.1.inverse_ref = f32[1024,1024]{1,0:T(8,128)S(1)} custom-call(f32[16,8,8,1024]{3,2,1,0:T(8,128)} %bitcast.8.gram_ref), custom_call_target="tpu_custom_call" | custom-call | flops 2147483648 | bytes 8388608 | tf_op jit(solution)/shard_map/inverse/pallas_call | solution.py:180
  158.7 0.0 copy-start.2
  158.7 1.9 %copy-done.2 = f32[1024,1024]{1,0:T(8,128)} copy-done((f32[1024,1024]{1,0:T(8,128)}, f32[1024,1024]{1,0:T(8,128)S(1)}, u32[]{:S(2)}) %copy-start.2) | copy-done | bytes 4194328
  160.7 0.7 all-to-all-done.2
  161.4 0.0 copy-start.3
  161.4 2.2 %copy-done.3 = f32[1024,1024]{1,0:T(8,128)S(1)} copy-done((f32[1024,1024]{1,0:T(8,128)S(1)}, f32[1024,1024]{1,0:T(8,128)}, u32[]{:S(2)}) %copy-start.3) | copy-done | bytes 4194328
  163.6 17.1 %change.1 = f32[128,4608]{1,0:T(8,128)} custom-call(s32[2]{0:T(128)S(1)} %pad_add_fusion.place_ref, s32[1,1024]{1,0:T(1,128)S(1)} %add.36.lead_ref, bf16[128,128]{1,0:T(8,128)(2,1)S(1)} %fusion.order_ref, f32[128,1024]{1,0:T(8,128)S(1)} %bitcast.12, f32[1024,1024]{1,0:T(8,128)S(1)} %copy-done.3, f32[128,4608]{1,0:T(8,128)S(1)} %bitcast.11, f32[4608,1024]{1,0:T(8,128)} %tile_ref.5), custom_call_target="tpu_custom_call" | custom-call | flops 3623878656 | bytes 23592960 | tf_op jit(solution)/shard_map/change/pallas_call | solution.py:206
  (3 shorter events, 0.1 us)
Async XLA Ops:
  0.0 9.3 %copy-start.4 = (s32[16]{0:T(128)S(1)}, s32[16]{0:T(128)}, u32[]{:S(2)}) copy-start(s32[16]{0:T(128)} %param.7) | copy-start | bytes 196
  0.0 40.5 %all-to-all-start = ((f32[16,8,4608]{2,1,0:T(8,128)}), f32[16,8,4608]{2,1,0:T(8,128)S(1)}, u32[]{:S(2)}, u32[]{:S(2)}) async-start(f32[16,8,4608]{2,1,0:T(8,128)} %bitcast.13), calls=%async_computation | async-start | bytes 4718592 | tf_op jit(solution)/shard_map/all_to_all | solution.py:159
  9.5 6.4 %copy-start = (f32[4608,1024]{1,0:T(8,128)S(1)}, f32[4608,1024]{1,0:T(8,128)}, u32[]{:S(2)}) copy-start(f32[4608,1024]{1,0:T(8,128)} %tile_ref.5) | copy-start | bytes 56623108
  40.5 22.9 %all-to-all-start.3 = ((f32[16,8,1024]{2,1,0:T(8,128)}), f32[16,8,1024]{2,1,0:T(8,128)S(1)}, u32[]{:S(2)}, u32[]{:S(2)}) async-start(f32[16,8,1024]{2,1,0:T(8,128)} %bitcast.7), calls=%async_computation.3 | async-start | bytes 1048576 | tf_op jit(solution)/shard_map/all_to_all | solution.py:174
  46.9 6.4 %copy-start.1 = (f32[4608,1024]{1,0:T(8,128)S(1)}, f32[4608,1024]{1,0:T(8,128)}, u32[]{:S(2)}) copy-start(f32[4608,1024]{1,0:T(8,128)} %tile_ref.5) | copy-start | bytes 56623108
  63.5 18.4 %all-to-all-start.1 = ((f32[16,8,1024]{2,1,0:T(8,128)}), f32[16,8,1024]{2,1,0:T(8,128)S(1)}, u32[]{:S(2)}, u32[]{:S(2)}) async-start(f32[16,8,1024]{2,1,0:T(8,128)} %bitcast.5), calls=%async_computation.1 | async-start | bytes 1048576 | tf_op jit(solution)/shard_map/all_to_all | solution.py:201
  84.3 65.9 %copy-start.5 = (s32[128]{0:T(128)S(1)}, s32[128]{0:T(128)}, u32[]{:S(2)}) copy-start(s32[128]{0:T(128)} %param.5) | copy-start | bytes 1540
  84.3 61.2 %all-to-all-start.4 = ((f32[128,8,1024]{2,1,0:T(8,128)}), f32[128,8,1024]{2,1,0:T(8,128)}, u32[]{:S(2)}, u32[]{:S(2)}) async-start(f32[128,8,1024]{2,1,0:T(8,128)} %broadcast_in_dim.5), calls=%async_computation.4 | async-start | bytes 8388608 | tf_op jit(solution)/shard_map/all_to_all | solution.py:178
  146.3 15.0 %all-to-all-start.2 = ((f32[16,8,1024]{2,1,0:T(8,128)}), f32[16,8,1024]{2,1,0:T(8,128)S(1)}, u32[]{:S(2)}, u32[]{:S(2)}) async-start(f32[16,8,1024]{2,1,0:T(8,128)} %broadcast_in_dim.4), calls=%async_computation.2 | async-start | bytes 1048576 | tf_op jit(solution)/shard_map/all_to_all | solution.py:204
  158.7 1.9 %copy-start.2 = (f32[1024,1024]{1,0:T(8,128)}, f32[1024,1024]{1,0:T(8,128)S(1)}, u32[]{:S(2)}) copy-start(f32[1024,1024]{1,0:T(8,128)S(1)} %inverse.1.inverse_ref) | copy-start | bytes 12582916
  161.4 2.2 %copy-start.3 = (f32[1024,1024]{1,0:T(8,128)S(1)}, f32[1024,1024]{1,0:T(8,128)}, u32[]{:S(2)}) copy-start(f32[1024,1024]{1,0:T(8,128)} %copy-done.2) | copy-start | bytes 12582916

commit v2 on v0

v2 whole, which is shorter than its diff:
```python
import jax
import jax.numpy as jnp
from jax import lax
from jax.experimental import pallas as pl
from jax.experimental.pallas import tpu as pltpu
from jax.sharding import PartitionSpec as P

F32 = jnp.float32
BF16 = jnp.bfloat16
TILE = 256
CHUNK = 16
SLOTS = 4
BLOCK = 128
HALF = 64
CORE, Z_HIGH, Z_LOW = 8, 16, 4
X_STEPS = (32, 96, 64)
Y_STEPS = (1, 3, 2)


def halves(x):
    high = x.astype(BF16)
    return high, (x - high.astype(F32)).astype(BF16)


def dot(a, b, ca=1, cb=0):
    return lax.dot_general(a, b, (((ca,), (cb,)), ((), ())), preferred_element_type=F32)


def dot3(a, b):
    ah, al = halves(a)
    bh, bl = halves(b)
    return dot(ah, bh) + (dot(ah, bl) + dot(al, bh))


def span(start, size):
    return pl.ds(start if isinstance(start, int) else pl.multiple_of(start, size), size)


def sweep(first, lead_ref, tiles_ref, slot_ref, even_ref, odd_ref, sem, use, keep=None):
    steps = tiles_ref.shape[0] // TILE
    total = tiles_ref.shape[1]
    index = lax.broadcasted_iota(jnp.int32, (CHUNK, total), 0)

    def fetch(step):
        slot = step % SLOTS if isinstance(step, int) else lax.rem(step, SLOTS)
        return pltpu.make_async_copy(tiles_ref.at[span(step * TILE, TILE), :], slot_ref.at[slot], sem.at[slot])

    def halve(step, ref):
        slot = step % SLOTS if isinstance(step, int) else lax.rem(step, SLOTS)
        start = lead_ref[...] - (first + step * TILE)
        for at in range(0, TILE, CHUNK):
            x = slot_ref[slot, at : at + CHUNK, :]
            lead = start - at
            x = jnp.where(index < lead, 0.0, jnp.where(index == lead, 1.0, x))
            high, low = halves(x)
            ref[0, at : at + CHUNK, :] = high
            ref[1, at : at + CHUNK, :] = low
            if keep is not None:
                part = span(step * TILE + at, CHUNK)
                keep[0][part, :] = high
                keep[1][part, :] = low

    for step in range(SLOTS - 1):
        fetch(step).start()
    fetch(0).wait()
    halve(0, even_ref)

    @pl.loop(0, steps // 2 - 1)
    def _(pair):
        for step, now, later in ((2 * pair, even_ref, odd_ref), (2 * pair + 1, odd_ref, even_ref)):

            @pl.when(step + SLOTS - 1 < steps)
            def _():
                fetch(step + SLOTS - 1).start()

            fetch(step + 1).wait()
            use(step, now)
            halve(step + 1, later)

    fetch(steps - 1).wait()
    use(steps - 2, even_ref)
    halve(steps - 1, odd_ref)
    use(steps - 1, odd_ref)


def gram_kernel(place_ref, lead_ref, tiles_ref, keep_ref, send_ref, slot_ref, even_ref, odd_ref, sum_ref, pack_ref, sem):
    total = tiles_ref.shape[1]
    first, core, x_at, col = place_ref[0], place_ref[1], place_ref[2], place_ref[3]
    parity = lax.rem(col, 2)
    block_a, block_b = col // 2, (15 - col) // 2
    lane_half = lax.broadcasted_iota(jnp.int32, (1, BLOCK), 1) // HALF
    from_a = jnp.where(lane_half == parity, 1.0, 0.0).astype(BF16)
    from_b = jnp.where(lane_half == parity, 0.0, 1.0).astype(BF16)

    def use(step, ref):
        def chosen(which):
            a = ref[which, :, span(block_a * BLOCK, BLOCK)]
            b = ref[which, :, span(block_b * BLOCK, BLOCK)]
            return a * from_a + b * from_b

        left = jnp.concatenate([chosen(0), chosen(1)], axis=1).T
        both = dot(left, ref[0])
        sum_ref[...] += both[:BLOCK] + (both[BLOCK:] + dot(left[:BLOCK], ref[1]))

    sum_ref[...] = jnp.zeros_like(sum_ref)
    sweep(first, lead_ref, tiles_ref, slot_ref, even_ref, odd_ref, sem, use)

    blocks_b = block_b + 1
    pack_ref[:, :total] = sum_ref[span((1 - parity) * HALF, HALF), :]
    for m in range(4):

        @pl.when(m <= block_a)
        def _():
            pack_ref[:, span((blocks_b + m) * BLOCK, BLOCK)] = sum_ref[
                span(parity * HALF, HALF), m * BLOCK : (m + 1) * BLOCK
            ]

    for k in range(4):
        at = jnp.bitwise_xor(x_at, k) * 8
        keep_ref[k * 8 : k * 8 + 8, :] = pack_ref[span(core * 32 + at, 8), :]
        send_ref[k * 8 : k * 8 + 8, :] = pack_ref[span((1 - core) * 32 + at, 8), :]


def product_kernel(
    place_ref, lead_ref, vec_ref, tiles_ref, high_ref, low_ref, keep_ref, send_ref, slot_ref, even_ref, odd_ref, sum_ref, sem
):
    count = vec_ref.shape[0]
    core, x_at = place_ref[1], place_ref[2]

    def use(step, ref):
        vh, vl = halves(vec_ref[:, span(step * TILE, TILE)])
        both = dot(jnp.concatenate([vh, vl], axis=0), ref[0])
        sum_ref[...] += both[:count] + (both[count:] + dot(vh, ref[1]))

    sum_ref[...] = jnp.zeros_like(sum_ref)
    sweep(place_ref[0], lead_ref, tiles_ref, slot_ref, even_ref, odd_ref, sem, use, (high_ref, low_ref))
    for k in range(4):
        at = jnp.bitwise_xor(x_at, k) * 16
        keep_ref[k * 16 : k * 16 + 16, :] = sum_ref[span(core * 64 + at, 16), :]
        send_ref[k * 16 : k * 16 + 16, :] = sum_ref[span((1 - core) * 64 + at, 16), :]


def join_kernel(*refs):
    *parts, out_ref = refs
    at = 0
    for part in parts:
        if part.ndim == 3:
            out_ref[at : at + part.shape[0]] = part[...]
            at += part.shape[0]


def reorder_kernel(order_ref, vec_ref, out_ref):
    order = order_ref[...]

    @pl.loop(0, vec_ref.shape[1] // TILE)
    def _(step):
        part = span(step * TILE, TILE)
        value = vec_ref[:, part]
        v1 = value.astype(BF16)
        rest = value - v1.astype(F32)
        v2, v3 = halves(rest)
        out_ref[:, part] = dot(order, v1) + (dot(order, v2) + dot(order, v3))


def inverse_kernel(place_ref, *refs):
    *gram_refs, high_ref, low_ref, lower_ref, out_ref = refs
    total = out_ref.shape[0]
    blocks = total // BLOCK
    core, x_at, col = place_ref[1], place_ref[2], place_ref[3]
    r = lax.broadcasted_iota(jnp.int32, (BLOCK, BLOCK), 0)
    c = lax.broadcasted_iota(jnp.int32, (BLOCK, BLOCK), 1)
    for q in range(8):
        width = (q // 2 + 1) * BLOCK
        rest = 9 * BLOCK - width
        away = jnp.bitwise_xor(col, q)
        for k in range(8):
            mine = lax.rem(away, 4) * 2 + away // 4
            near = jnp.bitwise_xor(x_at, k % 4)
            for j, ref in enumerate(gram_refs):

                @pl.when((near == j % 4) & (jnp.bitwise_xor(core, k // 4) == j // 4))
                def _():
                    piece = ref[mine]
                    top, low = (15 - q) * HALF + k * 8, q * HALF + k * 8
                    lower_ref[top : top + 8, :rest] = piece[:, :rest]
                    lower_ref[low : low + 8, :width] = piece[:, rest:]

    out_ref[...] = jnp.zeros_like(out_ref)
    lows, inverses = [], []
    for q in range(blocks):
        part = pl.ds(q * BLOCK, BLOCK)
        square = lower_ref[part, part]
        lows.append(square)
        inverses.append(jnp.where(r == c, 2.0 / square, 0.0))
    same = r // HALF == c // HALF
    scales = [jnp.sum(inverses[q], axis=0, keepdims=True) for q in range(blocks)]
    scaled = [jnp.sum(inverses[q], axis=1, keepdims=True) for q in range(blocks)]
    powers = [jnp.where(same & (r > c), -lows[q] * scaled[q], 0.0) for q in range(blocks)]
    identity = jnp.where(r == c, 1.0, 0.0)
    products = [identity + powers[q] for q in range(blocks)]
    for _ in range(5):
        powers = [dot3(powers[q], powers[q]) for q in range(blocks)]
        products = [products[q] + dot3(products[q], powers[q]) for q in range(blocks)]
    inverses = [products[q] * scales[q] for q in range(blocks)]
    pair = (r >= HALF) & (c < HALF)
    mids = [dot3(jnp.where(pair, lows[q], 0.0), inverses[q]) for q in range(blocks)]
    inverses = [inverses[q] - dot3(inverses[q], mids[q]) for q in range(blocks)]
    size = BLOCK
    for q in range(blocks):
        part = pl.ds(q * BLOCK, BLOCK)
        out_ref[part, part] = inverses[q]
    while size < total:
        for start in range(0, total, 2 * size):
            a, b = pl.ds(start, size), pl.ds(start + size, size)
            mid = dot3(lower_ref[b, a], out_ref[a, a])
            out_ref[b, a] = -dot3(out_ref[b, b], mid)
        size *= 2
    high, low = halves(out_ref[...])
    high_ref[...] = high
    low_ref[...] = low


def change_kernel(place_ref, order_ref, *refs):
    *sum_refs, th_ref, tl_ref, vec_ref, high_ref, low_ref, out_ref, sum_ref, w_ref, put_ref, put_sem = refs
    count, rows = vec_ref.shape
    steps = rows // TILE
    core, x_at = place_ref[1], place_ref[2]
    for j, ref in enumerate(sum_refs):
        at = jnp.bitwise_xor(core, j // 4) * 64 + jnp.bitwise_xor(x_at, j % 4) * 16
        sum_ref[span(at, 16), :] = ref[...]
    yh, yl = halves(sum_ref[...])
    both = dot(jnp.concatenate([yh, yl], axis=0), th_ref[...])
    weighted = both[:count] + (both[count:] + dot(yh, tl_ref[...]))
    order = order_ref[...]
    wh, wl = halves(weighted)
    w_ref[:count, :] = dot(order, wh).astype(BF16)
    w_ref[count:, :] = dot(order, wl).astype(BF16)

    def put(step, slot):
        return pltpu.make_async_copy(put_ref.at[slot], out_ref.at[:, span(step * TILE, TILE)], put_sem.at[slot])

    @pl.loop(0, steps)
    def _(step):
        at = lax.rem(step, 2)
        part = span(step * TILE, TILE)
        both = dot(w_ref[...], high_ref[part, :], 1, 1)
        change = both[:count] + (both[count:] + dot(w_ref[:count, :], low_ref[part, :], 1, 1))

        @pl.when(step >= 2)
        def _():
            put(step - 2, at).wait()

        put_ref[at] = vec_ref[:, part] - change
        put(step, at).start()

    for step in range(max(0, steps - 2), steps):
        put(step, step % 2).wait()


def params(mib):
    return pltpu.CompilerParams(vmem_limit_bytes=mib << 20)


def cost(flops, moved):
    return pl.CostEstimate(flops=flops, bytes_accessed=moved, transcendentals=0)


def swap(x, bits):
    return lax.ppermute(x, ("row", "col"), [(i, i ^ bits) for i in range(128)])


def scattered_sum(keep, send, size):
    both = keep + swap(send, CORE)
    total = both[:size]
    for k, bits in ((1, 32), (3, 96), (2, 64)):
        total = total + swap(both[k * size : (k + 1) * size], bits)
    return total + swap(total, Z_HIGH)


def gather(x, steps):
    near, far, across = (swap(x, bits) for bits in steps)
    return [x, near, across, far]


def join(*parts):
    places = [pl.BlockSpec(memory_space=pltpu.VMEM if part.ndim == 3 else pl.ANY) for part in parts]
    deep = sum(part.shape[0] for part in parts if part.ndim == 3)
    return pl.pallas_call(
        join_kernel,
        in_specs=places,
        out_specs=pl.BlockSpec(memory_space=pltpu.VMEM),
        out_shape=jax.ShapeDtypeStruct((deep,) + parts[-1].shape[1:], F32),
        compiler_params=params(4),
        cost_estimate=cost(1 << 16, 1 << 16),
        name="join",
    )(*parts)


def per_device(source_vectors, source_slot, reflectors, panel_offsets):
    row_count = lax.axis_size("row")
    col_count = lax.axis_size("col")
    src_block = source_vectors.shape[0]
    rows_dev, total = reflectors.shape
    width = total // panel_offsets.shape[0]
    count = src_block * row_count

    row = lax.axis_index("row")
    place = jnp.stack([row * rows_dev, row % 2, row // 4, lax.axis_index("col")]).astype(jnp.int32)
    lead = (panel_offsets[:, None] + jnp.arange(width, dtype=jnp.int32)[None, :]).reshape(1, total)
    placing = source_slot // (col_count * src_block) * src_block + source_slot % src_block
    order = (placing[:, None] == jnp.arange(count, dtype=jnp.int32)[None, :]).astype(BF16)

    smem = pl.BlockSpec(memory_space=pltpu.SMEM)
    vmem = pl.BlockSpec(memory_space=pltpu.VMEM)
    hbm = pl.BlockSpec(memory_space=pltpu.HBM)
    held = pltpu.VMEM((rows_dev, total), BF16)

    shaped = source_vectors.reshape(src_block, row_count, rows_dev).transpose(1, 0, 2)
    received = lax.all_to_all(shaped, "row", 0, 0, tiled=True).reshape(count, rows_dev)

    packed = 9 * BLOCK
    swept = [
        pltpu.VMEM((SLOTS, TILE, total), F32),
        pltpu.VMEM((2, TILE, total), BF16),
        pltpu.VMEM((2, TILE, total), BF16),
        pltpu.VMEM((BLOCK, total), F32),
    ]
    near_hbm = pltpu.with_memory_space_constraint(reflectors, pltpu.HBM)
    keep, send = pl.pallas_call(
        gram_kernel,
        in_specs=[smem, vmem, hbm],
        out_specs=[vmem, vmem],
        out_shape=[jax.ShapeDtypeStruct((HALF // 2, packed), F32)] * 2,
        scratch_shapes=swept + [pltpu.VMEM((HALF, packed), F32), pltpu.SemaphoreType.DMA((SLOTS,))],
        compiler_params=params(20),
        cost_estimate=cost(6 * rows_dev * BLOCK * total, 4 * rows_dev * total),
        name="gram",
    )(place, lead, near_hbm)
    piece = scattered_sum(keep, send, 8)[None]
    pieces = join(received, piece, swap(piece, Z_LOW))
    pieces = join(*gather(pieces, Y_STEPS))
    pieces = gather(pieces, X_STEPS)
    pieces = pieces + [swap(piece, CORE) for piece in pieces]
    t_high, t_low = pl.pallas_call(
        inverse_kernel,
        in_specs=[smem] + [vmem] * 8,
        out_specs=[vmem] * 2,
        out_shape=[jax.ShapeDtypeStruct((total, total), BF16)] * 2,
        scratch_shapes=[pltpu.VMEM((total, total), F32), pltpu.VMEM((total, total), F32)],
        compiler_params=params(24),
        cost_estimate=cost(2 * total**3, 8 * total**2),
        name="inverse",
    )(place, *pieces)

    high, low, keep, send = pl.pallas_call(
        product_kernel,
        in_specs=[smem, vmem, vmem, hbm],
        out_specs=[vmem] * 4,
        out_shape=[held, held] + [jax.ShapeDtypeStruct((count // 2, total), F32)] * 2,
        scratch_shapes=swept + [pltpu.SemaphoreType.DMA((SLOTS,))],
        compiler_params=params(20),
        cost_estimate=cost(6 * rows_dev * count * total, 4 * rows_dev * total),
        name="product",
    )(place, lead, received, near_hbm)
    ordered = pl.pallas_call(
        reorder_kernel,
        in_specs=[vmem, vmem],
        out_specs=vmem,
        out_shape=jax.ShapeDtypeStruct((count, rows_dev), F32),
        compiler_params=params(16),
        cost_estimate=cost(6 * rows_dev * count * count, 16 * rows_dev * count),
        name="reorder",
    )(order, received)
    sums = gather(scattered_sum(keep, send, count // 8), X_STEPS)
    sums = sums + [swap(part, CORE) for part in sums]

    return pl.pallas_call(
        change_kernel,
        in_specs=[smem] + [vmem] * 14,
        out_specs=hbm,
        out_shape=jax.ShapeDtypeStruct((count, rows_dev), F32),
        scratch_shapes=[
            pltpu.VMEM((count, total), F32),
            pltpu.VMEM((2 * count, total), BF16),
            pltpu.VMEM((2, count, TILE), F32),
            pltpu.SemaphoreType.DMA((2,)),
        ],
        compiler_params=params(16),
        cost_estimate=cost(6 * rows_dev * count * total, 4 * rows_dev * count),
        name="change",
    )(place, order, *sums, t_high, t_low, ordered, high, low)


def solution(mesh):
    in_specs = (P(("row", "col"), None), P("col"), P("row", None), P())
    out_specs = P("col", "row")
    return jax.shard_map(per_device, mesh=mesh, in_specs=in_specs, out_specs=out_specs, check_vma=False)
```

time: 1460 us -> 122 us (0.08)
  blocking collectives: 1040 us -> 0 us
  matrix products: 237 us -> 0 us
  waiting for transfers between devices: 129 us -> 25.7 us
  Pallas kernels: 0 us -> 52.1 us
  starting transfers between devices: 9.14 us -> 43.3 us
  other arithmetic: 16.5 us -> 0.34 us
    psum x16 -> x0, blocking collectives: 1040 us -> none  [the longest x15 974 us: panel_step(): product = lax.psum(local, 'row')]
    dot_general x59 -> x0, matrix products: 237 us -> none  [the longest x15 94.3 us: panel_step(): local = jnp.dot(current, panel, precision=lax.Precision.HIGHEST)]
    psum x1 -> x0, waiting for transfers between devices: 129 us -> none  [per_device(): inner = lax.psum(inner_local, 'row')]
    pallas_call x0 -> x7, Pallas kernels: none -> 52.1 us  [the longest x1 14.1 us: per_device(): pl.pallas_call(gram_kernel, in_specs=[smem, vmem, hbm], out_specs=[vmem,...]
    ppermute x0 -> x28, starting transfers between devices: none -> 34.1 us  [swap(): return lax.ppermute(x, ('row', 'col'), [(i, i ^ bits) for i in range(128)])]
    ppermute x0 -> x28, waiting for transfers between devices: none -> 25.7 us  [swap(): return lax.ppermute(x, ('row', 'col'), [(i, i ^ bits) for i in range(128)])]
    select_n x3 -> x0, other arithmetic: 15.6 us -> none  [the longest x1 15.6 us: reflector_block(): return jnp.where(rows < lead, 0.0, jnp.where(rows == lead, 1.0, reflectors))]
  transfers between devices with their start and end apart: 2 -> 29, of which waited for: 1 -> 7; matrix products, arithmetic and copies ran while one was open for 2% -> 0% of each run, Pallas kernels for 0% -> 34%
where the time goes in v2:
time: 122 us
  Pallas kernels  52.1 us (43%)
  starting transfers between devices  43.3 us (35%)
  waiting for transfers between devices  25.7 us (21%)
    ppermute x28, starting transfers between devices, swap(): return lax.ppermute(x, ('row', 'col'), [(i, i ^ bits) for i in range(128)])  34.1 us
    ppermute x28, waiting for transfers between devices, swap(): return lax.ppermute(x, ('row', 'col'), [(i, i ^ bits) for i in range(128)])  25.7 us
    pallas_call x1, Pallas kernels, per_device(): pl.pallas_call(gram_kernel, in_specs=[smem, vmem, hbm], out_specs=[vmem,...  14.1 us
    pallas_call x1, Pallas kernels, per_device(): pl.pallas_call(product_kernel, in_specs=[smem, vmem, vmem, hbm], out_spec...  13.3 us
    pallas_call x1, Pallas kernels, per_device(): pl.pallas_call(change_kernel, in_specs=[smem] + [vmem] * 14, out_specs=hb...  10.9 us
    pallas_call x1, Pallas kernels, per_device(): pl.pallas_call(inverse_kernel, in_specs=[smem] + [vmem] * 8, out_specs=[v...  10 us
    all_to_all x1, starting transfers between devices, per_device(): lax.all_to_all(shaped, 'row', 0, 0, tiled=True).reshape(count, rows_dev)  9.26 us
    pallas_call x1, Pallas kernels, per_device(): pl.pallas_call(reorder_kernel, in_specs=[vmem, vmem], out_specs=vmem, out...  3.83 us
  transfers between devices with their start and end apart: 29, of which 7 were waited for; matrix products, arithmetic and copies ran while one was open for 0% of the time, Pallas kernels for 34%

profile of v2, /device:TPU:1, one launch (start us, length us, event | category | flops | bytes accessed | tf_op | source)
XLA Modules:
  0.0 122.0 jit_solution(3868206066330874637)
XLA Ops:
  0.0 9.3 %all-to-all-start = ((f32[16,8,4608]{2,1,0:T(8,128)}), f32[16,8,4608]{2,1,0:T(8,128)S(1)}, u32[]{:S(2)}, u32[]{:S(2)}) async-start(f32[16,8,4608]{2,1,0:T(8,128)} %bitcast.13), calls=%async_computation | async-start | bytes 4718592 | tf_op jit(solution)/shard_map/all_to_all | solution.py:319
  9.5 14.1 %gram.1 = (f32[32,1152]{1,0:T(8,128)S(1)}, f32[32,1152]{1,0:T(8,128)S(1)}) custom-call(s32[4]{0:T(128)S(1)} %pad_add_fusion.place_ref, s32[1,1024]{1,0:T(1,128)S(1)} %add.74.lead_ref, f32[4608,1024]{1,0:T(8,128)} %tiles_ref.3), custom_call_target="tpu_custom_call" | custom-call | flops 3623878656 | bytes 18874368 | tf_op jit(solution)/shard_map/gram/pallas_call | solution.py:329
  23.8 1.2 %collective-permute-done.12 = f32[32,1152]{1,0:T(8,128)S(1)} collective-permute-done((f32[32,1152]{1,0:T(8,128)S(1)}, f32[32,1152]{1,0:T(8,128)S(1)}, u32[]{:S(2)}, u32[]{:S(2)}) %collective-permute-start.12) | collective-permute-done | bytes 147488 | tf_op jit(solution)/shard_map/ppermute | solution.py:269
  25.1 1.5 %collective-permute-start.13 = (f32[8,1152]{1,0:T(8,128)S(1)}, f32[8,1152]{1,0:T(8,128)S(1)}, u32[]{:S(2)}, u32[]{:S(2)}) collective-permute-start(f32[8,1152]{1,0:T(8,128)S(1)} %get-tuple-element.24), channel_id=1, source_target_pairs={{0,32},{1,33},{2,34},{3,35},{4,36},{5,37},{6,38},{7,39},{8,40},{9,... | collective-permute-start | bytes 110600 | tf_op jit(solution)/shard_map/ppermute | solution.py:269
  26.6 1.8 %collective-permute-start.14 = (f32[8,1152]{1,0:T(8,128)S(1)}, f32[8,1152]{1,0:T(8,128)S(1)}, u32[]{:S(2)}, u32[]{:S(2)}) collective-permute-start(f32[8,1152]{1,0:T(8,128)S(1)} %get-tuple-element.26), channel_id=1, source_target_pairs={{0,96},{1,97},{2,98},{3,99},{4,100},{5,101},{6,102},{7,103},{8,104... | collective-permute-start | bytes 110600 | tf_op jit(solution)/shard_map/ppermute | solution.py:269
  28.4 0.6 collective-permute-start.15
  29.0 8.8 %collective-permute-done.13 = f32[8,1152]{1,0:T(8,128)S(1)} collective-permute-done((f32[8,1152]{1,0:T(8,128)S(1)}, f32[8,1152]{1,0:T(8,128)S(1)}, u32[]{:S(2)}, u32[]{:S(2)}) %collective-permute-start.13) | collective-permute-done | bytes 36896 | tf_op jit(solution)/shard_map/ppermute | solution.py:269
  37.8 5.5 %collective-permute-done.15 = f32[8,1152]{1,0:T(8,128)S(1)} collective-permute-done((f32[8,1152]{1,0:T(8,128)S(1)}, f32[8,1152]{1,0:T(8,128)S(1)}, u32[]{:S(2)}, u32[]{:S(2)}) %collective-permute-start.15) | collective-permute-done | bytes 36896 | tf_op jit(solution)/shard_map/ppermute | solution.py:269
  43.4 13.3 %product.1 = (bf16[4608,1024]{1,0:T(8,128)(2,1)S(1)}, bf16[4608,1024]{1,0:T(8,128)(2,1)S(1)}, f32[64,1024]{1,0:T(8,128)S(1)}, f32[64,1024]{1,0:T(8,128)S(1)}) custom-call(s32[4]{0:T(128)S(1)} %pad_add_fusion.place_ref, s32[1,1024]{1,0:T(1,128)S(1)} %add.74.lead_ref, f32[128,4608]{1,0:T(8,128)S(1)} %bitcast.10, f32[4608,1024]{1,0:T(8,128)} %tiles_ref.3), custom_call_target="tpu_custom_call" | custom-call | flops 3623878656 | bytes 18874368 | tf_op jit(solution)/shard_map/product/pallas_call | solution.py:355
  56.6 1.2 %collective-permute-start = (f32[64,1024]{1,0:T(8,128)S(1)}, f32[64,1024]{1,0:T(8,128)S(1)}, u32[]{:S(2)}, u32[]{:S(2)}) collective-permute-start(f32[64,1024]{1,0:T(8,128)S(1)} %get-tuple-element.14), channel_id=1, source_target_pairs={{0,8},{1,9},{2,10},{3,11},{4,12},{5,13},{6,14},{7,15},{8,0},{9,1},... | collective-permute-start | bytes 786440 | tf_op jit(solution)/shard_map/ppermute | solution.py:269
  57.9 0.8 collective-permute-start.17
  58.7 2.1 %collective-permute-done.17.refs_2_ = f32[1,8,1152]{2,1,0:T(8,128)S(1)} collective-permute-done((f32[1,8,1152]{2,1,0:T(8,128)S(1)}, f32[1,8,1152]{2,1,0:T(8,128)S(1)}, u32[]{:S(2)}, u32[]{:S(2)}) %collective-permute-start.17) | collective-permute-done | bytes 36896 | tf_op jit(solution)/shard_map/ppermute | solution.py:269
  60.8 1.3 %collective-permute-start.18 = (f32[2,8,1152]{2,1,0:T(8,128)S(1)}, f32[2,8,1152]{2,1,0:T(8,128)S(1)}, u32[]{:S(2)}, u32[]{:S(2)}) collective-permute-start(f32[2,8,1152]{2,1,0:T(8,128)S(1)} %join.2.refs_0_), channel_id=1, source_target_pairs={{0,1},{1,0},{2,3},{3,2},{4,5},{5,4},{6,7},{7,6},{8,9},{9,8},{10,11... | collective-permute-start | bytes 221192 | tf_op jit(solution)/shard_map/ppermute | solution.py:269
  62.1 2.6 %collective-permute-start.19 = (f32[2,8,1152]{2,1,0:T(8,128)S(1)}, f32[2,8,1152]{2,1,0:T(8,128)S(1)}, u32[]{:S(2)}, u32[]{:S(2)}) collective-permute-start(f32[2,8,1152]{2,1,0:T(8,128)S(1)} %join.2.refs_0_), channel_id=1, source_target_pairs={{0,2},{1,3},{2,0},{3,1},{4,6},{5,7},{6,4},{7,5},{8,10},{9,11},{10,... | collective-permute-start | bytes 221192 | tf_op jit(solution)/shard_map/ppermute | solution.py:269
  64.9 2.0 %collective-permute-start.2 = (f32[16,1024]{1,0:T(8,128)S(1)}, f32[16,1024]{1,0:T(8,128)S(1)}, u32[]{:S(2)}, u32[]{:S(2)}) collective-permute-start(f32[16,1024]{1,0:T(8,128)S(1)} %get-tuple-element.23), channel_id=1, source_target_pairs={{0,96},{1,97},{2,98},{3,99},{4,100},{5,101},{6,102},{7,103},{8,104... | collective-permute-start | bytes 196616 | tf_op jit(solution)/shard_map/ppermute | solution.py:269
  66.9 1.2 collective-permute-start.3
  68.1 1.5 %collective-permute-done.20.refs_3_ = f32[2,8,1152]{2,1,0:T(8,128)S(1)} collective-permute-done((f32[2,8,1152]{2,1,0:T(8,128)S(1)}, f32[2,8,1152]{2,1,0:T(8,128)S(1)}, u32[]{:S(2)}, u32[]{:S(2)}) %collective-permute-start.20) | collective-permute-done | bytes 73760 | tf_op jit(solution)/shard_map/ppermute | solution.py:269
  69.8 3.1 %collective-permute-start.22 = (f32[8,8,1152]{2,1,0:T(8,128)S(1)}, f32[8,8,1152]{2,1,0:T(8,128)S(1)}, u32[]{:S(2)}, u32[]{:S(2)}) collective-permute-start(f32[8,8,1152]{2,1,0:T(8,128)S(1)} %join.3.refs_0_), channel_id=1, source_target_pairs={{0,64},{1,65},{2,66},{3,67},{4,68},{5,69},{6,70},{7,71},{8,72},{9,... | collective-permute-start | bytes 884744 | tf_op jit(solution)/shard_map/ppermute | solution.py:269
  72.9 0.7 collective-permute-start.23
  73.6 3.2 %collective-permute-start.24 = (f32[8,8,1152]{2,1,0:T(8,128)S(1)}, f32[8,8,1152]{2,1,0:T(8,128)S(1)}, u32[]{:S(2)}, u32[]{:S(2)}) collective-permute-start(f32[8,8,1152]{2,1,0:T(8,128)S(1)} %join.3.refs_0_), channel_id=1, source_target_pairs={{0,8},{1,9},{2,10},{3,11},{4,12},{5,13},{6,14},{7,15},{8,0},{9,1},... | collective-permute-start | bytes 884744 | tf_op jit(solution)/shard_map/ppermute | solution.py:269
  76.9 3.3 %collective-permute-start.4 = (f32[16,1024]{1,0:T(8,128)S(1)}, f32[16,1024]{1,0:T(8,128)S(1)}, u32[]{:S(2)}, u32[]{:S(2)}) collective-permute-start(f32[16,1024]{1,0:T(8,128)S(1)} %fusion.1), channel_id=1, source_target_pairs={{0,16},{1,17},{2,18},{3,19},{4,20},{5,21},{6,22},{7,23},{8,24},{9,... | collective-permute-start | bytes 196616 | tf_op jit(solution)/shard_map/ppermute | solution.py:269
  80.2 1.9 %collective-permute-start.25 = (f32[8,8,1152]{2,1,0:T(8,128)S(1)}, f32[8,8,1152]{2,1,0:T(8,128)S(1)}, u32[]{:S(2)}, u32[]{:S(2)}) collective-permute-start(f32[8,8,1152]{2,1,0:T(8,128)S(1)} %collective-permute-done.21.refs_1_), channel_id=1, source_target_pairs={{0,8},{1,9},{2,10},{3,11},{4,12},{5,13},{6,14},{7,15},{8,0},{9,1},... | collective-permute-start | bytes 884744 | tf_op jit(solution)/shard_map/ppermute | solution.py:269
  82.1 2.6 %collective-permute-done.22.refs_2_ = f32[8,8,1152]{2,1,0:T(8,128)S(1)} collective-permute-done((f32[8,8,1152]{2,1,0:T(8,128)S(1)}, f32[8,8,1152]{2,1,0:T(8,128)S(1)}, u32[]{:S(2)}, u32[]{:S(2)}) %collective-permute-start.22) | collective-permute-done | bytes 294944 | tf_op jit(solution)/shard_map/ppermute | solution.py:269
  84.7 3.0 %collective-permute-start.26 = (f32[8,8,1152]{2,1,0:T(8,128)S(1)}, f32[8,8,1152]{2,1,0:T(8,128)S(1)}, u32[]{:S(2)}, u32[]{:S(2)}) collective-permute-start(f32[8,8,1152]{2,1,0:T(8,128)S(1)} %collective-permute-done.22.refs_2_), channel_id=1, source_target_pairs={{0,8},{1,9},{2,10},{3,11},{4,12},{5,13},{6,14},{7,15},{8,0},{9,1},... | collective-permute-start | bytes 884744 | tf_op jit(solution)/shard_map/ppermute | solution.py:269
  87.7 2.2 %collective-permute-start.27 = (f32[8,8,1152]{2,1,0:T(8,128)S(1)}, f32[8,8,1152]{2,1,0:T(8,128)S(1)}, u32[]{:S(2)}, u32[]{:S(2)}) collective-permute-start(f32[8,8,1152]{2,1,0:T(8,128)S(1)} %collective-permute-done.23.refs_3_), channel_id=1, source_target_pairs={{0,8},{1,9},{2,10},{3,11},{4,12},{5,13},{6,14},{7,15},{8,0},{9,1},... | collective-permute-start | bytes 884744 | tf_op jit(solution)/shard_map/ppermute | solution.py:269
  90.0 1.3 %collective-permute-start.7 = (f32[16,1024]{1,0:T(8,128)S(1)}, f32[16,1024]{1,0:T(8,128)S(1)}, u32[]{:S(2)}, u32[]{:S(2)}) collective-permute-start(f32[16,1024]{1,0:T(8,128)S(1)} %add.79.refs_0_), channel_id=1, source_target_pairs={{0,96},{1,97},{2,98},{3,99},{4,100},{5,101},{6,102},{7,103},{8,104... | collective-permute-start | bytes 196616 | tf_op jit(solution)/shard_map/ppermute | solution.py:269
  91.4 3.9 %collective-permute-done.6.refs_2_ = f32[16,1024]{1,0:T(8,128)S(1)} collective-permute-done((f32[16,1024]{1,0:T(8,128)S(1)}, f32[16,1024]{1,0:T(8,128)S(1)}, u32[]{:S(2)}, u32[]{:S(2)}) %collective-permute-start.6) | collective-permute-done | bytes 65568 | tf_op jit(solution)/shard_map/ppermute | solution.py:269
  95.3 3.8 %reorder.1.refs_10_ = f32[128,4608]{1,0:T(8,128)S(1)} custom-call(bf16[128,128]{1,0:T(8,128)(2,1)S(1)} %fusion.2.order_ref, f32[128,4608]{1,0:T(8,128)S(1)} %bitcast.12), custom_call_target="tpu_custom_call" | custom-call | flops 452984832 | bytes 9437184 | tf_op jit(solution)/shard_map/reorder/pallas_call | solution.py:365
  99.2 0.9 collective-permute-start.8
  100.4 0.3 collective-permute-start.11
  100.9 10.0 %inverse.1 = (bf16[1024,1024]{1,0:T(8,128)(2,1)S(1)}, bf16[1024,1024]{1,0:T(8,128)(2,1)S(1)}) custom-call(s32[4]{0:T(128)S(1)} %pad_add_fusion.place_ref, f32[8,8,1152]{2,1,0:T(8,128)S(1)} %join.3.refs_0_, f32[8,8,1152]{2,1,0:T(8,128)S(1)} %collective-permute-done.21.refs_1_, f32[8,8,1152]{2,1,0:T(8,128)S(1)} %collective-permute-done.22.refs_2_, ...), custom_call_target="tpu_custom_call" | custom-call | flops 2147483648 | bytes 8388608 | tf_op jit(solution)/shard_map/inverse/pallas_call | solution.py:344
  111.0 10.9 %change.1 = f32[128,4608]{1,0:T(8,128)} custom-call(s32[4]{0:T(128)S(1)} %pad_add_fusion.place_ref, bf16[128,128]{1,0:T(8,128)(2,1)S(1)} %fusion.2.order_ref, f32[16,1024]{1,0:T(8,128)S(1)} %add.79.refs_0_, f32[16,1024]{1,0:T(8,128)S(1)} %collective-permute-done.5.refs_1_, f32[16,1024]{1,0:T(8,128)S(1)} %collective-permute-done.6.refs_2_, ...), custom_call_target="tpu_custom_call" | custom-call | flops 3623878656 | bytes 2359296 | tf_op jit(solution)/shard_map/change/pallas_call | solution.py:377
  (50 shorter events, 1.7 us)
Async XLA Ops:
  0.0 9.3 %copy-start = (s32[16]{0:T(128)S(1)}, s32[16]{0:T(128)}, u32[]{:S(2)}) copy-start(s32[16]{0:T(128)} %param.7) | copy-start | bytes 196
  0.0 43.4 %all-to-all-start = ((f32[16,8,4608]{2,1,0:T(8,128)}), f32[16,8,4608]{2,1,0:T(8,128)S(1)}, u32[]{:S(2)}, u32[]{:S(2)}) async-start(f32[16,8,4608]{2,1,0:T(8,128)} %bitcast.13), calls=%async_computation | async-start | bytes 4718592 | tf_op jit(solution)/shard_map/all_to_all | solution.py:319
  23.6 1.5 %collective-permute-start.12 = (f32[32,1152]{1,0:T(8,128)S(1)}, f32[32,1152]{1,0:T(8,128)S(1)}, u32[]{:S(2)}, u32[]{:S(2)}) collective-permute-start(f32[32,1152]{1,0:T(8,128)S(1)} %get-tuple-element.16), channel_id=1, source_target_pairs={{0,8},{1,9},{2,10},{3,11},{4,12},{5,13},{6,14},{7,15},{8,0},{9,1},... | collective-permute-start | bytes 442376 | tf_op jit(solution)/shard_map/ppermute | solution.py:269
  25.1 12.7 %collective-permute-start.13 = (f32[8,1152]{1,0:T(8,128)S(1)}, f32[8,1152]{1,0:T(8,128)S(1)}, u32[]{:S(2)}, u32[]{:S(2)}) collective-permute-start(f32[8,1152]{1,0:T(8,128)S(1)} %get-tuple-element.24), channel_id=1, source_target_pairs={{0,32},{1,33},{2,34},{3,35},{4,36},{5,37},{6,38},{7,39},{8,40},{9,... | collective-permute-start | bytes 110600 | tf_op jit(solution)/shard_map/ppermute | solution.py:269
  26.6 11.2 %collective-permute-start.14 = (f32[8,1152]{1,0:T(8,128)S(1)}, f32[8,1152]{1,0:T(8,128)S(1)}, u32[]{:S(2)}, u32[]{:S(2)}) collective-permute-start(f32[8,1152]{1,0:T(8,128)S(1)} %get-tuple-element.26), channel_id=1, source_target_pairs={{0,96},{1,97},{2,98},{3,99},{4,100},{5,101},{6,102},{7,103},{8,104... | collective-permute-start | bytes 110600 | tf_op jit(solution)/shard_map/ppermute | solution.py:269
  28.4 14.9 %collective-permute-start.15 = (f32[8,1152]{1,0:T(8,128)S(1)}, f32[8,1152]{1,0:T(8,128)S(1)}, u32[]{:S(2)}, u32[]{:S(2)}) collective-permute-start(f32[8,1152]{1,0:T(8,128)S(1)} %get-tuple-element.25), channel_id=1, source_target_pairs={{0,64},{1,65},{2,66},{3,67},{4,68},{5,69},{6,70},{7,71},{8,72},{9,... | collective-permute-start | bytes 110600 | tf_op jit(solution)/shard_map/ppermute | solution.py:269
  43.3 14.6 %collective-permute-start.16 = (f32[8,1152]{1,0:T(8,128)S(1)}, f32[8,1152]{1,0:T(8,128)S(1)}, u32[]{:S(2)}, u32[]{:S(2)}) collective-permute-start(f32[8,1152]{1,0:T(8,128)S(1)} %fusion.4), channel_id=1, source_target_pairs={{0,16},{1,17},{2,18},{3,19},{4,20},{5,21},{6,22},{7,23},{8,24},{9,... | collective-permute-start | bytes 110600 | tf_op jit(solution)/shard_map/ppermute | solution.py:269
  56.6 8.1 %collective-permute-start = (f32[64,1024]{1,0:T(8,128)S(1)}, f32[64,1024]{1,0:T(8,128)S(1)}, u32[]{:S(2)}, u32[]{:S(2)}) collective-permute-start(f32[64,1024]{1,0:T(8,128)S(1)} %get-tuple-element.14), channel_id=1, source_target_pairs={{0,8},{1,9},{2,10},{3,11},{4,12},{5,13},{6,14},{7,15},{8,0},{9,1},... | collective-permute-start | bytes 786440 | tf_op jit(solution)/shard_map/ppermute | solution.py:269
  57.9 32.1 %copy-start.1 = (s32[128]{0:T(128)S(1)}, s32[128]{0:T(128)}, u32[]{:S(2)}) copy-start(s32[128]{0:T(128)} %param.5) | copy-start | bytes 1540
  57.9 2.9 %collective-permute-start.17 = (f32[1,8,1152]{2,1,0:T(8,128)S(1)}, f32[1,8,1152]{2,1,0:T(8,128)S(1)}, u32[]{:S(2)}, u32[]{:S(2)}) collective-permute-start(f32[1,8,1152]{2,1,0:T(8,128)S(1)} %add_bitcast_fusion.refs_1_), channel_id=1, source_target_pairs={{0,4},{1,5},{2,6},{3,7},{4,0},{5,1},{6,2},{7,3},{8,12},{9,13},{10,... | collective-permute-start | bytes 110600 | tf_op jit(solution)/shard_map/ppermute | solution.py:269
  60.8 6.1 %collective-permute-start.18 = (f32[2,8,1152]{2,1,0:T(8,128)S(1)}, f32[2,8,1152]{2,1,0:T(8,128)S(1)}, u32[]{:S(2)}, u32[]{:S(2)}) collective-permute-start(f32[2,8,1152]{2,1,0:T(8,128)S(1)} %join.2.refs_0_), channel_id=1, source_target_pairs={{0,1},{1,0},{2,3},{3,2},{4,5},{5,4},{6,7},{7,6},{8,9},{9,8},{10,11... | collective-permute-start | bytes 221192 | tf_op jit(solution)/shard_map/ppermute | solution.py:269
  62.1 6.0 %collective-permute-start.19 = (f32[2,8,1152]{2,1,0:T(8,128)S(1)}, f32[2,8,1152]{2,1,0:T(8,128)S(1)}, u32[]{:S(2)}, u32[]{:S(2)}) collective-permute-start(f32[2,8,1152]{2,1,0:T(8,128)S(1)} %join.2.refs_0_), channel_id=1, source_target_pairs={{0,2},{1,3},{2,0},{3,1},{4,6},{5,7},{6,4},{7,5},{8,10},{9,11},{10,... | collective-permute-start | bytes 221192 | tf_op jit(solution)/shard_map/ppermute | solution.py:269
  64.7 5.0 %collective-permute-start.20 = (f32[2,8,1152]{2,1,0:T(8,128)S(1)}, f32[2,8,1152]{2,1,0:T(8,128)S(1)}, u32[]{:S(2)}, u32[]{:S(2)}) collective-permute-start(f32[2,8,1152]{2,1,0:T(8,128)S(1)} %join.2.refs_0_), channel_id=1, source_target_pairs={{0,3},{1,2},{2,1},{3,0},{4,7},{5,6},{6,5},{7,4},{8,11},{9,10},{10,... | collective-permute-start | bytes 221192 | tf_op jit(solution)/shard_map/ppermute | solution.py:269
  64.8 8.1 %collective-permute-start.1 = (f32[16,1024]{1,0:T(8,128)S(1)}, f32[16,1024]{1,0:T(8,128)S(1)}, u32[]{:S(2)}, u32[]{:S(2)}) collective-permute-start(f32[16,1024]{1,0:T(8,128)S(1)} %get-tuple-element.21), channel_id=1, source_target_pairs={{0,32},{1,33},{2,34},{3,35},{4,36},{5,37},{6,38},{7,39},{8,40},{9,... | collective-permute-start | bytes 196616 | tf_op jit(solution)/shard_map/ppermute | solution.py:269
  64.9 8.7 %collective-permute-start.2 = (f32[16,1024]{1,0:T(8,128)S(1)}, f32[16,1024]{1,0:T(8,128)S(1)}, u32[]{:S(2)}, u32[]{:S(2)}) collective-permute-start(f32[16,1024]{1,0:T(8,128)S(1)} %get-tuple-element.23), channel_id=1, source_target_pairs={{0,96},{1,97},{2,98},{3,99},{4,100},{5,101},{6,102},{7,103},{8,104... | collective-permute-start | bytes 196616 | tf_op jit(solution)/shard_map/ppermute | solution.py:269
  66.9 9.9 %collective-permute-start.3 = (f32[16,1024]{1,0:T(8,128)S(1)}, f32[16,1024]{1,0:T(8,128)S(1)}, u32[]{:S(2)}, u32[]{:S(2)}) collective-permute-start(f32[16,1024]{1,0:T(8,128)S(1)} %get-tuple-element.22), channel_id=1, source_target_pairs={{0,64},{1,65},{2,66},{3,67},{4,68},{5,69},{6,70},{7,71},{8,72},{9,... | collective-permute-start | bytes 196616 | tf_op jit(solution)/shard_map/ppermute | solution.py:269
  69.7 10.5 %collective-permute-start.21 = (f32[8,8,1152]{2,1,0:T(8,128)S(1)}, f32[8,8,1152]{2,1,0:T(8,128)S(1)}, u32[]{:S(2)}, u32[]{:S(2)}) collective-permute-start(f32[8,8,1152]{2,1,0:T(8,128)S(1)} %join.3.refs_0_), channel_id=1, source_target_pairs={{0,32},{1,33},{2,34},{3,35},{4,36},{5,37},{6,38},{7,39},{8,40},{9,... | collective-permute-start | bytes 884744 | tf_op jit(solution)/shard_map/ppermute | solution.py:269
  69.8 14.9 %collective-permute-start.22 = (f32[8,8,1152]{2,1,0:T(8,128)S(1)}, f32[8,8,1152]{2,1,0:T(8,128)S(1)}, u32[]{:S(2)}, u32[]{:S(2)}) collective-permute-start(f32[8,8,1152]{2,1,0:T(8,128)S(1)} %join.3.refs_0_), channel_id=1, source_target_pairs={{0,64},{1,65},{2,66},{3,67},{4,68},{5,69},{6,70},{7,71},{8,72},{9,... | collective-permute-start | bytes 884744 | tf_op jit(solution)/shard_map/ppermute | solution.py:269
  72.9 14.8 %collective-permute-start.23 = (f32[8,8,1152]{2,1,0:T(8,128)S(1)}, f32[8,8,1152]{2,1,0:T(8,128)S(1)}, u32[]{:S(2)}, u32[]{:S(2)}) collective-permute-start(f32[8,8,1152]{2,1,0:T(8,128)S(1)} %join.3.refs_0_), channel_id=1, source_target_pairs={{0,96},{1,97},{2,98},{3,99},{4,100},{5,101},{6,102},{7,103},{8,104... | collective-permute-start | bytes 884744 | tf_op jit(solution)/shard_map/ppermute | solution.py:269
  73.6 16.4 %collective-permute-start.24 = (f32[8,8,1152]{2,1,0:T(8,128)S(1)}, f32[8,8,1152]{2,1,0:T(8,128)S(1)}, u32[]{:S(2)}, u32[]{:S(2)}) collective-permute-start(f32[8,8,1152]{2,1,0:T(8,128)S(1)} %join.3.refs_0_), channel_id=1, source_target_pairs={{0,8},{1,9},{2,10},{3,11},{4,12},{5,13},{6,14},{7,15},{8,0},{9,1},... | collective-permute-start | bytes 884744 | tf_op jit(solution)/shard_map/ppermute | solution.py:269
  76.9 13.0 %collective-permute-start.4 = (f32[16,1024]{1,0:T(8,128)S(1)}, f32[16,1024]{1,0:T(8,128)S(1)}, u32[]{:S(2)}, u32[]{:S(2)}) collective-permute-start(f32[16,1024]{1,0:T(8,128)S(1)} %fusion.1), channel_id=1, source_target_pairs={{0,16},{1,17},{2,18},{3,19},{4,20},{5,21},{6,22},{7,23},{8,24},{9,... | collective-permute-start | bytes 196616 | tf_op jit(solution)/shard_map/ppermute | solution.py:269
  80.2 20.2 %collective-permute-start.25 = (f32[8,8,1152]{2,1,0:T(8,128)S(1)}, f32[8,8,1152]{2,1,0:T(8,128)S(1)}, u32[]{:S(2)}, u32[]{:S(2)}) collective-permute-start(f32[8,8,1152]{2,1,0:T(8,128)S(1)} %collective-permute-done.21.refs_1_), channel_id=1, source_target_pairs={{0,8},{1,9},{2,10},{3,11},{4,12},{5,13},{6,14},{7,15},{8,0},{9,1},... | collective-permute-start | bytes 884744 | tf_op jit(solution)/shard_map/ppermute | solution.py:269
  84.7 15.9 %collective-permute-start.26 = (f32[8,8,1152]{2,1,0:T(8,128)S(1)}, f32[8,8,1152]{2,1,0:T(8,128)S(1)}, u32[]{:S(2)}, u32[]{:S(2)}) collective-permute-start(f32[8,8,1152]{2,1,0:T(8,128)S(1)} %collective-permute-done.22.refs_2_), channel_id=1, source_target_pairs={{0,8},{1,9},{2,10},{3,11},{4,12},{5,13},{6,14},{7,15},{8,0},{9,1},... | collective-permute-start | bytes 884744 | tf_op jit(solution)/shard_map/ppermute | solution.py:269
  87.7 13.2 %collective-permute-start.27 = (f32[8,8,1152]{2,1,0:T(8,128)S(1)}, f32[8,8,1152]{2,1,0:T(8,128)S(1)}, u32[]{:S(2)}, u32[]{:S(2)}) collective-permute-start(f32[8,8,1152]{2,1,0:T(8,128)S(1)} %collective-permute-done.23.refs_3_), channel_id=1, source_target_pairs={{0,8},{1,9},{2,10},{3,11},{4,12},{5,13},{6,14},{7,15},{8,0},{9,1},... | collective-permute-start | bytes 884744 | tf_op jit(solution)/shard_map/ppermute | solution.py:269
  89.9 5.4 %collective-permute-start.6 = (f32[16,1024]{1,0:T(8,128)S(1)}, f32[16,1024]{1,0:T(8,128)S(1)}, u32[]{:S(2)}, u32[]{:S(2)}) collective-permute-start(f32[16,1024]{1,0:T(8,128)S(1)} %add.79.refs_0_), channel_id=1, source_target_pairs={{0,64},{1,65},{2,66},{3,67},{4,68},{5,69},{6,70},{7,71},{8,72},{9,... | collective-permute-start | bytes 196616 | tf_op jit(solution)/shard_map/ppermute | solution.py:269
  90.0 9.2 %collective-permute-start.7 = (f32[16,1024]{1,0:T(8,128)S(1)}, f32[16,1024]{1,0:T(8,128)S(1)}, u32[]{:S(2)}, u32[]{:S(2)}) collective-permute-start(f32[16,1024]{1,0:T(8,128)S(1)} %add.79.refs_0_), channel_id=1, source_target_pairs={{0,96},{1,97},{2,98},{3,99},{4,100},{5,101},{6,102},{7,103},{8,104... | collective-permute-start | bytes 196616 | tf_op jit(solution)/shard_map/ppermute | solution.py:269
  95.2 4.9 %collective-permute-start.5 = (f32[16,1024]{1,0:T(8,128)S(1)}, f32[16,1024]{1,0:T(8,128)S(1)}, u32[]{:S(2)}, u32[]{:S(2)}) collective-permute-start(f32[16,1024]{1,0:T(8,128)S(1)} %add.79.refs_0_), channel_id=1, source_target_pairs={{0,32},{1,33},{2,34},{3,35},{4,36},{5,37},{6,38},{7,39},{8,40},{9,... | collective-permute-start | bytes 196616 | tf_op jit(solution)/shard_map/ppermute | solution.py:269
  99.2 11.7 %collective-permute-start.8 = (f32[16,1024]{1,0:T(8,128)S(1)}, f32[16,1024]{1,0:T(8,128)S(1)}, u32[]{:S(2)}, u32[]{:S(2)}) collective-permute-start(f32[16,1024]{1,0:T(8,128)S(1)} %add.79.refs_0_), channel_id=1, source_target_pairs={{0,8},{1,9},{2,10},{3,11},{4,12},{5,13},{6,14},{7,15},{8,0},{9,1},... | collective-permute-start | bytes 196616 | tf_op jit(solution)/shard_map/ppermute | solution.py:269
  100.1 10.8 %collective-permute-start.10 = (f32[16,1024]{1,0:T(8,128)S(1)}, f32[16,1024]{1,0:T(8,128)S(1)}, u32[]{:S(2)}, u32[]{:S(2)}) collective-permute-start(f32[16,1024]{1,0:T(8,128)S(1)} %collective-permute-done.6.refs_2_), channel_id=1, source_target_pairs={{0,8},{1,9},{2,10},{3,11},{4,12},{5,13},{6,14},{7,15},{8,0},{9,1},... | collective-permute-start | bytes 196616 | tf_op jit(solution)/shard_map/ppermute | solution.py:269
  100.4 10.6 %collective-permute-start.11 = (f32[16,1024]{1,0:T(8,128)S(1)}, f32[16,1024]{1,0:T(8,128)S(1)}, u32[]{:S(2)}, u32[]{:S(2)}) collective-permute-start(f32[16,1024]{1,0:T(8,128)S(1)} %collective-permute-done.7.refs_3_), channel_id=1, source_target_pairs={{0,8},{1,9},{2,10},{3,11},{4,12},{5,13},{6,14},{7,15},{8,0},{9,1},... | collective-permute-start | bytes 196616 | tf_op jit(solution)/shard_map/ppermute | solution.py:269
  100.6 10.3 %collective-permute-start.9 = (f32[16,1024]{1,0:T(8,128)S(1)}, f32[16,1024]{1,0:T(8,128)S(1)}, u32[]{:S(2)}, u32[]{:S(2)}) collective-permute-start(f32[16,1024]{1,0:T(8,128)S(1)} %collective-permute-done.5.refs_1_), channel_id=1, source_target_pairs={{0,8},{1,9},{2,10},{3,11},{4,12},{5,13},{6,14},{7,15},{8,0},{9,1},... | collective-permute-start | bytes 196616 | tf_op jit(solution)/shard_map/ppermute | solution.py:269

commit v3 on v2

v3 whole, which is shorter than its diff:
```python
import jax
import jax.numpy as jnp
from jax import lax
from jax.experimental import pallas as pl
from jax.experimental.pallas import tpu as pltpu
from jax.sharding import PartitionSpec as P

F32 = jnp.float32
BF16 = jnp.bfloat16
TILE = 256
WIDE = 512
CHUNK = 16
SLOTS = 4
BLOCK = 128
HALF = 64
CORE, Z_HIGH, Z_LOW = 8, 16, 4
X_STEPS = (32, 96, 64)
Y_STEPS = (1, 3, 2)


def halves(x):
    high = x.astype(BF16)
    return high, (x - high.astype(F32)).astype(BF16)


def dot(a, b, ca=1, cb=0):
    return lax.dot_general(a, b, (((ca,), (cb,)), ((), ())), preferred_element_type=F32)


def dot3(a, b):
    m, n = a.shape[0], b.shape[1]
    both = dot(jnp.concatenate(halves(a), axis=0), jnp.concatenate(halves(b), axis=1))
    return both[:m, :n] + (both[:m, n:] + both[m:, :n])


def span(start, size):
    return pl.ds(start if isinstance(start, int) else pl.multiple_of(start, size), size)


def sweep(first, lead_ref, tiles_ref, slot_ref, even_ref, odd_ref, sem, put_sem, prepare, use, high_ref, low_ref):
    steps = tiles_ref.shape[0] // TILE
    total = tiles_ref.shape[1]
    index = lax.broadcasted_iota(jnp.int32, (CHUNK, total), 0)

    def fetch(step):
        slot = step % SLOTS if isinstance(step, int) else lax.rem(step, SLOTS)
        return pltpu.make_async_copy(tiles_ref.at[span(step * TILE, TILE), :], slot_ref.at[slot], sem.at[slot])

    def put(step, ref, at):
        part = span(step * TILE, TILE)
        return (
            pltpu.make_async_copy(ref.at[0], high_ref.at[part, :], put_sem.at[at, 0]),
            pltpu.make_async_copy(ref.at[1], low_ref.at[part, :], put_sem.at[at, 1]),
        )

    def halve(step, ref, quarter):
        slot = step % SLOTS if isinstance(step, int) else lax.rem(step, SLOTS)
        start = lead_ref[...] - (first + step * TILE)
        for at in range(quarter * TILE // 4, (quarter + 1) * TILE // 4, CHUNK):
            x = slot_ref[slot, at : at + CHUNK, :]
            lead = start - at
            x = jnp.where(index < lead, 0.0, jnp.where(index == lead, 1.0, x))
            high, low = halves(x)
            ref[0, at : at + CHUNK, :] = high
            ref[1, at : at + CHUNK, :] = low

    def work(step, now, later):
        left = prepare(step, now)
        for quarter in range(4):
            use(left, now, quarter)
            if later is not None:
                halve(step + 1, later, quarter)

    for step in range(SLOTS - 1):
        fetch(step).start()
    fetch(0).wait()
    for quarter in range(4):
        halve(0, even_ref, quarter)
    for copy in put(0, even_ref, 0):
        copy.start()

    @pl.loop(0, steps // 2 - 1)
    def _(pair):
        for step, now, later, at in ((2 * pair, even_ref, odd_ref, 1), (2 * pair + 1, odd_ref, even_ref, 0)):

            @pl.when(step + SLOTS - 1 < steps)
            def _():
                fetch(step + SLOTS - 1).start()

            @pl.when(step >= 1)
            def _():
                for copy in put(step - 1, later, at):
                    copy.wait()

            fetch(step + 1).wait()
            work(step, now, later)
            for copy in put(step + 1, later, at):
                copy.start()

    fetch(steps - 1).wait()
    for copy in put(steps - 3, odd_ref, 1):
        copy.wait()
    work(steps - 2, even_ref, odd_ref)
    for copy in put(steps - 1, odd_ref, 1):
        copy.start()
    work(steps - 1, odd_ref, None)
    for copy in put(steps - 2, even_ref, 0) + put(steps - 1, odd_ref, 1):
        copy.wait()


def add_product(sum_ref):
    count, total = sum_ref.shape
    part = total // 4

    def use(left, ref, quarter):
        at = slice(quarter * part, (quarter + 1) * part)
        both = dot(left, ref[0, :, at])
        sum_ref[:, at] += both[:count] + (both[count:] + dot(left[:count], ref[1, :, at]))

    return use


def gram_kernel(
    place_ref, lead_ref, tiles_ref, high_ref, low_ref, keep_ref, send_ref, slot_ref, even_ref, odd_ref, sum_ref, pack_ref, sem, put_sem
):
    total = tiles_ref.shape[1]
    first, core, x_at, col = place_ref[0], place_ref[1], place_ref[2], place_ref[3]
    lane_half = lax.broadcasted_iota(jnp.int32, (1, BLOCK), 1) // HALF
    turns = []
    for turn in (lax.rem(col, 4), 7 - lax.rem(col, 4)):
        parity = lax.rem(turn, 2)
        from_a = jnp.where(lane_half == parity, 1.0, 0.0).astype(BF16)
        from_b = jnp.where(lane_half == parity, 0.0, 1.0).astype(BF16)
        turns.append((parity, turn // 2, (15 - turn) // 2, from_a, from_b))

    def prepare(step, ref):
        def chosen(which, block_a, block_b, from_a, from_b):
            a = ref[which, :, span(block_a * BLOCK, BLOCK)]
            b = ref[which, :, span(block_b * BLOCK, BLOCK)]
            return a * from_a + b * from_b

        return jnp.concatenate([chosen(which, *turn[1:]) for which in (0, 1) for turn in turns], axis=1).T

    sum_ref[...] = jnp.zeros_like(sum_ref)
    sweep(
        first, lead_ref, tiles_ref, slot_ref, even_ref, odd_ref, sem, put_sem, prepare, add_product(sum_ref), high_ref, low_ref
    )

    for p, (parity, block_a, block_b, _, _) in enumerate(turns):
        pack_ref[p, :, :total] = sum_ref[span(p * BLOCK + (1 - parity) * HALF, HALF), :]
        for m in range(4):

            @pl.when(m <= block_a)
            def _():
                pack_ref[p, :, span((block_b + 1 + m) * BLOCK, BLOCK)] = sum_ref[
                    span(p * BLOCK + parity * HALF, HALF), m * BLOCK : (m + 1) * BLOCK
                ]

        for k in range(4):
            at = jnp.bitwise_xor(x_at, k) * 8
            to = slice(k * 16 + p * 8, k * 16 + p * 8 + 8)
            keep_ref[to, :] = pack_ref[p, span(core * 32 + at, 8), :]
            send_ref[to, :] = pack_ref[p, span((1 - core) * 32 + at, 8), :]


def product_copies(from_refs, to_refs, first, sem):
    rows = to_refs[0].shape[0]
    return [
        [
            pltpu.make_async_copy(a.at[first + at : first + at + WIDE, :], b.at[at : at + WIDE, :], sem.at[at // WIDE, i])
            for i, (a, b) in enumerate(zip(from_refs, to_refs))
        ]
        for at in range(0, rows, WIDE)
    ]


def product(vec_ref, from_refs, to_refs, first, sem, sum_ref, total):
    copies = product_copies(from_refs, to_refs, first, sem)
    count = vec_ref.shape[0]
    for pair in copies:
        for copy in pair:
            copy.start()
    for step, pair in enumerate(copies):
        at = step * WIDE
        left = jnp.concatenate(halves(vec_ref[:, first + at : first + at + WIDE]), axis=0)
        for copy in pair:
            copy.wait()
        both = dot(left, to_refs[0][at : at + WIDE, :])
        added = both[:count] + (both[count:] + dot(left[:count], to_refs[1][at : at + WIDE, :]))
        if total is not None:
            added = added + total[...]
        total = sum_ref
        sum_ref[...] = added


def first_product_kernel(_, vec_ref, from_high_ref, from_low_ref, high_ref, low_ref, sum_ref, sem):
    product(vec_ref, (from_high_ref, from_low_ref), (high_ref, low_ref), 0, sem, sum_ref, None)


def last_product_kernel(
    _, place_ref, total_ref, vec_ref, from_high_ref, from_low_ref, high_ref, low_ref, keep_ref, send_ref, sum_ref, sem
):
    first = vec_ref.shape[1] - high_ref.shape[0]
    product(vec_ref, (from_high_ref, from_low_ref), (high_ref, low_ref), first, sem, sum_ref, total_ref)
    core, x_at = place_ref[1], place_ref[2]
    for k in range(4):
        at = jnp.bitwise_xor(x_at, k) * 16
        keep_ref[k * 16 : k * 16 + 16, :] = sum_ref[span(core * 64 + at, 16), :]
        send_ref[k * 16 : k * 16 + 16, :] = sum_ref[span((1 - core) * 64 + at, 16), :]


def add_kernel(_, a_ref, b_ref, out_ref):
    out_ref[...] = a_ref[...] + b_ref[...]


def join_kernel(_, *refs):
    *parts, out_ref = refs
    at = 0
    for part in parts:
        out_ref[at : at + part.shape[0], :] = part[...]
        at += part.shape[0]


def sum_kernel(*refs):
    *parts, out_ref = refs
    a, b, c, d = (part[...] for part in parts)
    out_ref[...] = (a + b) + (c + d)


def reorder_kernel(order_ref, vec_ref, out_ref):
    order = order_ref[...]

    @pl.loop(0, vec_ref.shape[1] // WIDE)
    def _(step):
        part = span(step * WIDE, WIDE)
        value = vec_ref[:, part]
        v1 = value.astype(BF16)
        rest = value - v1.astype(F32)
        v2, v3 = halves(rest)
        out_ref[:, part] = dot(order, v1) + (dot(order, v2) + dot(order, v3))


def inverse_kernel(place_ref, *refs):
    *gram_refs, high_ref, low_ref, stage_ref, lower_ref, out_ref = refs
    total = out_ref.shape[0]
    blocks = total // BLOCK
    core, x_at, col = place_ref[1], place_ref[2], place_ref[3]
    r = lax.broadcasted_iota(jnp.int32, (BLOCK, BLOCK), 0)
    c = lax.broadcasted_iota(jnp.int32, (BLOCK, BLOCK), 1)
    for j in range(8):
        to = jnp.bitwise_xor(core, j // 4) * 4 + jnp.bitwise_xor(lax.rem(col, 4), j % 4)
        stage_ref[to] = gram_refs[j // 4][j % 4 * 64 : j % 4 * 64 + 64, :]
    for q in range(8):
        width = (q // 2 + 1) * BLOCK
        rest = 9 * BLOCK - width
        for k in range(8):
            at = jnp.bitwise_xor(x_at, k % 4) * 16 + q // 4 * 8
            piece = stage_ref[k // 4 * 4 + (q if q < 4 else 7 - q), span(at, 8), :]
            top, low = (15 - q) * HALF + k * 8, q * HALF + k * 8
            lower_ref[top : top + 8, :rest] = piece[:, :rest]
            lower_ref[low : low + 8, :width] = piece[:, rest:]
    out_ref[...] = jnp.zeros_like(out_ref)
    lows, inverses = [], []
    for q in range(blocks):
        part = pl.ds(q * BLOCK, BLOCK)
        square = lower_ref[part, part]
        lows.append(square)
        inverses.append(jnp.where(r == c, 2.0 / square, 0.0))
    same = r // HALF == c // HALF
    scales = [jnp.sum(inverses[q], axis=0, keepdims=True) for q in range(blocks)]
    scaled = [jnp.sum(inverses[q], axis=1, keepdims=True) for q in range(blocks)]
    powers = [jnp.where(same & (r > c), -lows[q] * scaled[q], 0.0) for q in range(blocks)]
    identity = jnp.where(r == c, 1.0, 0.0)
    products = [identity + powers[q] for q in range(blocks)]
    for _ in range(5):
        powers = [dot3(powers[q], powers[q]) for q in range(blocks)]
        products = [products[q] + dot3(products[q], powers[q]) for q in range(blocks)]
    inverses = [products[q] * scales[q] for q in range(blocks)]
    pair = (r >= HALF) & (c < HALF)
    mids = [dot3(jnp.where(pair, lows[q], 0.0), inverses[q]) for q in range(blocks)]
    inverses = [inverses[q] - dot3(inverses[q], mids[q]) for q in range(blocks)]
    size = BLOCK
    for q in range(blocks):
        part = pl.ds(q * BLOCK, BLOCK)
        out_ref[part, part] = inverses[q]
    while size < total:
        for start in range(0, total, 2 * size):
            a, b = pl.ds(start, size), pl.ds(start + size, size)
            mid = dot3(lower_ref[b, a], out_ref[a, a])
            out_ref[b, a] = -dot3(out_ref[b, b], mid)
        size *= 2
    high, low = halves(out_ref[...])
    high_ref[...] = high
    low_ref[...] = low


def change_kernel(place_ref, order_ref, *refs):
    mine_ref, other_ref, th_ref, tl_ref, vec_ref, *held_refs, out_ref, sum_ref, w_ref, put_ref, put_sem = refs
    count, rows = vec_ref.shape
    core, x_at = place_ref[1], place_ref[2]
    for k in range(4):
        at = jnp.bitwise_xor(x_at, k) * 16
        sum_ref[span(core * 64 + at, 16), :] = mine_ref[k * 16 : k * 16 + 16, :]
        sum_ref[span((1 - core) * 64 + at, 16), :] = other_ref[k * 16 : k * 16 + 16, :]
    yh, yl = halves(sum_ref[...])
    both = dot(jnp.concatenate([yh, yl], axis=0), th_ref[...])
    weighted = both[:count] + (both[count:] + dot(yh, tl_ref[...]))
    order = order_ref[...]
    wh, wl = halves(weighted)
    w_ref[:count, :] = dot(order, wh).astype(BF16)
    w_ref[count:, :] = dot(order, wl).astype(BF16)

    copies = []
    for step, at in enumerate(range(0, rows, WIDE)):
        part = slice(at, at + WIDE)
        split = held_refs[0].shape[0]
        high_ref, low_ref = held_refs[:2] if at < split else held_refs[2:]
        held = slice(at, at + WIDE) if at < split else slice(at - split, at - split + WIDE)
        both = dot(w_ref[...], high_ref[held, :], 1, 1)
        change = both[:count] + (both[count:] + dot(w_ref[:count, :], low_ref[held, :], 1, 1))
        put_ref[:, part] = vec_ref[:, part] - change
        copies.append(pltpu.make_async_copy(put_ref.at[:, part], out_ref.at[:, part], put_sem.at[step]))
        copies[-1].start()
    for copy in copies:
        copy.wait()


def params(mib):
    return pltpu.CompilerParams(vmem_limit_bytes=mib << 20)


def cost(flops, moved):
    return pl.CostEstimate(flops=flops, bytes_accessed=moved, transcendentals=0)


def swap(x, bits):
    return lax.ppermute(x, ("row", "col"), [(i, i ^ bits) for i in range(128)])


def gather(x, steps):
    near, far, across = (swap(x, bits) for bits in steps)
    return [x, near, across, far]


def small(kernel, shape, name, before, parts):
    after = [pl.BlockSpec(memory_space=pl.ANY)] * len(before)
    return pl.pallas_call(
        kernel,
        in_specs=after + [pl.BlockSpec(memory_space=pltpu.VMEM)] * len(parts),
        out_specs=pl.BlockSpec(memory_space=pltpu.VMEM),
        out_shape=jax.ShapeDtypeStruct(shape, F32),
        compiler_params=params(4),
        cost_estimate=cost(1 << 16, 1 << 16),
        name=name,
    )(*before, *parts)


def per_device(source_vectors, source_slot, reflectors, panel_offsets):
    row_count = lax.axis_size("row")
    col_count = lax.axis_size("col")
    src_block = source_vectors.shape[0]
    rows_dev, total = reflectors.shape
    width = total // panel_offsets.shape[0]
    count = src_block * row_count

    row = lax.axis_index("row")
    place = jnp.stack([row * rows_dev, row % 2, row // 4, lax.axis_index("col")]).astype(jnp.int32)
    lead = (panel_offsets[:, None] + jnp.arange(width, dtype=jnp.int32)[None, :]).reshape(1, total)
    placing = source_slot // (col_count * src_block) * src_block + source_slot % src_block
    order = (placing[:, None] == jnp.arange(count, dtype=jnp.int32)[None, :]).astype(BF16)

    smem = pl.BlockSpec(memory_space=pltpu.SMEM)
    vmem = pl.BlockSpec(memory_space=pltpu.VMEM)
    hbm = pl.BlockSpec(memory_space=pltpu.HBM)

    shaped = source_vectors.reshape(src_block, row_count, rows_dev).transpose(1, 0, 2)
    received = lax.all_to_all(shaped, "row", 0, 0, tiled=True).reshape(count, rows_dev)

    packed = 9 * BLOCK
    halved = pltpu.HBM((rows_dev, total), BF16)
    steps = rows_dev // WIDE
    high, low, keep, send = pl.pallas_call(
        gram_kernel,
        in_specs=[smem, vmem, hbm],
        out_specs=[hbm, hbm, vmem, vmem],
        out_shape=[halved, halved] + [jax.ShapeDtypeStruct((HALF, packed), F32)] * 2,
        scratch_shapes=[
            pltpu.VMEM((SLOTS, TILE, total), F32),
            pltpu.VMEM((2, TILE, total), BF16),
            pltpu.VMEM((2, TILE, total), BF16),
            pltpu.VMEM((2 * BLOCK, total), F32),
            pltpu.VMEM((2, HALF, packed), F32),
            pltpu.SemaphoreType.DMA((SLOTS,)),
            pltpu.SemaphoreType.DMA((2, 2)),
        ],
        compiler_params=params(20),
        cost_estimate=cost(12 * rows_dev * BLOCK * total, 8 * rows_dev * total),
        name="gram",
    )(place, lead, pltpu.with_memory_space_constraint(reflectors, pltpu.HBM))
    both = keep + swap(send, CORE)
    part = both[:16]
    for k, bits in ((1, 32), (3, 96), (2, 64)):
        part = part + swap(both[k * 16 : k * 16 + 16], bits)
    near = swap(part, Z_HIGH)

    after = pl.BlockSpec(memory_space=pl.ANY)
    high = pltpu.with_memory_space_constraint(high, pltpu.HBM)
    low = pltpu.with_memory_space_constraint(low, pltpu.HBM)
    split = steps // 2 * WIDE
    first_held, last_held = ([pltpu.VMEM((n, total), BF16)] * 2 for n in (split, rows_dev - split))
    summed = jax.ShapeDtypeStruct((count, total), F32)
    semaphores = pltpu.SemaphoreType.DMA((steps, 2))
    first_high, first_low, sums = pl.pallas_call(
        first_product_kernel,
        in_specs=[after, vmem, hbm, hbm],
        out_specs=[vmem] * 3,
        out_shape=first_held + [summed],
        scratch_shapes=[semaphores],
        compiler_params=params(8),
        cost_estimate=cost(3 * rows_dev * count * total, 2 * rows_dev * total),
        name="product_first",
    )(part, received, high, low)
    piece = small(add_kernel, (16, packed), "gram_z", [sums], [part, near])
    pieces = gather(piece, X_STEPS)
    last_high, last_low, keep, send = pl.pallas_call(
        last_product_kernel,
        in_specs=[after, smem, vmem, vmem, hbm, hbm],
        out_specs=[vmem] * 4,
        out_shape=last_held + [jax.ShapeDtypeStruct((count // 2, total), F32)] * 2,
        scratch_shapes=[pltpu.VMEM((count, total), F32), semaphores],
        compiler_params=params(8),
        cost_estimate=cost(3 * rows_dev * count * total, 2 * rows_dev * total),
        name="product_last",
    )(piece, place, sums, received, high, low)
    grams = small(join_kernel, (64, packed), "gram_x", [keep], pieces)
    pieces = gather(grams, Y_STEPS)

    ordered = pl.pallas_call(
        reorder_kernel,
        in_specs=[vmem, vmem],
        out_specs=vmem,
        out_shape=jax.ShapeDtypeStruct((count, rows_dev), F32),
        compiler_params=params(8),
        cost_estimate=cost(6 * rows_dev * count * count, 16 * rows_dev * count),
        name="reorder",
    )(order, received)
    both = small(add_kernel, (count // 2, total), "sum_core", [grams], [keep, swap(send, CORE)])
    parts = [both[: count // 8]]
    for k, bits in ((1, 32), (2, 64), (3, 96)):
        parts.append(swap(both[k * count // 8 : (k + 1) * count // 8], bits))
    sums = small(sum_kernel, (count // 8, total), "sum_x", [], parts)
    sums = small(add_kernel, (count // 8, total), "sum_z", [ordered], [sums, swap(sums, Z_HIGH)])
    mine = small(join_kernel, (count // 2, total), "sum_join", [ordered], gather(sums, X_STEPS))
    other = swap(mine, CORE)
    pieces = small(join_kernel, (256, packed), "gram_y", [mine], pieces)
    t_high, t_low = pl.pallas_call(
        inverse_kernel,
        in_specs=[smem] + [vmem] * 2,
        out_specs=[vmem] * 2,
        out_shape=[jax.ShapeDtypeStruct((total, total), BF16)] * 2,
        scratch_shapes=[
            pltpu.VMEM((8, 64, packed), F32),
            pltpu.VMEM((total, total), F32),
            pltpu.VMEM((total, total), F32),
        ],
        compiler_params=params(18),
        cost_estimate=cost(6 * total**3, 8 * total**2),
        name="inverse",
    )(place, pieces, swap(pieces, CORE))
    return pl.pallas_call(
        change_kernel,
        in_specs=[smem] + [vmem] * 10,
        out_specs=hbm,
        out_shape=jax.ShapeDtypeStruct((count, rows_dev), F32),
        scratch_shapes=[
            pltpu.VMEM((count, total), F32),
            pltpu.VMEM((2 * count, total), BF16),
            pltpu.VMEM((count, rows_dev), F32),
            pltpu.SemaphoreType.DMA((steps,)),
        ],
        compiler_params=params(12),
        cost_estimate=cost(6 * rows_dev * count * total, 4 * rows_dev * count),
        name="change",
    )(place, order, mine, other, t_high, t_low, ordered, first_high, first_low, last_high, last_low)


def solution(mesh):
    in_specs = (P(("row", "col"), None), P("col"), P("row", None), P())
    out_specs = P("col", "row")
    return jax.shard_map(per_device, mesh=mesh, in_specs=in_specs, out_specs=out_specs, check_vma=False)
```

time: 122 us -> 109 us (0.89)
  waiting for transfers between devices: 25.7 us -> 20.8 us
  Pallas kernels: 52.1 us -> 48.1 us
  starting transfers between devices: 43.3 us -> 39.4 us
    ppermute x28 -> x21, waiting for transfers between devices: 25.7 us -> 20.8 us  [swap(): return lax.ppermute(x, ('row', 'col'), [(i, i ^ bits) for i in range(128)])]
    ppermute x28 -> x21, starting transfers between devices: 34.1 us -> 30.1 us  [swap(): return lax.ppermute(x, ('row', 'col'), [(i, i ^ bits) for i in range(128)])]
    pallas_call x6 -> x12, Pallas kernels: 48.3 us -> 45.5 us  [the longest x1 19.9 us: per_device(): pl.pallas_call(gram_kernel, in_specs=[smem, vmem, hbm], out_specs=[hbm, h...]
    pallas_call x1, Pallas kernels: 3.83 us -> 2.59 us  [per_device(): pl.pallas_call(reorder_kernel, in_specs=[vmem, vmem], out_specs=vmem, out...]
  transfers between devices with their start and end apart: 29 -> 22, of which waited for: 7 -> 12; matrix products, arithmetic and copies ran while one was open for 0% -> 0% of each run, Pallas kernels for 34% -> 32%
where the time goes in v3:
time: 109 us
  Pallas kernels  48.1 us (44%)
  starting transfers between devices  39.4 us (36%)
  waiting for transfers between devices  20.8 us (19%)
    ppermute x21, starting transfers between devices, swap(): return lax.ppermute(x, ('row', 'col'), [(i, i ^ bits) for i in range(128)])  30.1 us
    ppermute x21, waiting for transfers between devices, swap(): return lax.ppermute(x, ('row', 'col'), [(i, i ^ bits) for i in range(128)])  20.8 us
    pallas_call x1, Pallas kernels, per_device(): pl.pallas_call(gram_kernel, in_specs=[smem, vmem, hbm], out_specs=[hbm, h...  19.9 us
    all_to_all x1, starting transfers between devices, per_device(): lax.all_to_all(shaped, 'row', 0, 0, tiled=True).reshape(count, rows_dev)  9.26 us
    pallas_call x1, Pallas kernels, per_device(): pl.pallas_call(change_kernel, in_specs=[smem] + [vmem] * 10, out_specs=hb...  8.12 us
    pallas_call x1, Pallas kernels, per_device(): pl.pallas_call(inverse_kernel, in_specs=[smem] + [vmem] * 2, out_specs=[v...  7.76 us
    pallas_call x1, Pallas kernels, per_device(): pl.pallas_call(last_product_kernel, in_specs=[after, smem, vmem, vmem, hb...  5.32 us
    pallas_call x1, Pallas kernels, per_device(): pl.pallas_call(first_product_kernel, in_specs=[after, vmem, hbm, hbm], ou...  4.14 us
  transfers between devices with their start and end apart: 22, of which 12 were waited for; matrix products, arithmetic and copies ran while one was open for 0% of the time, Pallas kernels for 32%

profile of v3, /device:TPU:1, one launch (start us, length us, event | category | flops | bytes accessed | tf_op | source)
XLA Modules:
  0.0 109.0 jit_solution(15844309120981162406)
XLA Ops:
  0.0 9.3 %all-to-all-start = ((f32[16,8,4608]{2,1,0:T(8,128)}), f32[16,8,4608]{2,1,0:T(8,128)S(1)}, u32[]{:S(2)}, u32[]{:S(2)}) async-start(f32[16,8,4608]{2,1,0:T(8,128)} %bitcast.11), calls=%async_computation | async-start | bytes 4718592 | tf_op jit(solution)/shard_map/all_to_all | solution.py:377
  9.5 19.9 %gram.1 = (bf16[4608,1024]{1,0:T(8,128)(2,1)}, bf16[4608,1024]{1,0:T(8,128)(2,1)}, f32[64,1152]{1,0:T(8,128)S(1)}, f32[64,1152]{1,0:T(8,128)S(1)}) custom-call(s32[4]{0:T(128)S(1)} %pad_add_fusion.place_ref, s32[1,1024]{1,0:T(1,128)S(1)} %add.56.lead_ref, f32[4608,1024]{1,0:T(8,128)} %tiles_ref.1), custom_call_target="tpu_custom_call" | custom-call | flops 7247757312 | bytes 37748736 | tf_op jit(solution)/shard_map/gram/pallas_call | solution.py:382
  29.6 1.5 %collective-permute-done = f32[64,1152]{1,0:T(8,128)S(1)} collective-permute-done((f32[64,1152]{1,0:T(8,128)S(1)}, f32[64,1152]{1,0:T(8,128)S(1)}, u32[]{:S(2)}, u32[]{:S(2)}) %collective-permute-start) | collective-permute-done | bytes 294944 | tf_op jit(solution)/shard_map/ppermute | solution.py:337
  31.2 1.5 %collective-permute-start.1 = (f32[16,1152]{1,0:T(8,128)S(1)}, f32[16,1152]{1,0:T(8,128)S(1)}, u32[]{:S(2)}, u32[]{:S(2)}) collective-permute-start(f32[16,1152]{1,0:T(8,128)S(1)} %get-tuple-element.31), channel_id=1, source_target_pairs={{0,32},{1,33},{2,34},{3,35},{4,36},{5,37},{6,38},{7,39},{8,40},{9,... | collective-permute-start | bytes 221192 | tf_op jit(solution)/shard_map/ppermute | solution.py:337
  32.6 1.8 %collective-permute-start.2 = (f32[16,1152]{1,0:T(8,128)S(1)}, f32[16,1152]{1,0:T(8,128)S(1)}, u32[]{:S(2)}, u32[]{:S(2)}) collective-permute-start(f32[16,1152]{1,0:T(8,128)S(1)} %get-tuple-element.33), channel_id=1, source_target_pairs={{0,96},{1,97},{2,98},{3,99},{4,100},{5,101},{6,102},{7,103},{8,104... | collective-permute-start | bytes 221192 | tf_op jit(solution)/shard_map/ppermute | solution.py:337
  34.4 0.6 collective-permute-start.3
  35.0 3.5 %collective-permute-done.1 = f32[16,1152]{1,0:T(8,128)S(1)} collective-permute-done((f32[16,1152]{1,0:T(8,128)S(1)}, f32[16,1152]{1,0:T(8,128)S(1)}, u32[]{:S(2)}, u32[]{:S(2)}) %collective-permute-start.1) | collective-permute-done | bytes 73760 | tf_op jit(solution)/shard_map/ppermute | solution.py:337
  38.6 5.6 %collective-permute-done.2 = f32[16,1152]{1,0:T(8,128)S(1)} collective-permute-done((f32[16,1152]{1,0:T(8,128)S(1)}, f32[16,1152]{1,0:T(8,128)S(1)}, u32[]{:S(2)}, u32[]{:S(2)}) %collective-permute-start.2) | collective-permute-done | bytes 73760 | tf_op jit(solution)/shard_map/ppermute | solution.py:337
  44.2 1.0 collective-permute-done.3
  45.3 4.1 %product_first.1 = (bf16[2048,1024]{1,0:T(8,128)(2,1)S(1)}, bf16[2048,1024]{1,0:T(8,128)(2,1)S(1)}, f32[128,1024]{1,0:T(8,128)S(1)}) custom-call(f32[16,1152]{1,0:T(8,128)S(1)} %fusion.1._.a_ref, f32[128,4608]{1,0:T(8,128)S(1)} %bitcast.8, bf16[4608,1024]{1,0:T(8,128)(2,1)} %get-tuple-element.20.from_high_ref, bf16[4608,1024]{1,0:T(8,128)(2,1)} %get-tuple-element.21.from_low_ref), custom_call_target="tpu_custom_call" | custom-call | flops 1811939328 | bytes 9437184 | tf_op jit(solution)/shard_map/product_first/pallas_call | solution.py:413
  49.4 0.5 collective-permute-done.4.b_ref
  50.0 5.3 %product_last.1 = (bf16[2560,1024]{1,0:T(8,128)(2,1)S(1)}, bf16[2560,1024]{1,0:T(8,128)(2,1)S(1)}, f32[64,1024]{1,0:T(8,128)S(1)}, f32[64,1024]{1,0:T(8,128)S(1)}) custom-call(f32[16,1152]{1,0:T(8,128)S(1)} %gram_z.1._.refs_0_, s32[4]{0:T(128)S(1)} %pad_add_fusion.place_ref, f32[128,1024]{1,0:T(8,128)S(1)} %get-tuple-element.22._.total_ref, ...), custom_call_target="tpu_custom_call" | custom-call | flops 1811939328 | bytes 9437184 | tf_op jit(solution)/shard_map/product_last/pallas_call | solution.py:425
  55.3 2.1 %collective-permute-start.8 = (f32[64,1024]{1,0:T(8,128)S(1)}, f32[64,1024]{1,0:T(8,128)S(1)}, u32[]{:S(2)}, u32[]{:S(2)}) collective-permute-start(f32[64,1024]{1,0:T(8,128)S(1)} %get-tuple-element.24), channel_id=1, source_target_pairs={{0,8},{1,9},{2,10},{3,11},{4,12},{5,13},{6,14},{7,15},{8,0},{9,1},... | collective-permute-start | bytes 786440 | tf_op jit(solution)/shard_map/ppermute | solution.py:337
  57.4 1.4 %collective-permute-start.6 = (f32[16,1152]{1,0:T(8,128)S(1)}, f32[16,1152]{1,0:T(8,128)S(1)}, u32[]{:S(2)}, u32[]{:S(2)}) collective-permute-start(f32[16,1152]{1,0:T(8,128)S(1)} %gram_z.1._.refs_0_), channel_id=1, source_target_pairs={{0,64},{1,65},{2,66},{3,67},{4,68},{5,69},{6,70},{7,71},{8,72},{9,... | collective-permute-start | bytes 221192 | tf_op jit(solution)/shard_map/ppermute | solution.py:337
  58.9 2.4 %collective-permute-start.7 = (f32[16,1152]{1,0:T(8,128)S(1)}, f32[16,1152]{1,0:T(8,128)S(1)}, u32[]{:S(2)}, u32[]{:S(2)}) collective-permute-start(f32[16,1152]{1,0:T(8,128)S(1)} %gram_z.1._.refs_0_), channel_id=1, source_target_pairs={{0,96},{1,97},{2,98},{3,99},{4,100},{5,101},{6,102},{7,103},{8,104... | collective-permute-start | bytes 221192 | tf_op jit(solution)/shard_map/ppermute | solution.py:337
  61.3 1.3 %collective-permute-done.6.refs_2_ = f32[16,1152]{1,0:T(8,128)S(1)} collective-permute-done((f32[16,1152]{1,0:T(8,128)S(1)}, f32[16,1152]{1,0:T(8,128)S(1)}, u32[]{:S(2)}, u32[]{:S(2)}) %collective-permute-start.6) | collective-permute-done | bytes 73760 | tf_op jit(solution)/shard_map/ppermute | solution.py:337
  62.6 1.6 %collective-permute-done.7.refs_3_ = f32[16,1152]{1,0:T(8,128)S(1)} collective-permute-done((f32[16,1152]{1,0:T(8,128)S(1)}, f32[16,1152]{1,0:T(8,128)S(1)}, u32[]{:S(2)}, u32[]{:S(2)}) %collective-permute-start.7) | collective-permute-done | bytes 73760 | tf_op jit(solution)/shard_map/ppermute | solution.py:337
  64.3 1.9 %collective-permute-start.10 = (f32[16,1024]{1,0:T(8,128)S(1)}, f32[16,1024]{1,0:T(8,128)S(1)}, u32[]{:S(2)}, u32[]{:S(2)}) collective-permute-start(f32[16,1024]{1,0:T(8,128)S(1)} %get-tuple-element.35), channel_id=1, source_target_pairs={{0,64},{1,65},{2,66},{3,67},{4,68},{5,69},{6,70},{7,71},{8,72},{9,... | collective-permute-start | bytes 196616 | tf_op jit(solution)/shard_map/ppermute | solution.py:337
  66.2 0.7 collective-permute-start.11
  67.4 1.4 %collective-permute-start.17 = (f32[64,1152]{1,0:T(8,128)S(1)}, f32[64,1152]{1,0:T(8,128)S(1)}, u32[]{:S(2)}, u32[]{:S(2)}) collective-permute-start(f32[64,1152]{1,0:T(8,128)S(1)} %gram_x.1._.refs_0_), channel_id=1, source_target_pairs={{0,1},{1,0},{2,3},{3,2},{4,5},{5,4},{6,7},{7,6},{8,9},{9,8},{10,11... | collective-permute-start | bytes 884744 | tf_op jit(solution)/shard_map/ppermute | solution.py:337
  68.8 2.6 %collective-permute-start.18 = (f32[64,1152]{1,0:T(8,128)S(1)}, f32[64,1152]{1,0:T(8,128)S(1)}, u32[]{:S(2)}, u32[]{:S(2)}) collective-permute-start(f32[64,1152]{1,0:T(8,128)S(1)} %gram_x.1._.refs_0_), channel_id=1, source_target_pairs={{0,2},{1,3},{2,0},{3,1},{4,6},{5,7},{6,4},{7,5},{8,10},{9,11},{10,... | collective-permute-start | bytes 884744 | tf_op jit(solution)/shard_map/ppermute | solution.py:337
  71.8 1.7 %collective-permute-start.12 = (f32[16,1024]{1,0:T(8,128)S(1)}, f32[16,1024]{1,0:T(8,128)S(1)}, u32[]{:S(2)}, u32[]{:S(2)}) collective-permute-start(f32[16,1024]{1,0:T(8,128)S(1)} %sum_x.1.a_ref), channel_id=1, source_target_pairs={{0,16},{1,17},{2,18},{3,19},{4,20},{5,21},{6,22},{7,23},{8,24},{9,... | collective-permute-start | bytes 196616 | tf_op jit(solution)/shard_map/ppermute | solution.py:337
  73.6 2.6 %reorder.1._.refs_4_ = f32[128,4608]{1,0:T(8,128)S(1)} custom-call(bf16[128,128]{1,0:T(8,128)(2,1)S(1)} %fusion.2.order_ref, f32[128,4608]{1,0:T(8,128)S(1)} %bitcast.10), custom_call_target="tpu_custom_call" | custom-call | flops 452984832 | bytes 9437184 | tf_op jit(solution)/shard_map/reorder/pallas_call | solution.py:438
  76.5 0.9 collective-permute-start.13
  77.4 3.1 %collective-permute-start.14 = (f32[16,1024]{1,0:T(8,128)S(1)}, f32[16,1024]{1,0:T(8,128)S(1)}, u32[]{:S(2)}, u32[]{:S(2)}) collective-permute-start(f32[16,1024]{1,0:T(8,128)S(1)} %sum_z.1.refs_0_), channel_id=1, source_target_pairs={{0,64},{1,65},{2,66},{3,67},{4,68},{5,69},{6,70},{7,71},{8,72},{9,... | collective-permute-start | bytes 196616 | tf_op jit(solution)/shard_map/ppermute | solution.py:337
  80.5 2.2 %collective-permute-start.15 = (f32[16,1024]{1,0:T(8,128)S(1)}, f32[16,1024]{1,0:T(8,128)S(1)}, u32[]{:S(2)}, u32[]{:S(2)}) collective-permute-start(f32[16,1024]{1,0:T(8,128)S(1)} %sum_z.1.refs_0_), channel_id=1, source_target_pairs={{0,96},{1,97},{2,98},{3,99},{4,100},{5,101},{6,102},{7,103},{8,104... | collective-permute-start | bytes 196616 | tf_op jit(solution)/shard_map/ppermute | solution.py:337
  83.1 2.0 %collective-permute-done.15.refs_3_ = f32[16,1024]{1,0:T(8,128)S(1)} collective-permute-done((f32[16,1024]{1,0:T(8,128)S(1)}, f32[16,1024]{1,0:T(8,128)S(1)}, u32[]{:S(2)}, u32[]{:S(2)}) %collective-permute-start.15) | collective-permute-done | bytes 65568 | tf_op jit(solution)/shard_map/ppermute | solution.py:337
  85.2 0.7 collective-permute-done.19.refs_3_
  85.9 4.5 %collective-permute-start.20 = (f32[256,1152]{1,0:T(8,128)S(1)}, f32[256,1152]{1,0:T(8,128)S(1)}, u32[]{:S(2)}, u32[]{:S(2)}) collective-permute-start(f32[256,1152]{1,0:T(8,128)S(1)} %gram_y.1.refs_0_), channel_id=1, source_target_pairs={{0,8},{1,9},{2,10},{3,11},{4,12},{5,13},{6,14},{7,15},{8,0},{9,1},... | collective-permute-start | bytes 3538952 | tf_op jit(solution)/shard_map/ppermute | solution.py:337
  90.6 2.4 %collective-permute-done.20.refs_1_ = f32[256,1152]{1,0:T(8,128)S(1)} collective-permute-done((f32[256,1152]{1,0:T(8,128)S(1)}, f32[256,1152]{1,0:T(8,128)S(1)}, u32[]{:S(2)}, u32[]{:S(2)}) %collective-permute-start.20) | collective-permute-done | bytes 1179680 | tf_op jit(solution)/shard_map/ppermute | solution.py:337
  93.0 7.8 %inverse.1 = (bf16[1024,1024]{1,0:T(8,128)(2,1)S(1)}, bf16[1024,1024]{1,0:T(8,128)(2,1)S(1)}) custom-call(s32[4]{0:T(128)S(1)} %pad_add_fusion.place_ref, f32[256,1152]{1,0:T(8,128)S(1)} %gram_y.1.refs_0_, f32[256,1152]{1,0:T(8,128)S(1)} %collective-permute-done.20.refs_1_), custom_call_target="tpu_custom_call" | custom-call | flops 6442450944 | bytes 8388608 | tf_op jit(solution)/shard_map/inverse/pallas_call | solution.py:456
  100.7 8.1 %change.1 = f32[128,4608]{1,0:T(8,128)} custom-call(s32[4]{0:T(128)S(1)} %pad_add_fusion.place_ref, bf16[128,128]{1,0:T(8,128)(2,1)S(1)} %fusion.2.order_ref, f32[64,1024]{1,0:T(8,128)S(1)} %sum_join.1._.refs_0_, f32[64,1024]{1,0:T(8,128)S(1)} %collective-permute-done.16.refs_1_, bf16[1024,1024]{1,0:T(8,128)(2,1)S(1)} %get-tuple-element.25.refs_2_, ...), custom_call_target="tpu_custom_call" | custom-call | flops 3623878656 | bytes 2359296 | tf_op jit(solution)/shard_map/change/pallas_call | solution.py:470
  (38 shorter events, 2.6 us)
Async XLA Ops:
  0.0 9.3 %copy-start = (s32[16]{0:T(128)S(1)}, s32[16]{0:T(128)}, u32[]{:S(2)}) copy-start(s32[16]{0:T(128)} %param.7) | copy-start | bytes 196
  0.0 45.3 %all-to-all-start = ((f32[16,8,4608]{2,1,0:T(8,128)}), f32[16,8,4608]{2,1,0:T(8,128)S(1)}, u32[]{:S(2)}, u32[]{:S(2)}) async-start(f32[16,8,4608]{2,1,0:T(8,128)} %bitcast.11), calls=%async_computation | async-start | bytes 4718592 | tf_op jit(solution)/shard_map/all_to_all | solution.py:377
  29.4 1.7 %collective-permute-start = (f32[64,1152]{1,0:T(8,128)S(1)}, f32[64,1152]{1,0:T(8,128)S(1)}, u32[]{:S(2)}, u32[]{:S(2)}) collective-permute-start(f32[64,1152]{1,0:T(8,128)S(1)} %get-tuple-element.19), channel_id=1, source_target_pairs={{0,8},{1,9},{2,10},{3,11},{4,12},{5,13},{6,14},{7,15},{8,0},{9,1},... | collective-permute-start | bytes 884744 | tf_op jit(solution)/shard_map/ppermute | solution.py:337
  31.2 7.4 %collective-permute-start.1 = (f32[16,1152]{1,0:T(8,128)S(1)}, f32[16,1152]{1,0:T(8,128)S(1)}, u32[]{:S(2)}, u32[]{:S(2)}) collective-permute-start(f32[16,1152]{1,0:T(8,128)S(1)} %get-tuple-element.31), channel_id=1, source_target_pairs={{0,32},{1,33},{2,34},{3,35},{4,36},{5,37},{6,38},{7,39},{8,40},{9,... | collective-permute-start | bytes 221192 | tf_op jit(solution)/shard_map/ppermute | solution.py:337
  32.6 11.5 %collective-permute-start.2 = (f32[16,1152]{1,0:T(8,128)S(1)}, f32[16,1152]{1,0:T(8,128)S(1)}, u32[]{:S(2)}, u32[]{:S(2)}) collective-permute-start(f32[16,1152]{1,0:T(8,128)S(1)} %get-tuple-element.33), channel_id=1, source_target_pairs={{0,96},{1,97},{2,98},{3,99},{4,100},{5,101},{6,102},{7,103},{8,104... | collective-permute-start | bytes 221192 | tf_op jit(solution)/shard_map/ppermute | solution.py:337
  34.4 10.7 %collective-permute-start.3 = (f32[16,1152]{1,0:T(8,128)S(1)}, f32[16,1152]{1,0:T(8,128)S(1)}, u32[]{:S(2)}, u32[]{:S(2)}) collective-permute-start(f32[16,1152]{1,0:T(8,128)S(1)} %get-tuple-element.32), channel_id=1, source_target_pairs={{0,64},{1,65},{2,66},{3,67},{4,68},{5,69},{6,70},{7,71},{8,72},{9,... | collective-permute-start | bytes 221192 | tf_op jit(solution)/shard_map/ppermute | solution.py:337
  45.2 4.8 %collective-permute-start.4 = (f32[16,1152]{1,0:T(8,128)S(1)}, f32[16,1152]{1,0:T(8,128)S(1)}, u32[]{:S(2)}, u32[]{:S(2)}) collective-permute-start(f32[16,1152]{1,0:T(8,128)S(1)} %fusion.1._.a_ref), channel_id=1, source_target_pairs={{0,16},{1,17},{2,18},{3,19},{4,20},{5,21},{6,22},{7,23},{8,24},{9,... | collective-permute-start | bytes 221192 | tf_op jit(solution)/shard_map/ppermute | solution.py:337
  55.3 12.1 %copy-start.1 = (s32[128]{0:T(128)S(1)}, s32[128]{0:T(128)}, u32[]{:S(2)}) copy-start(s32[128]{0:T(128)} %param.5) | copy-start | bytes 1540
  55.3 8.9 %collective-permute-start.8 = (f32[64,1024]{1,0:T(8,128)S(1)}, f32[64,1024]{1,0:T(8,128)S(1)}, u32[]{:S(2)}, u32[]{:S(2)}) collective-permute-start(f32[64,1024]{1,0:T(8,128)S(1)} %get-tuple-element.24), channel_id=1, source_target_pairs={{0,8},{1,9},{2,10},{3,11},{4,12},{5,13},{6,14},{7,15},{8,0},{9,1},... | collective-permute-start | bytes 786440 | tf_op jit(solution)/shard_map/ppermute | solution.py:337
  57.4 3.9 %collective-permute-start.5 = (f32[16,1152]{1,0:T(8,128)S(1)}, f32[16,1152]{1,0:T(8,128)S(1)}, u32[]{:S(2)}, u32[]{:S(2)}) collective-permute-start(f32[16,1152]{1,0:T(8,128)S(1)} %gram_z.1._.refs_0_), channel_id=1, source_target_pairs={{0,32},{1,33},{2,34},{3,35},{4,36},{5,37},{6,38},{7,39},{8,40},{9,... | collective-permute-start | bytes 221192 | tf_op jit(solution)/shard_map/ppermute | solution.py:337
  57.4 5.1 %collective-permute-start.6 = (f32[16,1152]{1,0:T(8,128)S(1)}, f32[16,1152]{1,0:T(8,128)S(1)}, u32[]{:S(2)}, u32[]{:S(2)}) collective-permute-start(f32[16,1152]{1,0:T(8,128)S(1)} %gram_z.1._.refs_0_), channel_id=1, source_target_pairs={{0,64},{1,65},{2,66},{3,67},{4,68},{5,69},{6,70},{7,71},{8,72},{9,... | collective-permute-start | bytes 221192 | tf_op jit(solution)/shard_map/ppermute | solution.py:337
  58.9 5.4 %collective-permute-start.7 = (f32[16,1152]{1,0:T(8,128)S(1)}, f32[16,1152]{1,0:T(8,128)S(1)}, u32[]{:S(2)}, u32[]{:S(2)}) collective-permute-start(f32[16,1152]{1,0:T(8,128)S(1)} %gram_z.1._.refs_0_), channel_id=1, source_target_pairs={{0,96},{1,97},{2,98},{3,99},{4,100},{5,101},{6,102},{7,103},{8,104... | collective-permute-start | bytes 221192 | tf_op jit(solution)/shard_map/ppermute | solution.py:337
  64.3 7.1 %collective-permute-start.10 = (f32[16,1024]{1,0:T(8,128)S(1)}, f32[16,1024]{1,0:T(8,128)S(1)}, u32[]{:S(2)}, u32[]{:S(2)}) collective-permute-start(f32[16,1024]{1,0:T(8,128)S(1)} %get-tuple-element.35), channel_id=1, source_target_pairs={{0,64},{1,65},{2,66},{3,67},{4,68},{5,69},{6,70},{7,71},{8,72},{9,... | collective-permute-start | bytes 196616 | tf_op jit(solution)/shard_map/ppermute | solution.py:337
  66.2 5.6 %collective-permute-start.11 = (f32[16,1024]{1,0:T(8,128)S(1)}, f32[16,1024]{1,0:T(8,128)S(1)}, u32[]{:S(2)}, u32[]{:S(2)}) collective-permute-start(f32[16,1024]{1,0:T(8,128)S(1)} %get-tuple-element.34), channel_id=1, source_target_pairs={{0,96},{1,97},{2,98},{3,99},{4,100},{5,101},{6,102},{7,103},{8,104... | collective-permute-start | bytes 196616 | tf_op jit(solution)/shard_map/ppermute | solution.py:337
  66.9 4.8 %collective-permute-start.9 = (f32[16,1024]{1,0:T(8,128)S(1)}, f32[16,1024]{1,0:T(8,128)S(1)}, u32[]{:S(2)}, u32[]{:S(2)}) collective-permute-start(f32[16,1024]{1,0:T(8,128)S(1)} %get-tuple-element.36), channel_id=1, source_target_pairs={{0,32},{1,33},{2,34},{3,35},{4,36},{5,37},{6,38},{7,39},{8,40},{9,... | collective-permute-start | bytes 196616 | tf_op jit(solution)/shard_map/ppermute | solution.py:337
  67.4 17.7 %collective-permute-start.17 = (f32[64,1152]{1,0:T(8,128)S(1)}, f32[64,1152]{1,0:T(8,128)S(1)}, u32[]{:S(2)}, u32[]{:S(2)}) collective-permute-start(f32[64,1152]{1,0:T(8,128)S(1)} %gram_x.1._.refs_0_), channel_id=1, source_target_pairs={{0,1},{1,0},{2,3},{3,2},{4,5},{5,4},{6,7},{7,6},{8,9},{9,8},{10,11... | collective-permute-start | bytes 884744 | tf_op jit(solution)/shard_map/ppermute | solution.py:337
  68.8 16.3 %collective-permute-start.18 = (f32[64,1152]{1,0:T(8,128)S(1)}, f32[64,1152]{1,0:T(8,128)S(1)}, u32[]{:S(2)}, u32[]{:S(2)}) collective-permute-start(f32[64,1152]{1,0:T(8,128)S(1)} %gram_x.1._.refs_0_), channel_id=1, source_target_pairs={{0,2},{1,3},{2,0},{3,1},{4,6},{5,7},{6,4},{7,5},{8,10},{9,11},{10,... | collective-permute-start | bytes 884744 | tf_op jit(solution)/shard_map/ppermute | solution.py:337
  71.4 14.4 %collective-permute-start.19 = (f32[64,1152]{1,0:T(8,128)S(1)}, f32[64,1152]{1,0:T(8,128)S(1)}, u32[]{:S(2)}, u32[]{:S(2)}) collective-permute-start(f32[64,1152]{1,0:T(8,128)S(1)} %gram_x.1._.refs_0_), channel_id=1, source_target_pairs={{0,3},{1,2},{2,1},{3,0},{4,7},{5,6},{6,5},{7,4},{8,11},{9,10},{10,... | collective-permute-start | bytes 884744 | tf_op jit(solution)/shard_map/ppermute | solution.py:337
  71.8 4.7 %collective-permute-start.12 = (f32[16,1024]{1,0:T(8,128)S(1)}, f32[16,1024]{1,0:T(8,128)S(1)}, u32[]{:S(2)}, u32[]{:S(2)}) collective-permute-start(f32[16,1024]{1,0:T(8,128)S(1)} %sum_x.1.a_ref), channel_id=1, source_target_pairs={{0,16},{1,17},{2,18},{3,19},{4,20},{5,21},{6,22},{7,23},{8,24},{9,... | collective-permute-start | bytes 196616 | tf_op jit(solution)/shard_map/ppermute | solution.py:337
  76.5 4.0 %collective-permute-start.13 = (f32[16,1024]{1,0:T(8,128)S(1)}, f32[16,1024]{1,0:T(8,128)S(1)}, u32[]{:S(2)}, u32[]{:S(2)}) collective-permute-start(f32[16,1024]{1,0:T(8,128)S(1)} %sum_z.1.refs_0_), channel_id=1, source_target_pairs={{0,32},{1,33},{2,34},{3,35},{4,36},{5,37},{6,38},{7,39},{8,40},{9,... | collective-permute-start | bytes 196616 | tf_op jit(solution)/shard_map/ppermute | solution.py:337
  77.4 5.7 %collective-permute-start.14 = (f32[16,1024]{1,0:T(8,128)S(1)}, f32[16,1024]{1,0:T(8,128)S(1)}, u32[]{:S(2)}, u32[]{:S(2)}) collective-permute-start(f32[16,1024]{1,0:T(8,128)S(1)} %sum_z.1.refs_0_), channel_id=1, source_target_pairs={{0,64},{1,65},{2,66},{3,67},{4,68},{5,69},{6,70},{7,71},{8,72},{9,... | collective-permute-start | bytes 196616 | tf_op jit(solution)/shard_map/ppermute | solution.py:337
  80.5 4.6 %collective-permute-start.15 = (f32[16,1024]{1,0:T(8,128)S(1)}, f32[16,1024]{1,0:T(8,128)S(1)}, u32[]{:S(2)}, u32[]{:S(2)}) collective-permute-start(f32[16,1024]{1,0:T(8,128)S(1)} %sum_z.1.refs_0_), channel_id=1, source_target_pairs={{0,96},{1,97},{2,98},{3,99},{4,100},{5,101},{6,102},{7,103},{8,104... | collective-permute-start | bytes 196616 | tf_op jit(solution)/shard_map/ppermute | solution.py:337
  85.9 7.0 %collective-permute-start.20 = (f32[256,1152]{1,0:T(8,128)S(1)}, f32[256,1152]{1,0:T(8,128)S(1)}, u32[]{:S(2)}, u32[]{:S(2)}) collective-permute-start(f32[256,1152]{1,0:T(8,128)S(1)} %gram_y.1.refs_0_), channel_id=1, source_target_pairs={{0,8},{1,9},{2,10},{3,11},{4,12},{5,13},{6,14},{7,15},{8,0},{9,1},... | collective-permute-start | bytes 3538952 | tf_op jit(solution)/shard_map/ppermute | solution.py:337
  90.5 10.2 %collective-permute-start.16 = (f32[64,1024]{1,0:T(8,128)S(1)}, f32[64,1024]{1,0:T(8,128)S(1)}, u32[]{:S(2)}, u32[]{:S(2)}) collective-permute-start(f32[64,1024]{1,0:T(8,128)S(1)} %sum_join.1._.refs_0_), channel_id=1, source_target_pairs={{0,8},{1,9},{2,10},{3,11},{4,12},{5,13},{6,14},{7,15},{8,0},{9,1},... | collective-permute-start | bytes 786440 | tf_op jit(solution)/shard_map/ppermute | solution.py:337

commit v4 on v3

--- a/solution.py
+++ b/solution.py
@@ -198,19 +198,23 @@
 
 
 def last_product_kernel(
-    _, place_ref, total_ref, vec_ref, from_high_ref, from_low_ref, high_ref, low_ref, keep_ref, send_ref, sum_ref, sem
+    _, place_ref, total_ref, vec_ref, from_high_ref, from_low_ref, high_ref, low_ref, out_ref, sum_ref, sem
 ):
     first = vec_ref.shape[1] - high_ref.shape[0]
     product(vec_ref, (from_high_ref, from_low_ref), (high_ref, low_ref), first, sem, sum_ref, total_ref)
     core, x_at = place_ref[1], place_ref[2]
-    for k in range(4):
-        at = jnp.bitwise_xor(x_at, k) * 16
-        keep_ref[k * 16 : k * 16 + 16, :] = sum_ref[span(core * 64 + at, 16), :]
-        send_ref[k * 16 : k * 16 + 16, :] = sum_ref[span((1 - core) * 64 + at, 16), :]
-
-
-def add_kernel(_, a_ref, b_ref, out_ref):
-    out_ref[...] = a_ref[...] + b_ref[...]
+    for k in range(8):
+        at = jnp.bitwise_xor(core, k // 4) * 64 + jnp.bitwise_xor(x_at, k % 4) * 16
+        out_ref[k * 16 : k * 16 + 16, :] = sum_ref[span(at, 16), :]
+
+
+def split_kernel(_, sum_ref, send_ref):
+    send_ref[...] = sum_ref[send_ref.shape[0] :, :]
+
+
+def add_kernel(*refs):
+    *_, a_ref, b_ref, out_ref = refs
+    out_ref[...] = a_ref[: b_ref.shape[0], :] + b_ref[...]
 
 
 def join_kernel(_, *refs):
@@ -221,7 +225,7 @@
         at += part.shape[0]
 
 
-def sum_kernel(*refs):
+def sum_kernel(_, *refs):
     *parts, out_ref = refs
     a, b, c, d = (part[...] for part in parts)
     out_ref[...] = (a + b) + (c + d)
@@ -240,9 +244,9 @@
         out_ref[:, part] = dot(order, v1) + (dot(order, v2) + dot(order, v3))
 
 
-def inverse_kernel(place_ref, *refs):
-    *gram_refs, high_ref, low_ref, stage_ref, lower_ref, out_ref = refs
-    total = out_ref.shape[0]
+def blocks_kernel(place_ref, *refs):
+    *gram_refs, lower_ref, blocks_ref, stage_ref = refs
+    total = lower_ref.shape[0]
     blocks = total // BLOCK
     core, x_at, col = place_ref[1], place_ref[2], place_ref[3]
     r = lax.broadcasted_iota(jnp.int32, (BLOCK, BLOCK), 0)
@@ -259,7 +263,6 @@
             top, low = (15 - q) * HALF + k * 8, q * HALF + k * 8
             lower_ref[top : top + 8, :rest] = piece[:, :rest]
             lower_ref[low : low + 8, :width] = piece[:, rest:]
-    out_ref[...] = jnp.zeros_like(out_ref)
     lows, inverses = [], []
     for q in range(blocks):
         part = pl.ds(q * BLOCK, BLOCK)
@@ -279,36 +282,53 @@
     pair = (r >= HALF) & (c < HALF)
     mids = [dot3(jnp.where(pair, lows[q], 0.0), inverses[q]) for q in range(blocks)]
     inverses = [inverses[q] - dot3(inverses[q], mids[q]) for q in range(blocks)]
-    size = BLOCK
     for q in range(blocks):
-        part = pl.ds(q * BLOCK, BLOCK)
-        out_ref[part, part] = inverses[q]
-    while size < total:
-        for start in range(0, total, 2 * size):
-            a, b = pl.ds(start, size), pl.ds(start + size, size)
-            mid = dot3(lower_ref[b, a], out_ref[a, a])
-            out_ref[b, a] = -dot3(out_ref[b, b], mid)
-        size *= 2
-    high, low = halves(out_ref[...])
-    high_ref[...] = high
-    low_ref[...] = low
+        blocks_ref[q] = inverses[q]
+
+
+def inverse_kernel(lower_ref, blocks_ref, th_ref, tl_ref, lh_ref, ll_ref, out_ref):
+    total = lower_ref.shape[0]
+    half = total // 2
+    for start in range(0, total, 2 * BLOCK):
+        at = start % half
+        a, b = slice(start, start + BLOCK), slice(start + BLOCK, start + 2 * BLOCK)
+        ac, bc = slice(at, at + BLOCK), slice(at + BLOCK, at + 2 * BLOCK)
+        first, last = blocks_ref[start // BLOCK], blocks_ref[start // BLOCK + 1]
+        out_ref[a, ac] = first
+        out_ref[b, bc] = last
+        out_ref[a, bc] = jnp.zeros((BLOCK, BLOCK), F32)
+        out_ref[b, ac] = -dot3(last, dot3(lower_ref[b, a], first))
+    quarter = half // 2
+    for start in (0, half):
+        a, b = slice(start, start + quarter), slice(start + quarter, start + half)
+        out_ref[a, quarter:] = jnp.zeros((quarter, quarter), F32)
+        out_ref[b, :quarter] = -dot3(out_ref[b, quarter:], dot3(lower_ref[b, a], out_ref[a, :quarter]))
+    th_ref[...], tl_ref[...] = halves(out_ref[...])
+    lh_ref[...], ll_ref[...] = halves(lower_ref[half:, :half])
 
 
 def change_kernel(place_ref, order_ref, *refs):
-    mine_ref, other_ref, th_ref, tl_ref, vec_ref, *held_refs, out_ref, sum_ref, w_ref, put_ref, put_sem = refs
+    mine_ref, other_ref, th_ref, tl_ref, lh_ref, ll_ref, vec_ref, *held_refs, out_ref, sum_ref, w_ref, put_ref, put_sem = refs
     count, rows = vec_ref.shape
     core, x_at = place_ref[1], place_ref[2]
     for k in range(4):
         at = jnp.bitwise_xor(x_at, k) * 16
         sum_ref[span(core * 64 + at, 16), :] = mine_ref[k * 16 : k * 16 + 16, :]
         sum_ref[span((1 - core) * 64 + at, 16), :] = other_ref[k * 16 : k * 16 + 16, :]
-    yh, yl = halves(sum_ref[...])
-    both = dot(jnp.concatenate([yh, yl], axis=0), th_ref[...])
-    weighted = both[:count] + (both[count:] + dot(yh, tl_ref[...]))
+    def times(x, high, low):
+        xh, xl = halves(x)
+        both = dot(jnp.concatenate([xh, xl], axis=0), high)
+        return both[:count] + (both[count:] + dot(xh, low))
+
+    half = sum_ref.shape[1] // 2
     order = order_ref[...]
-    wh, wl = halves(weighted)
-    w_ref[:count, :] = dot(order, wh).astype(BF16)
-    w_ref[count:, :] = dot(order, wl).astype(BF16)
+    last = times(sum_ref[:, half:], th_ref[half:, :], tl_ref[half:, :])
+    first = sum_ref[:, :half] - times(last, lh_ref[...], ll_ref[...])
+    first = times(first, th_ref[:half, :], tl_ref[:half, :])
+    for at, part in ((0, first), (half, last)):
+        wh, wl = halves(part)
+        w_ref[:count, at : at + half] = dot(order, wh).astype(BF16)
+        w_ref[count:, at : at + half] = dot(order, wl).astype(BF16)
 
     copies = []
     for step, at in enumerate(range(0, rows, WIDE)):
@@ -338,7 +358,7 @@
 
 
 def gather(x, steps):
-    near, far, across = (swap(x, bits) for bits in steps)
+    across, far, near = (swap(x, bits) for bits in reversed(steps))
     return [x, near, across, far]
 
 
@@ -406,7 +426,7 @@
     after = pl.BlockSpec(memory_space=pl.ANY)
     high = pltpu.with_memory_space_constraint(high, pltpu.HBM)
     low = pltpu.with_memory_space_constraint(low, pltpu.HBM)
-    split = steps // 2 * WIDE
+    split = (steps + 1) // 2 * WIDE
     first_held, last_held = ([pltpu.VMEM((n, total), BF16)] * 2 for n in (split, rows_dev - split))
     summed = jax.ShapeDtypeStruct((count, total), F32)
     semaphores = pltpu.SemaphoreType.DMA((steps, 2))
@@ -422,19 +442,19 @@
     )(part, received, high, low)
     piece = small(add_kernel, (16, packed), "gram_z", [sums], [part, near])
     pieces = gather(piece, X_STEPS)
-    last_high, last_low, keep, send = pl.pallas_call(
+    last_high, last_low, sums = pl.pallas_call(
         last_product_kernel,
         in_specs=[after, smem, vmem, vmem, hbm, hbm],
-        out_specs=[vmem] * 4,
-        out_shape=last_held + [jax.ShapeDtypeStruct((count // 2, total), F32)] * 2,
+        out_specs=[vmem] * 3,
+        out_shape=last_held + [summed],
         scratch_shapes=[pltpu.VMEM((count, total), F32), semaphores],
         compiler_params=params(8),
         cost_estimate=cost(3 * rows_dev * count * total, 2 * rows_dev * total),
         name="product_last",
     )(piece, place, sums, received, high, low)
-    grams = small(join_kernel, (64, packed), "gram_x", [keep], pieces)
+    grams = small(join_kernel, (64, packed), "gram_x", [sums], pieces)
     pieces = gather(grams, Y_STEPS)
-
+    send = small(split_kernel, (count // 2, total), "sum_split", [grams], [sums])
     ordered = pl.pallas_call(
         reorder_kernel,
         in_specs=[vmem, vmem],
@@ -444,32 +464,41 @@
         cost_estimate=cost(6 * rows_dev * count * count, 16 * rows_dev * count),
         name="reorder",
     )(order, received)
-    both = small(add_kernel, (count // 2, total), "sum_core", [grams], [keep, swap(send, CORE)])
+    both = small(add_kernel, (count // 2, total), "sum_core", [grams], [sums, swap(send, CORE)])
     parts = [both[: count // 8]]
     for k, bits in ((1, 32), (2, 64), (3, 96)):
         parts.append(swap(both[k * count // 8 : (k + 1) * count // 8], bits))
-    sums = small(sum_kernel, (count // 8, total), "sum_x", [], parts)
+    sums = small(sum_kernel, (count // 8, total), "sum_x", [pieces[1]], parts)
     sums = small(add_kernel, (count // 8, total), "sum_z", [ordered], [sums, swap(sums, Z_HIGH)])
-    mine = small(join_kernel, (count // 2, total), "sum_join", [ordered], gather(sums, X_STEPS))
-    other = swap(mine, CORE)
-    pieces = small(join_kernel, (256, packed), "gram_y", [mine], pieces)
-    t_high, t_low = pl.pallas_call(
-        inverse_kernel,
+    before_y = sums
+    sums = gather(sums, X_STEPS)
+    grams = small(join_kernel, (256, packed), "gram_y", [before_y], pieces)
+    lower, blocks = pl.pallas_call(
+        blocks_kernel,
         in_specs=[smem] + [vmem] * 2,
         out_specs=[vmem] * 2,
-        out_shape=[jax.ShapeDtypeStruct((total, total), BF16)] * 2,
-        scratch_shapes=[
-            pltpu.VMEM((8, 64, packed), F32),
-            pltpu.VMEM((total, total), F32),
-            pltpu.VMEM((total, total), F32),
-        ],
-        compiler_params=params(18),
-        cost_estimate=cost(6 * total**3, 8 * total**2),
+        out_shape=[jax.ShapeDtypeStruct((total, total), F32), jax.ShapeDtypeStruct((total // BLOCK, BLOCK, BLOCK), F32)],
+        scratch_shapes=[pltpu.VMEM((8, 64, packed), F32)],
+        compiler_params=params(12),
+        cost_estimate=cost(4 * total**3, 4 * total**2),
+        name="inverse_blocks",
+    )(place, grams, swap(grams, CORE))
+    mine = small(join_kernel, (count // 2, total), "sum_join", [blocks], sums)
+    other = swap(mine, CORE)
+    inverses = pl.pallas_call(
+        inverse_kernel,
+        in_specs=[vmem] * 2,
+        out_specs=[vmem] * 4,
+        out_shape=[jax.ShapeDtypeStruct((total, total // 2), BF16)] * 2 + [jax.ShapeDtypeStruct((total // 2, total // 2), BF16)] * 2,
+        scratch_shapes=[pltpu.VMEM((total, total // 2), F32)],
+        compiler_params=params(12),
+        cost_estimate=cost(4 * total**3, 4 * total**2),
         name="inverse",
-    )(place, pieces, swap(pieces, CORE))
+    )(lower, blocks)
+
     return pl.pallas_call(
         change_kernel,
-        in_specs=[smem] + [vmem] * 10,
+        in_specs=[smem] + [vmem] * 12,
         out_specs=hbm,
         out_shape=jax.ShapeDtypeStruct((count, rows_dev), F32),
         scratch_shapes=[
@@ -481,7 +510,7 @@
         compiler_params=params(12),
         cost_estimate=cost(6 * rows_dev * count * total, 4 * rows_dev * count),
         name="change",
-    )(place, order, mine, other, t_high, t_low, ordered, first_high, first_low, last_high, last_low)
+    )(place, order, mine, other, *inverses, ordered, first_high, first_low, last_high, last_low)
 
 
 def solution(mesh):

time: 109 us -> 103 us (0.945)
  starting transfers between devices: 39.4 us -> 36.6 us
  waiting for transfers between devices: 20.8 us -> 18.9 us
  Pallas kernels: 48.1 us -> 46.3 us
    ppermute x21, starting transfers between devices: 30.1 us -> 27.3 us  [swap(): return lax.ppermute(x, ('row', 'col'), [(i, i ^ bits) for i in range(128)])]
    ppermute x21, waiting for transfers between devices: 20.8 us -> 18.9 us  [swap(): return lax.ppermute(x, ('row', 'col'), [(i, i ^ bits) for i in range(128)])]
    pallas_call x2 -> x3, Pallas kernels: 15.9 us -> 14.2 us  [the longest x1 8.21 us: per_device(): pl.pallas_call(change_kernel, in_specs=[smem] + [vmem] * 12, out_specs=hb...]
  transfers between devices with their start and end apart: 22 -> 22, of which waited for: 12 -> 7; matrix products, arithmetic and copies ran while one was open for 0% -> 0% of each run, Pallas kernels for 32% -> 37%
where the time goes in v4:
time: 103 us
  Pallas kernels  46.3 us (45%)
  starting transfers between devices  36.6 us (36%)
  waiting for transfers between devices  18.9 us (18%)
    ppermute x21, starting transfers between devices, swap(): return lax.ppermute(x, ('row', 'col'), [(i, i ^ bits) for i in range(128)])  27.3 us
    pallas_call x1, Pallas kernels, per_device(): pl.pallas_call(gram_kernel, in_specs=[smem, vmem, hbm], out_specs=[hbm, h...  19.9 us
    ppermute x21, waiting for transfers between devices, swap(): return lax.ppermute(x, ('row', 'col'), [(i, i ^ bits) for i in range(128)])  18.9 us
    all_to_all x1, starting transfers between devices, per_device(): lax.all_to_all(shaped, 'row', 0, 0, tiled=True).reshape(count, rows_dev)  9.26 us
    pallas_call x1, Pallas kernels, per_device(): pl.pallas_call(change_kernel, in_specs=[smem] + [vmem] * 12, out_specs=hb...  8.21 us
    pallas_call x1, Pallas kernels, per_device(): pl.pallas_call(first_product_kernel, in_specs=[after, vmem, hbm, hbm], ou...  4.74 us
    pallas_call x1, Pallas kernels, per_device(): pl.pallas_call(last_product_kernel, in_specs=[after, smem, vmem, vmem, hb...  4.72 us
    pallas_call x1, Pallas kernels, per_device(): pl.pallas_call(blocks_kernel, in_specs=[smem] + [vmem] * 2, out_specs=[vm...  4.35 us
  transfers between devices with their start and end apart: 22, of which 7 were waited for; matrix products, arithmetic and copies ran while one was open for 0% of the time, Pallas kernels for 37%

profile of v4, /device:TPU:1, one launch (start us, length us, event | category | flops | bytes accessed | tf_op | source)
XLA Modules:
  0.0 102.7 jit_solution(9669606225232975013)
XLA Ops:
  0.0 9.3 %all-to-all-start = ((f32[16,8,4608]{2,1,0:T(8,128)}), f32[16,8,4608]{2,1,0:T(8,128)S(1)}, u32[]{:S(2)}, u32[]{:S(2)}) async-start(f32[16,8,4608]{2,1,0:T(8,128)} %bitcast.11), calls=%async_computation | async-start | bytes 4718592 | tf_op jit(solution)/shard_map/all_to_all | solution.py:397
  9.5 19.9 %gram.1 = (bf16[4608,1024]{1,0:T(8,128)(2,1)}, bf16[4608,1024]{1,0:T(8,128)(2,1)}, f32[64,1152]{1,0:T(8,128)S(1)}, f32[64,1152]{1,0:T(8,128)S(1)}) custom-call(s32[4]{0:T(128)S(1)} %pad_add_fusion.place_ref, s32[1,1024]{1,0:T(1,128)S(1)} %add.56.lead_ref, f32[4608,1024]{1,0:T(8,128)} %tiles_ref.1), custom_call_target="tpu_custom_call" | custom-call | flops 7247757312 | bytes 37748736 | tf_op jit(solution)/shard_map/gram/pallas_call | solution.py:402
  29.4 0.2 collective-permute-start
  29.6 1.5 %collective-permute-done = f32[64,1152]{1,0:T(8,128)S(1)} collective-permute-done((f32[64,1152]{1,0:T(8,128)S(1)}, f32[64,1152]{1,0:T(8,128)S(1)}, u32[]{:S(2)}, u32[]{:S(2)}) %collective-permute-start) | collective-permute-done | bytes 294944 | tf_op jit(solution)/shard_map/ppermute | solution.py:357
  31.1 1.5 %collective-permute-start.1 = (f32[16,1152]{1,0:T(8,128)S(1)}, f32[16,1152]{1,0:T(8,128)S(1)}, u32[]{:S(2)}, u32[]{:S(2)}) collective-permute-start(f32[16,1152]{1,0:T(8,128)S(1)} %get-tuple-element.37), channel_id=1, source_target_pairs={{0,32},{1,33},{2,34},{3,35},{4,36},{5,37},{6,38},{7,39},{8,40},{9,... | collective-permute-start | bytes 221192 | tf_op jit(solution)/shard_map/ppermute | solution.py:357
  32.6 1.8 %collective-permute-start.2 = (f32[16,1152]{1,0:T(8,128)S(1)}, f32[16,1152]{1,0:T(8,128)S(1)}, u32[]{:S(2)}, u32[]{:S(2)}) collective-permute-start(f32[16,1152]{1,0:T(8,128)S(1)} %get-tuple-element.39), channel_id=1, source_target_pairs={{0,96},{1,97},{2,98},{3,99},{4,100},{5,101},{6,102},{7,103},{8,104... | collective-permute-start | bytes 221192 | tf_op jit(solution)/shard_map/ppermute | solution.py:357
  34.4 0.6 collective-permute-start.3
  35.0 3.6 %collective-permute-done.1 = f32[16,1152]{1,0:T(8,128)S(1)} collective-permute-done((f32[16,1152]{1,0:T(8,128)S(1)}, f32[16,1152]{1,0:T(8,128)S(1)}, u32[]{:S(2)}, u32[]{:S(2)}) %collective-permute-start.1) | collective-permute-done | bytes 73760 | tf_op jit(solution)/shard_map/ppermute | solution.py:357
  38.6 5.5 %collective-permute-done.2 = f32[16,1152]{1,0:T(8,128)S(1)} collective-permute-done((f32[16,1152]{1,0:T(8,128)S(1)}, f32[16,1152]{1,0:T(8,128)S(1)}, u32[]{:S(2)}, u32[]{:S(2)}) %collective-permute-start.2) | collective-permute-done | bytes 73760 | tf_op jit(solution)/shard_map/ppermute | solution.py:357
  44.1 1.1 %collective-permute-done.3 = f32[16,1152]{1,0:T(8,128)S(1)} collective-permute-done((f32[16,1152]{1,0:T(8,128)S(1)}, f32[16,1152]{1,0:T(8,128)S(1)}, u32[]{:S(2)}, u32[]{:S(2)}) %collective-permute-start.3) | collective-permute-done | bytes 73760 | tf_op jit(solution)/shard_map/ppermute | solution.py:357
  45.3 4.7 %product_first.1 = (bf16[2560,1024]{1,0:T(8,128)(2,1)S(1)}, bf16[2560,1024]{1,0:T(8,128)(2,1)S(1)}, f32[128,1024]{1,0:T(8,128)S(1)}) custom-call(f32[16,1152]{1,0:T(8,128)S(1)} %fusion.1._.refs_1_, f32[128,4608]{1,0:T(8,128)S(1)} %bitcast.8, bf16[4608,1024]{1,0:T(8,128)(2,1)} %get-tuple-element.23.from_high_ref, ...), custom_call_target="tpu_custom_call" | custom-call | flops 1811939328 | bytes 9437184 | tf_op jit(solution)/shard_map/product_first/pallas_call | solution.py:433
  50.1 0.1 collective-permute-start.5
  50.2 2.8 %collective-permute-start.6 = (f32[16,1152]{1,0:T(8,128)S(1)}, f32[16,1152]{1,0:T(8,128)S(1)}, u32[]{:S(2)}, u32[]{:S(2)}) collective-permute-start(f32[16,1152]{1,0:T(8,128)S(1)} %gram_z.1._.refs_0_), channel_id=1, source_target_pairs={{0,64},{1,65},{2,66},{3,67},{4,68},{5,69},{6,70},{7,71},{8,72},{9,... | collective-permute-start | bytes 221192 | tf_op jit(solution)/shard_map/ppermute | solution.py:357
  53.0 1.0 %collective-permute-start.7 = (f32[16,1152]{1,0:T(8,128)S(1)}, f32[16,1152]{1,0:T(8,128)S(1)}, u32[]{:S(2)}, u32[]{:S(2)}) collective-permute-start(f32[16,1152]{1,0:T(8,128)S(1)} %gram_z.1._.refs_0_), channel_id=1, source_target_pairs={{0,96},{1,97},{2,98},{3,99},{4,100},{5,101},{6,102},{7,103},{8,104... | collective-permute-start | bytes 221192 | tf_op jit(solution)/shard_map/ppermute | solution.py:357
  54.0 4.7 %product_last.1 = (bf16[2048,1024]{1,0:T(8,128)(2,1)S(1)}, bf16[2048,1024]{1,0:T(8,128)(2,1)S(1)}, f32[128,1024]{1,0:T(8,128)S(1)}) custom-call(f32[16,1152]{1,0:T(8,128)S(1)} %gram_z.1._.refs_0_, s32[4]{0:T(128)S(1)} %pad_add_fusion.place_ref, f32[128,1024]{1,0:T(8,128)S(1)} %get-tuple-element.25.refs_0_.total_ref, f32[128,4608]{1,0:T(8,128)S(1)} %bitcast.9, ...), custom_call_target="tpu_custom_call" | custom-call | flops 1811939328 | bytes 9437184 | tf_op jit(solution)/shard_map/product_last/pallas_call | solution.py:445
  58.8 2.9 %collective-permute-start.9 = (f32[64,1024]{1,0:T(8,128)S(1)}, f32[64,1024]{1,0:T(8,128)S(1)}, u32[]{:S(2)}, u32[]{:S(2)}) collective-permute-start(f32[64,1024]{1,0:T(8,128)S(1)} %sum_split.1), channel_id=1, source_target_pairs={{0,8},{1,9},{2,10},{3,11},{4,12},{5,13},{6,14},{7,15},{8,0},{9,1},... | collective-permute-start | bytes 786440 | tf_op jit(solution)/shard_map/ppermute | solution.py:357
  61.7 1.3 %collective-permute-start.8 = (f32[64,1152]{1,0:T(8,128)S(1)}, f32[64,1152]{1,0:T(8,128)S(1)}, u32[]{:S(2)}, u32[]{:S(2)}) collective-permute-start(f32[64,1152]{1,0:T(8,128)S(1)} %gram_x.1._.refs_0_), channel_id=1, source_target_pairs={{0,1},{1,0},{2,3},{3,2},{4,5},{5,4},{6,7},{7,6},{8,9},{9,8},{10,11... | collective-permute-start | bytes 884744 | tf_op jit(solution)/shard_map/ppermute | solution.py:357
  63.0 2.6 %collective-permute-start.14 = (f32[64,1152]{1,0:T(8,128)S(1)}, f32[64,1152]{1,0:T(8,128)S(1)}, u32[]{:S(2)}, u32[]{:S(2)}) collective-permute-start(f32[64,1152]{1,0:T(8,128)S(1)} %gram_x.1._.refs_0_), channel_id=1, source_target_pairs={{0,2},{1,3},{2,0},{3,1},{4,6},{5,7},{6,4},{7,5},{8,10},{9,11},{10,... | collective-permute-start | bytes 884744 | tf_op jit(solution)/shard_map/ppermute | solution.py:357
  65.8 2.0 %collective-permute-start.11 = (f32[16,1024]{1,0:T(8,128)S(1)}, f32[16,1024]{1,0:T(8,128)S(1)}, u32[]{:S(2)}, u32[]{:S(2)}) collective-permute-start(f32[16,1024]{1,0:T(8,128)S(1)} %get-tuple-element.41), channel_id=1, source_target_pairs={{0,64},{1,65},{2,66},{3,67},{4,68},{5,69},{6,70},{7,71},{8,72},{9,... | collective-permute-start | bytes 196616 | tf_op jit(solution)/shard_map/ppermute | solution.py:357
  67.8 2.4 %collective-permute-done.8._.refs_1_ = f32[64,1152]{1,0:T(8,128)S(1)} collective-permute-done((f32[64,1152]{1,0:T(8,128)S(1)}, f32[64,1152]{1,0:T(8,128)S(1)}, u32[]{:S(2)}, u32[]{:S(2)}) %collective-permute-start.8) | collective-permute-done | bytes 294944 | tf_op jit(solution)/shard_map/ppermute | solution.py:357
  70.3 0.9 collective-permute-start.12
  71.2 3.7 %collective-permute-done.12.refs_3_ = f32[16,1024]{1,0:T(8,128)S(1)} collective-permute-done((f32[16,1024]{1,0:T(8,128)S(1)}, f32[16,1024]{1,0:T(8,128)S(1)}, u32[]{:S(2)}, u32[]{:S(2)}) %collective-permute-start.12) | collective-permute-done | bytes 65568 | tf_op jit(solution)/shard_map/ppermute | solution.py:357
  74.9 2.4 %collective-permute-start.13 = (f32[16,1024]{1,0:T(8,128)S(1)}, f32[16,1024]{1,0:T(8,128)S(1)}, u32[]{:S(2)}, u32[]{:S(2)}) collective-permute-start(f32[16,1024]{1,0:T(8,128)S(1)} %sum_x.1.refs_1_), channel_id=1, source_target_pairs={{0,16},{1,17},{2,18},{3,19},{4,20},{5,21},{6,22},{7,23},{8,24},{9,... | collective-permute-start | bytes 196616 | tf_op jit(solution)/shard_map/ppermute | solution.py:357
  77.4 2.6 %reorder.1.refs_0_.refs_6_ = f32[128,4608]{1,0:T(8,128)S(1)} custom-call(bf16[128,128]{1,0:T(8,128)(2,1)S(1)} %fusion.2.order_ref, f32[128,4608]{1,0:T(8,128)S(1)} %bitcast.10), custom_call_target="tpu_custom_call" | custom-call | flops 452984832 | bytes 9437184 | tf_op jit(solution)/shard_map/reorder/pallas_call | solution.py:458
  80.1 1.0 collective-permute-done.15.refs_3_
  81.2 2.2 %collective-permute-start.16 = (f32[256,1152]{1,0:T(8,128)S(1)}, f32[256,1152]{1,0:T(8,128)S(1)}, u32[]{:S(2)}, u32[]{:S(2)}) collective-permute-start(f32[256,1152]{1,0:T(8,128)S(1)} %gram_y.1.refs_0_), channel_id=1, source_target_pairs={{0,8},{1,9},{2,10},{3,11},{4,12},{5,13},{6,14},{7,15},{8,0},{9,1},... | collective-permute-start | bytes 3538952 | tf_op jit(solution)/shard_map/ppermute | solution.py:357
  83.3 2.0 %collective-permute-start.18 = (f32[16,1024]{1,0:T(8,128)S(1)}, f32[16,1024]{1,0:T(8,128)S(1)}, u32[]{:S(2)}, u32[]{:S(2)}) collective-permute-start(f32[16,1024]{1,0:T(8,128)S(1)} %sum_z.1._.refs_0_), channel_id=1, source_target_pairs={{0,64},{1,65},{2,66},{3,67},{4,68},{5,69},{6,70},{7,71},{8,72},{9,... | collective-permute-start | bytes 196616 | tf_op jit(solution)/shard_map/ppermute | solution.py:357
  85.4 1.8 %collective-permute-start.19 = (f32[16,1024]{1,0:T(8,128)S(1)}, f32[16,1024]{1,0:T(8,128)S(1)}, u32[]{:S(2)}, u32[]{:S(2)}) collective-permute-start(f32[16,1024]{1,0:T(8,128)S(1)} %sum_z.1._.refs_0_), channel_id=1, source_target_pairs={{0,96},{1,97},{2,98},{3,99},{4,100},{5,101},{6,102},{7,103},{8,104... | collective-permute-start | bytes 196616 | tf_op jit(solution)/shard_map/ppermute | solution.py:357
  87.2 4.4 %inverse_blocks.1 = (f32[1024,1024]{1,0:T(8,128)S(1)}, f32[8,128,128]{2,1,0:T(8,128)S(1)}) custom-call(s32[4]{0:T(128)S(1)} %pad_add_fusion.place_ref, f32[256,1152]{1,0:T(8,128)S(1)} %gram_y.1.refs_0_, f32[256,1152]{1,0:T(8,128)S(1)} %collective-permute-done.16.refs_1_), custom_call_target="tpu_custom_call" | custom-call | flops 4294967296 | bytes 4194304 | tf_op jit(solution)/shard_map/inverse_blocks/pallas_call | solution.py:476
  91.6 1.0 collective-permute-start.20
  92.6 1.6 %inverse.1 = (bf16[1024,512]{1,0:T(8,128)(2,1)S(1)}, bf16[1024,512]{1,0:T(8,128)(2,1)S(1)}, bf16[512,512]{1,0:T(8,128)(2,1)S(1)}, bf16[512,512]{1,0:T(8,128)(2,1)S(1)}) custom-call(f32[1024,1024]{1,0:T(8,128)S(1)} %get-tuple-element.28.lower_ref, f32[8,128,128]{2,1,0:T(8,128)S(1)} %get-tuple-element.27._.blocks_ref), custom_call_target="tpu_custom_call" | custom-call | flops 4294967296 | bytes 4194304 | tf_op jit(solution)/shard_map/inverse/pallas_call | solution.py:488
  94.3 8.2 %change.1 = f32[128,4608]{1,0:T(8,128)} custom-call(s32[4]{0:T(128)S(1)} %pad_add_fusion.place_ref, bf16[128,128]{1,0:T(8,128)(2,1)S(1)} %fusion.2.order_ref, f32[64,1024]{1,0:T(8,128)S(1)} %sum_join.1.refs_0_, f32[64,1024]{1,0:T(8,128)S(1)} %collective-permute-done.20.refs_1_, bf16[1024,512]{1,0:T(8,128)(2,1)S(1)} %get-tuple-element.29.refs_2_, ...), custom_call_target="tpu_custom_call" | custom-call | flops 3623878656 | bytes 2359296 | tf_op jit(solution)/shard_map/change/pallas_call | solution.py:499
  (40 shorter events, 0.9 us)
Async XLA Ops:
  0.0 9.3 %copy-start = (s32[16]{0:T(128)S(1)}, s32[16]{0:T(128)}, u32[]{:S(2)}) copy-start(s32[16]{0:T(128)} %param.7) | copy-start | bytes 196
  0.0 45.3 %all-to-all-start = ((f32[16,8,4608]{2,1,0:T(8,128)}), f32[16,8,4608]{2,1,0:T(8,128)S(1)}, u32[]{:S(2)}, u32[]{:S(2)}) async-start(f32[16,8,4608]{2,1,0:T(8,128)} %bitcast.11), calls=%async_computation | async-start | bytes 4718592 | tf_op jit(solution)/shard_map/all_to_all | solution.py:397
  29.4 1.7 %collective-permute-start = (f32[64,1152]{1,0:T(8,128)S(1)}, f32[64,1152]{1,0:T(8,128)S(1)}, u32[]{:S(2)}, u32[]{:S(2)}) collective-permute-start(f32[64,1152]{1,0:T(8,128)S(1)} %get-tuple-element.22), channel_id=1, source_target_pairs={{0,8},{1,9},{2,10},{3,11},{4,12},{5,13},{6,14},{7,15},{8,0},{9,1},... | collective-permute-start | bytes 884744 | tf_op jit(solution)/shard_map/ppermute | solution.py:357
  31.1 7.5 %collective-permute-start.1 = (f32[16,1152]{1,0:T(8,128)S(1)}, f32[16,1152]{1,0:T(8,128)S(1)}, u32[]{:S(2)}, u32[]{:S(2)}) collective-permute-start(f32[16,1152]{1,0:T(8,128)S(1)} %get-tuple-element.37), channel_id=1, source_target_pairs={{0,32},{1,33},{2,34},{3,35},{4,36},{5,37},{6,38},{7,39},{8,40},{9,... | collective-permute-start | bytes 221192 | tf_op jit(solution)/shard_map/ppermute | solution.py:357
  32.6 11.5 %collective-permute-start.2 = (f32[16,1152]{1,0:T(8,128)S(1)}, f32[16,1152]{1,0:T(8,128)S(1)}, u32[]{:S(2)}, u32[]{:S(2)}) collective-permute-start(f32[16,1152]{1,0:T(8,128)S(1)} %get-tuple-element.39), channel_id=1, source_target_pairs={{0,96},{1,97},{2,98},{3,99},{4,100},{5,101},{6,102},{7,103},{8,104... | collective-permute-start | bytes 221192 | tf_op jit(solution)/shard_map/ppermute | solution.py:357
  34.4 10.8 %collective-permute-start.3 = (f32[16,1152]{1,0:T(8,128)S(1)}, f32[16,1152]{1,0:T(8,128)S(1)}, u32[]{:S(2)}, u32[]{:S(2)}) collective-permute-start(f32[16,1152]{1,0:T(8,128)S(1)} %get-tuple-element.38), channel_id=1, source_target_pairs={{0,64},{1,65},{2,66},{3,67},{4,68},{5,69},{6,70},{7,71},{8,72},{9,... | collective-permute-start | bytes 221192 | tf_op jit(solution)/shard_map/ppermute | solution.py:357
  45.2 4.9 %collective-permute-start.4 = (f32[16,1152]{1,0:T(8,128)S(1)}, f32[16,1152]{1,0:T(8,128)S(1)}, u32[]{:S(2)}, u32[]{:S(2)}) collective-permute-start(f32[16,1152]{1,0:T(8,128)S(1)} %fusion.1._.refs_1_), channel_id=1, source_target_pairs={{0,16},{1,17},{2,18},{3,19},{4,20},{5,21},{6,22},{7,23},{8,24},{9,... | collective-permute-start | bytes 221192 | tf_op jit(solution)/shard_map/ppermute | solution.py:357
  50.1 21.0 %copy-start.1 = (s32[128]{0:T(128)S(1)}, s32[128]{0:T(128)}, u32[]{:S(2)}) copy-start(s32[128]{0:T(128)} %param.5) | copy-start | bytes 1540
  50.1 8.7 %collective-permute-start.5 = (f32[16,1152]{1,0:T(8,128)S(1)}, f32[16,1152]{1,0:T(8,128)S(1)}, u32[]{:S(2)}, u32[]{:S(2)}) collective-permute-start(f32[16,1152]{1,0:T(8,128)S(1)} %gram_z.1._.refs_0_), channel_id=1, source_target_pairs={{0,32},{1,33},{2,34},{3,35},{4,36},{5,37},{6,38},{7,39},{8,40},{9,... | collective-permute-start | bytes 221192 | tf_op jit(solution)/shard_map/ppermute | solution.py:357
  50.2 8.6 %collective-permute-start.6 = (f32[16,1152]{1,0:T(8,128)S(1)}, f32[16,1152]{1,0:T(8,128)S(1)}, u32[]{:S(2)}, u32[]{:S(2)}) collective-permute-start(f32[16,1152]{1,0:T(8,128)S(1)} %gram_z.1._.refs_0_), channel_id=1, source_target_pairs={{0,64},{1,65},{2,66},{3,67},{4,68},{5,69},{6,70},{7,71},{8,72},{9,... | collective-permute-start | bytes 221192 | tf_op jit(solution)/shard_map/ppermute | solution.py:357
  53.0 5.8 %collective-permute-start.7 = (f32[16,1152]{1,0:T(8,128)S(1)}, f32[16,1152]{1,0:T(8,128)S(1)}, u32[]{:S(2)}, u32[]{:S(2)}) collective-permute-start(f32[16,1152]{1,0:T(8,128)S(1)} %gram_z.1._.refs_0_), channel_id=1, source_target_pairs={{0,96},{1,97},{2,98},{3,99},{4,100},{5,101},{6,102},{7,103},{8,104... | collective-permute-start | bytes 221192 | tf_op jit(solution)/shard_map/ppermute | solution.py:357
  58.8 6.8 %collective-permute-start.9 = (f32[64,1024]{1,0:T(8,128)S(1)}, f32[64,1024]{1,0:T(8,128)S(1)}, u32[]{:S(2)}, u32[]{:S(2)}) collective-permute-start(f32[64,1024]{1,0:T(8,128)S(1)} %sum_split.1), channel_id=1, source_target_pairs={{0,8},{1,9},{2,10},{3,11},{4,12},{5,13},{6,14},{7,15},{8,0},{9,1},... | collective-permute-start | bytes 786440 | tf_op jit(solution)/shard_map/ppermute | solution.py:357
  61.7 8.6 %collective-permute-start.8 = (f32[64,1152]{1,0:T(8,128)S(1)}, f32[64,1152]{1,0:T(8,128)S(1)}, u32[]{:S(2)}, u32[]{:S(2)}) collective-permute-start(f32[64,1152]{1,0:T(8,128)S(1)} %gram_x.1._.refs_0_), channel_id=1, source_target_pairs={{0,1},{1,0},{2,3},{3,2},{4,5},{5,4},{6,7},{7,6},{8,9},{9,8},{10,11... | collective-permute-start | bytes 884744 | tf_op jit(solution)/shard_map/ppermute | solution.py:357
  63.0 17.0 %collective-permute-start.14 = (f32[64,1152]{1,0:T(8,128)S(1)}, f32[64,1152]{1,0:T(8,128)S(1)}, u32[]{:S(2)}, u32[]{:S(2)}) collective-permute-start(f32[64,1152]{1,0:T(8,128)S(1)} %gram_x.1._.refs_0_), channel_id=1, source_target_pairs={{0,2},{1,3},{2,0},{3,1},{4,6},{5,7},{6,4},{7,5},{8,10},{9,11},{10,... | collective-permute-start | bytes 884744 | tf_op jit(solution)/shard_map/ppermute | solution.py:357
  65.6 15.4 %collective-permute-start.15 = (f32[64,1152]{1,0:T(8,128)S(1)}, f32[64,1152]{1,0:T(8,128)S(1)}, u32[]{:S(2)}, u32[]{:S(2)}) collective-permute-start(f32[64,1152]{1,0:T(8,128)S(1)} %gram_x.1._.refs_0_), channel_id=1, source_target_pairs={{0,3},{1,2},{2,1},{3,0},{4,7},{5,6},{6,5},{7,4},{8,11},{9,10},{10,... | collective-permute-start | bytes 884744 | tf_op jit(solution)/shard_map/ppermute | solution.py:357
  65.7 5.4 %collective-permute-start.10 = (f32[16,1024]{1,0:T(8,128)S(1)}, f32[16,1024]{1,0:T(8,128)S(1)}, u32[]{:S(2)}, u32[]{:S(2)}) collective-permute-start(f32[16,1024]{1,0:T(8,128)S(1)} %get-tuple-element.42), channel_id=1, source_target_pairs={{0,32},{1,33},{2,34},{3,35},{4,36},{5,37},{6,38},{7,39},{8,40},{9,... | collective-permute-start | bytes 196616 | tf_op jit(solution)/shard_map/ppermute | solution.py:357
  65.8 5.3 %collective-permute-start.11 = (f32[16,1024]{1,0:T(8,128)S(1)}, f32[16,1024]{1,0:T(8,128)S(1)}, u32[]{:S(2)}, u32[]{:S(2)}) collective-permute-start(f32[16,1024]{1,0:T(8,128)S(1)} %get-tuple-element.41), channel_id=1, source_target_pairs={{0,64},{1,65},{2,66},{3,67},{4,68},{5,69},{6,70},{7,71},{8,72},{9,... | collective-permute-start | bytes 196616 | tf_op jit(solution)/shard_map/ppermute | solution.py:357
  70.3 4.6 %collective-permute-start.12 = (f32[16,1024]{1,0:T(8,128)S(1)}, f32[16,1024]{1,0:T(8,128)S(1)}, u32[]{:S(2)}, u32[]{:S(2)}) collective-permute-start(f32[16,1024]{1,0:T(8,128)S(1)} %get-tuple-element.40), channel_id=1, source_target_pairs={{0,96},{1,97},{2,98},{3,99},{4,100},{5,101},{6,102},{7,103},{8,104... | collective-permute-start | bytes 196616 | tf_op jit(solution)/shard_map/ppermute | solution.py:357
  74.9 5.1 %collective-permute-start.13 = (f32[16,1024]{1,0:T(8,128)S(1)}, f32[16,1024]{1,0:T(8,128)S(1)}, u32[]{:S(2)}, u32[]{:S(2)}) collective-permute-start(f32[16,1024]{1,0:T(8,128)S(1)} %sum_x.1.refs_1_), channel_id=1, source_target_pairs={{0,16},{1,17},{2,18},{3,19},{4,20},{5,21},{6,22},{7,23},{8,24},{9,... | collective-permute-start | bytes 196616 | tf_op jit(solution)/shard_map/ppermute | solution.py:357
  81.2 6.1 %collective-permute-start.16 = (f32[256,1152]{1,0:T(8,128)S(1)}, f32[256,1152]{1,0:T(8,128)S(1)}, u32[]{:S(2)}, u32[]{:S(2)}) collective-permute-start(f32[256,1152]{1,0:T(8,128)S(1)} %gram_y.1.refs_0_), channel_id=1, source_target_pairs={{0,8},{1,9},{2,10},{3,11},{4,12},{5,13},{6,14},{7,15},{8,0},{9,1},... | collective-permute-start | bytes 3538952 | tf_op jit(solution)/shard_map/ppermute | solution.py:357
  83.3 8.2 %collective-permute-start.17 = (f32[16,1024]{1,0:T(8,128)S(1)}, f32[16,1024]{1,0:T(8,128)S(1)}, u32[]{:S(2)}, u32[]{:S(2)}) collective-permute-start(f32[16,1024]{1,0:T(8,128)S(1)} %sum_z.1._.refs_0_), channel_id=1, source_target_pairs={{0,32},{1,33},{2,34},{3,35},{4,36},{5,37},{6,38},{7,39},{8,40},{9,... | collective-permute-start | bytes 196616 | tf_op jit(solution)/shard_map/ppermute | solution.py:357
  83.3 8.2 %collective-permute-start.18 = (f32[16,1024]{1,0:T(8,128)S(1)}, f32[16,1024]{1,0:T(8,128)S(1)}, u32[]{:S(2)}, u32[]{:S(2)}) collective-permute-start(f32[16,1024]{1,0:T(8,128)S(1)} %sum_z.1._.refs_0_), channel_id=1, source_target_pairs={{0,64},{1,65},{2,66},{3,67},{4,68},{5,69},{6,70},{7,71},{8,72},{9,... | collective-permute-start | bytes 196616 | tf_op jit(solution)/shard_map/ppermute | solution.py:357
  85.4 6.2 %collective-permute-start.19 = (f32[16,1024]{1,0:T(8,128)S(1)}, f32[16,1024]{1,0:T(8,128)S(1)}, u32[]{:S(2)}, u32[]{:S(2)}) collective-permute-start(f32[16,1024]{1,0:T(8,128)S(1)} %sum_z.1._.refs_0_), channel_id=1, source_target_pairs={{0,96},{1,97},{2,98},{3,99},{4,100},{5,101},{6,102},{7,103},{8,104... | collective-permute-start | bytes 196616 | tf_op jit(solution)/shard_map/ppermute | solution.py:357
  91.6 2.6 %collective-permute-start.20 = (f32[64,1024]{1,0:T(8,128)S(1)}, f32[64,1024]{1,0:T(8,128)S(1)}, u32[]{:S(2)}, u32[]{:S(2)}) collective-permute-start(f32[64,1024]{1,0:T(8,128)S(1)} %sum_join.1.refs_0_), channel_id=1, source_target_pairs={{0,8},{1,9},{2,10},{3,11},{4,12},{5,13},{6,14},{7,15},{8,0},{9,1},... | collective-permute-start | bytes 786440 | tf_op jit(solution)/shard_map/ppermute | solution.py:357

commit v5 on v4

--- a/solution.py
+++ b/solution.py
@@ -275,9 +275,12 @@
     powers = [jnp.where(same & (r > c), -lows[q] * scaled[q], 0.0) for q in range(blocks)]
     identity = jnp.where(r == c, 1.0, 0.0)
     products = [identity + powers[q] for q in range(blocks)]
-    for _ in range(5):
-        powers = [dot3(powers[q], powers[q]) for q in range(blocks)]
-        products = [products[q] + dot3(products[q], powers[q]) for q in range(blocks)]
+    powers = [dot3(power, power) for power in powers]
+    for _ in range(4):
+        both = [dot3(jnp.concatenate([powers[q], products[q]], axis=0), powers[q]) for q in range(blocks)]
+        powers = [part[:BLOCK] for part in both]
+        products = [products[q] + both[q][BLOCK:] for q in range(blocks)]
+    products = [products[q] + dot3(products[q], powers[q]) for q in range(blocks)]
     inverses = [products[q] * scales[q] for q in range(blocks)]
     pair = (r >= HALF) & (c < HALF)
     mids = [dot3(jnp.where(pair, lows[q], 0.0), inverses[q]) for q in range(blocks)]
@@ -331,11 +334,12 @@
         w_ref[count:, at : at + half] = dot(order, wl).astype(BF16)
 
     copies = []
-    for step, at in enumerate(range(0, rows, WIDE)):
-        part = slice(at, at + WIDE)
+    edges = list(range(0, rows, WIDE)) + [rows - WIDE // 2, rows]
+    for step, (at, end) in enumerate(zip(edges, edges[1:])):
+        part = slice(at, end)
         split = held_refs[0].shape[0]
         high_ref, low_ref = held_refs[:2] if at < split else held_refs[2:]
-        held = slice(at, at + WIDE) if at < split else slice(at - split, at - split + WIDE)
+        held = slice(at, end) if at < split else slice(at - split, end - split)
         both = dot(w_ref[...], high_ref[held, :], 1, 1)
         change = both[:count] + (both[count:] + dot(w_ref[:count, :], low_ref[held, :], 1, 1))
         put_ref[:, part] = vec_ref[:, part] - change
@@ -505,7 +509,7 @@
             pltpu.VMEM((count, total), F32),
             pltpu.VMEM((2 * count, total), BF16),
             pltpu.VMEM((count, rows_dev), F32),
-            pltpu.SemaphoreType.DMA((steps,)),
+            pltpu.SemaphoreType.DMA((steps + 1,)),
         ],
         compiler_params=params(12),
         cost_estimate=cost(6 * rows_dev * count * total, 4 * rows_dev * count),

time: 103 us -> 103 us (level)
  no operation moved by 1% of the time
where the time goes in v5:
time: 103 us
  Pallas kernels  46.3 us (45%)
  starting transfers between devices  36.6 us (36%)
  waiting for transfers between devices  18.9 us (18%)
    ppermute x21, starting transfers between devices, swap(): return lax.ppermute(x, ('row', 'col'), [(i, i ^ bits) for i in range(128)])  27.3 us
    pallas_call x1, Pallas kernels, per_device(): pl.pallas_call(gram_kernel, in_specs=[smem, vmem, hbm], out_specs=[hbm, h...  19.9 us
    ppermute x21, waiting for transfers between devices, swap(): return lax.ppermute(x, ('row', 'col'), [(i, i ^ bits) for i in range(128)])  18.9 us
    all_to_all x1, starting transfers between devices, per_device(): lax.all_to_all(shaped, 'row', 0, 0, tiled=True).reshape(count, rows_dev)  9.26 us
    pallas_call x1, Pallas kernels, per_device(): pl.pallas_call(change_kernel, in_specs=[smem] + [vmem] * 12, out_specs=hb...  8.21 us
    pallas_call x1, Pallas kernels, per_device(): pl.pallas_call(first_product_kernel, in_specs=[after, vmem, hbm, hbm], ou...  4.74 us
    pallas_call x1, Pallas kernels, per_device(): pl.pallas_call(last_product_kernel, in_specs=[after, smem, vmem, vmem, hb...  4.72 us
    pallas_call x1, Pallas kernels, per_device(): pl.pallas_call(blocks_kernel, in_specs=[smem] + [vmem] * 2, out_specs=[vm...  4.36 us
  transfers between devices with their start and end apart: 22, of which 7 were waited for; matrix products, arithmetic and copies ran while one was open for 0% of the time, Pallas kernels for 37%

profile of v5, /device:TPU:1, one launch (start us, length us, event | category | flops | bytes accessed | tf_op | source)
XLA Modules:
  0.0 102.7 jit_solution(17621584477370759269)
XLA Ops:
  0.0 9.3 %all-to-all-start = ((f32[16,8,4608]{2,1,0:T(8,128)}), f32[16,8,4608]{2,1,0:T(8,128)S(1)}, u32[]{:S(2)}, u32[]{:S(2)}) async-start(f32[16,8,4608]{2,1,0:T(8,128)} %bitcast.11), calls=%async_computation | async-start | bytes 4718592 | tf_op jit(solution)/shard_map/all_to_all | solution.py:401
  9.5 19.9 %gram.1 = (bf16[4608,1024]{1,0:T(8,128)(2,1)}, bf16[4608,1024]{1,0:T(8,128)(2,1)}, f32[64,1152]{1,0:T(8,128)S(1)}, f32[64,1152]{1,0:T(8,128)S(1)}) custom-call(s32[4]{0:T(128)S(1)} %pad_add_fusion.place_ref, s32[1,1024]{1,0:T(1,128)S(1)} %add.56.lead_ref, f32[4608,1024]{1,0:T(8,128)} %tiles_ref.1), custom_call_target="tpu_custom_call" | custom-call | flops 7247757312 | bytes 37748736 | tf_op jit(solution)/shard_map/gram/pallas_call | solution.py:406
  29.4 0.2 collective-permute-start
  29.6 1.5 %collective-permute-done = f32[64,1152]{1,0:T(8,128)S(1)} collective-permute-done((f32[64,1152]{1,0:T(8,128)S(1)}, f32[64,1152]{1,0:T(8,128)S(1)}, u32[]{:S(2)}, u32[]{:S(2)}) %collective-permute-start) | collective-permute-done | bytes 294944 | tf_op jit(solution)/shard_map/ppermute | solution.py:361
  31.1 1.5 %collective-permute-start.1 = (f32[16,1152]{1,0:T(8,128)S(1)}, f32[16,1152]{1,0:T(8,128)S(1)}, u32[]{:S(2)}, u32[]{:S(2)}) collective-permute-start(f32[16,1152]{1,0:T(8,128)S(1)} %get-tuple-element.37), channel_id=1, source_target_pairs={{0,32},{1,33},{2,34},{3,35},{4,36},{5,37},{6,38},{7,39},{8,40},{9,... | collective-permute-start | bytes 221192 | tf_op jit(solution)/shard_map/ppermute | solution.py:361
  32.6 1.8 %collective-permute-start.2 = (f32[16,1152]{1,0:T(8,128)S(1)}, f32[16,1152]{1,0:T(8,128)S(1)}, u32[]{:S(2)}, u32[]{:S(2)}) collective-permute-start(f32[16,1152]{1,0:T(8,128)S(1)} %get-tuple-element.39), channel_id=1, source_target_pairs={{0,96},{1,97},{2,98},{3,99},{4,100},{5,101},{6,102},{7,103},{8,104... | collective-permute-start | bytes 221192 | tf_op jit(solution)/shard_map/ppermute | solution.py:361
  34.4 0.6 collective-permute-start.3
  35.0 3.6 %collective-permute-done.1 = f32[16,1152]{1,0:T(8,128)S(1)} collective-permute-done((f32[16,1152]{1,0:T(8,128)S(1)}, f32[16,1152]{1,0:T(8,128)S(1)}, u32[]{:S(2)}, u32[]{:S(2)}) %collective-permute-start.1) | collective-permute-done | bytes 73760 | tf_op jit(solution)/shard_map/ppermute | solution.py:361
  38.6 5.5 %collective-permute-done.2 = f32[16,1152]{1,0:T(8,128)S(1)} collective-permute-done((f32[16,1152]{1,0:T(8,128)S(1)}, f32[16,1152]{1,0:T(8,128)S(1)}, u32[]{:S(2)}, u32[]{:S(2)}) %collective-permute-start.2) | collective-permute-done | bytes 73760 | tf_op jit(solution)/shard_map/ppermute | solution.py:361
  44.1 1.1 %collective-permute-done.3 = f32[16,1152]{1,0:T(8,128)S(1)} collective-permute-done((f32[16,1152]{1,0:T(8,128)S(1)}, f32[16,1152]{1,0:T(8,128)S(1)}, u32[]{:S(2)}, u32[]{:S(2)}) %collective-permute-start.3) | collective-permute-done | bytes 73760 | tf_op jit(solution)/shard_map/ppermute | solution.py:361
  45.3 4.7 %product_first.1 = (bf16[2560,1024]{1,0:T(8,128)(2,1)S(1)}, bf16[2560,1024]{1,0:T(8,128)(2,1)S(1)}, f32[128,1024]{1,0:T(8,128)S(1)}) custom-call(f32[16,1152]{1,0:T(8,128)S(1)} %fusion.1._.refs_1_, f32[128,4608]{1,0:T(8,128)S(1)} %bitcast.8, bf16[4608,1024]{1,0:T(8,128)(2,1)} %get-tuple-element.23.from_high_ref, ...), custom_call_target="tpu_custom_call" | custom-call | flops 1811939328 | bytes 9437184 | tf_op jit(solution)/shard_map/product_first/pallas_call | solution.py:437
  50.1 0.1 collective-permute-start.5
  50.2 2.8 %collective-permute-start.6 = (f32[16,1152]{1,0:T(8,128)S(1)}, f32[16,1152]{1,0:T(8,128)S(1)}, u32[]{:S(2)}, u32[]{:S(2)}) collective-permute-start(f32[16,1152]{1,0:T(8,128)S(1)} %gram_z.1._.refs_0_), channel_id=1, source_target_pairs={{0,64},{1,65},{2,66},{3,67},{4,68},{5,69},{6,70},{7,71},{8,72},{9,... | collective-permute-start | bytes 221192 | tf_op jit(solution)/shard_map/ppermute | solution.py:361
  53.0 1.0 %collective-permute-start.7 = (f32[16,1152]{1,0:T(8,128)S(1)}, f32[16,1152]{1,0:T(8,128)S(1)}, u32[]{:S(2)}, u32[]{:S(2)}) collective-permute-start(f32[16,1152]{1,0:T(8,128)S(1)} %gram_z.1._.refs_0_), channel_id=1, source_target_pairs={{0,96},{1,97},{2,98},{3,99},{4,100},{5,101},{6,102},{7,103},{8,104... | collective-permute-start | bytes 221192 | tf_op jit(solution)/shard_map/ppermute | solution.py:361
  54.0 4.7 %product_last.1 = (bf16[2048,1024]{1,0:T(8,128)(2,1)S(1)}, bf16[2048,1024]{1,0:T(8,128)(2,1)S(1)}, f32[128,1024]{1,0:T(8,128)S(1)}) custom-call(f32[16,1152]{1,0:T(8,128)S(1)} %gram_z.1._.refs_0_, s32[4]{0:T(128)S(1)} %pad_add_fusion.place_ref, f32[128,1024]{1,0:T(8,128)S(1)} %get-tuple-element.25.refs_0_.total_ref, f32[128,4608]{1,0:T(8,128)S(1)} %bitcast.9, ...), custom_call_target="tpu_custom_call" | custom-call | flops 1811939328 | bytes 9437184 | tf_op jit(solution)/shard_map/product_last/pallas_call | solution.py:449
  58.8 2.9 %collective-permute-start.9 = (f32[64,1024]{1,0:T(8,128)S(1)}, f32[64,1024]{1,0:T(8,128)S(1)}, u32[]{:S(2)}, u32[]{:S(2)}) collective-permute-start(f32[64,1024]{1,0:T(8,128)S(1)} %sum_split.1), channel_id=1, source_target_pairs={{0,8},{1,9},{2,10},{3,11},{4,12},{5,13},{6,14},{7,15},{8,0},{9,1},... | collective-permute-start | bytes 786440 | tf_op jit(solution)/shard_map/ppermute | solution.py:361
  61.7 1.3 %collective-permute-start.8 = (f32[64,1152]{1,0:T(8,128)S(1)}, f32[64,1152]{1,0:T(8,128)S(1)}, u32[]{:S(2)}, u32[]{:S(2)}) collective-permute-start(f32[64,1152]{1,0:T(8,128)S(1)} %gram_x.1._.refs_0_), channel_id=1, source_target_pairs={{0,1},{1,0},{2,3},{3,2},{4,5},{5,4},{6,7},{7,6},{8,9},{9,8},{10,11... | collective-permute-start | bytes 884744 | tf_op jit(solution)/shard_map/ppermute | solution.py:361
  63.0 2.6 %collective-permute-start.14 = (f32[64,1152]{1,0:T(8,128)S(1)}, f32[64,1152]{1,0:T(8,128)S(1)}, u32[]{:S(2)}, u32[]{:S(2)}) collective-permute-start(f32[64,1152]{1,0:T(8,128)S(1)} %gram_x.1._.refs_0_), channel_id=1, source_target_pairs={{0,2},{1,3},{2,0},{3,1},{4,6},{5,7},{6,4},{7,5},{8,10},{9,11},{10,... | collective-permute-start | bytes 884744 | tf_op jit(solution)/shard_map/ppermute | solution.py:361
  65.8 2.0 %collective-permute-start.11 = (f32[16,1024]{1,0:T(8,128)S(1)}, f32[16,1024]{1,0:T(8,128)S(1)}, u32[]{:S(2)}, u32[]{:S(2)}) collective-permute-start(f32[16,1024]{1,0:T(8,128)S(1)} %get-tuple-element.41), channel_id=1, source_target_pairs={{0,64},{1,65},{2,66},{3,67},{4,68},{5,69},{6,70},{7,71},{8,72},{9,... | collective-permute-start | bytes 196616 | tf_op jit(solution)/shard_map/ppermute | solution.py:361
  67.8 2.4 %collective-permute-done.8._.refs_1_ = f32[64,1152]{1,0:T(8,128)S(1)} collective-permute-done((f32[64,1152]{1,0:T(8,128)S(1)}, f32[64,1152]{1,0:T(8,128)S(1)}, u32[]{:S(2)}, u32[]{:S(2)}) %collective-permute-start.8) | collective-permute-done | bytes 294944 | tf_op jit(solution)/shard_map/ppermute | solution.py:361
  70.3 0.9 collective-permute-start.12
  71.2 3.7 %collective-permute-done.12.refs_3_ = f32[16,1024]{1,0:T(8,128)S(1)} collective-permute-done((f32[16,1024]{1,0:T(8,128)S(1)}, f32[16,1024]{1,0:T(8,128)S(1)}, u32[]{:S(2)}, u32[]{:S(2)}) %collective-permute-start.12) | collective-permute-done | bytes 65568 | tf_op jit(solution)/shard_map/ppermute | solution.py:361
  74.9 2.4 %collective-permute-start.13 = (f32[16,1024]{1,0:T(8,128)S(1)}, f32[16,1024]{1,0:T(8,128)S(1)}, u32[]{:S(2)}, u32[]{:S(2)}) collective-permute-start(f32[16,1024]{1,0:T(8,128)S(1)} %sum_x.1.refs_1_), channel_id=1, source_target_pairs={{0,16},{1,17},{2,18},{3,19},{4,20},{5,21},{6,22},{7,23},{8,24},{9,... | collective-permute-start | bytes 196616 | tf_op jit(solution)/shard_map/ppermute | solution.py:361
  77.4 2.6 %reorder.1.refs_0_.refs_6_ = f32[128,4608]{1,0:T(8,128)S(1)} custom-call(bf16[128,128]{1,0:T(8,128)(2,1)S(1)} %fusion.2.order_ref, f32[128,4608]{1,0:T(8,128)S(1)} %bitcast.10), custom_call_target="tpu_custom_call" | custom-call | flops 452984832 | bytes 9437184 | tf_op jit(solution)/shard_map/reorder/pallas_call | solution.py:462
  80.1 1.0 collective-permute-done.15.refs_3_
  81.2 2.2 %collective-permute-start.16 = (f32[256,1152]{1,0:T(8,128)S(1)}, f32[256,1152]{1,0:T(8,128)S(1)}, u32[]{:S(2)}, u32[]{:S(2)}) collective-permute-start(f32[256,1152]{1,0:T(8,128)S(1)} %gram_y.1.refs_0_), channel_id=1, source_target_pairs={{0,8},{1,9},{2,10},{3,11},{4,12},{5,13},{6,14},{7,15},{8,0},{9,1},... | collective-permute-start | bytes 3538952 | tf_op jit(solution)/shard_map/ppermute | solution.py:361
  83.3 2.0 %collective-permute-start.18 = (f32[16,1024]{1,0:T(8,128)S(1)}, f32[16,1024]{1,0:T(8,128)S(1)}, u32[]{:S(2)}, u32[]{:S(2)}) collective-permute-start(f32[16,1024]{1,0:T(8,128)S(1)} %sum_z.1._.refs_0_), channel_id=1, source_target_pairs={{0,64},{1,65},{2,66},{3,67},{4,68},{5,69},{6,70},{7,71},{8,72},{9,... | collective-permute-start | bytes 196616 | tf_op jit(solution)/shard_map/ppermute | solution.py:361
  85.4 1.8 %collective-permute-start.19 = (f32[16,1024]{1,0:T(8,128)S(1)}, f32[16,1024]{1,0:T(8,128)S(1)}, u32[]{:S(2)}, u32[]{:S(2)}) collective-permute-start(f32[16,1024]{1,0:T(8,128)S(1)} %sum_z.1._.refs_0_), channel_id=1, source_target_pairs={{0,96},{1,97},{2,98},{3,99},{4,100},{5,101},{6,102},{7,103},{8,104... | collective-permute-start | bytes 196616 | tf_op jit(solution)/shard_map/ppermute | solution.py:361
  87.2 4.4 %inverse_blocks.1 = (f32[1024,1024]{1,0:T(8,128)S(1)}, f32[8,128,128]{2,1,0:T(8,128)S(1)}) custom-call(s32[4]{0:T(128)S(1)} %pad_add_fusion.place_ref, f32[256,1152]{1,0:T(8,128)S(1)} %gram_y.1.refs_0_, f32[256,1152]{1,0:T(8,128)S(1)} %collective-permute-done.16.refs_1_), custom_call_target="tpu_custom_call" | custom-call | flops 4294967296 | bytes 4194304 | tf_op jit(solution)/shard_map/inverse_blocks/pallas_call | solution.py:480
  91.6 1.0 collective-permute-start.20
  92.6 1.6 %inverse.1 = (bf16[1024,512]{1,0:T(8,128)(2,1)S(1)}, bf16[1024,512]{1,0:T(8,128)(2,1)S(1)}, bf16[512,512]{1,0:T(8,128)(2,1)S(1)}, bf16[512,512]{1,0:T(8,128)(2,1)S(1)}) custom-call(f32[1024,1024]{1,0:T(8,128)S(1)} %get-tuple-element.28.lower_ref, f32[8,128,128]{2,1,0:T(8,128)S(1)} %get-tuple-element.27._.blocks_ref), custom_call_target="tpu_custom_call" | custom-call | flops 4294967296 | bytes 4194304 | tf_op jit(solution)/shard_map/inverse/pallas_call | solution.py:492
  94.3 8.2 %change.1 = f32[128,4608]{1,0:T(8,128)} custom-call(s32[4]{0:T(128)S(1)} %pad_add_fusion.place_ref, bf16[128,128]{1,0:T(8,128)(2,1)S(1)} %fusion.2.order_ref, f32[64,1024]{1,0:T(8,128)S(1)} %sum_join.1.refs_0_, f32[64,1024]{1,0:T(8,128)S(1)} %collective-permute-done.20.refs_1_, bf16[1024,512]{1,0:T(8,128)(2,1)S(1)} %get-tuple-element.29.refs_2_, ...), custom_call_target="tpu_custom_call" | custom-call | flops 3623878656 | bytes 2359296 | tf_op jit(solution)/shard_map/change/pallas_call | solution.py:503
  (40 shorter events, 0.9 us)
Async XLA Ops:
  0.0 9.3 %copy-start = (s32[16]{0:T(128)S(1)}, s32[16]{0:T(128)}, u32[]{:S(2)}) copy-start(s32[16]{0:T(128)} %param.7) | copy-start | bytes 196
  0.0 45.3 %all-to-all-start = ((f32[16,8,4608]{2,1,0:T(8,128)}), f32[16,8,4608]{2,1,0:T(8,128)S(1)}, u32[]{:S(2)}, u32[]{:S(2)}) async-start(f32[16,8,4608]{2,1,0:T(8,128)} %bitcast.11), calls=%async_computation | async-start | bytes 4718592 | tf_op jit(solution)/shard_map/all_to_all | solution.py:401
  29.4 1.7 %collective-permute-start = (f32[64,1152]{1,0:T(8,128)S(1)}, f32[64,1152]{1,0:T(8,128)S(1)}, u32[]{:S(2)}, u32[]{:S(2)}) collective-permute-start(f32[64,1152]{1,0:T(8,128)S(1)} %get-tuple-element.22), channel_id=1, source_target_pairs={{0,8},{1,9},{2,10},{3,11},{4,12},{5,13},{6,14},{7,15},{8,0},{9,1},... | collective-permute-start | bytes 884744 | tf_op jit(solution)/shard_map/ppermute | solution.py:361
  31.1 7.5 %collective-permute-start.1 = (f32[16,1152]{1,0:T(8,128)S(1)}, f32[16,1152]{1,0:T(8,128)S(1)}, u32[]{:S(2)}, u32[]{:S(2)}) collective-permute-start(f32[16,1152]{1,0:T(8,128)S(1)} %get-tuple-element.37), channel_id=1, source_target_pairs={{0,32},{1,33},{2,34},{3,35},{4,36},{5,37},{6,38},{7,39},{8,40},{9,... | collective-permute-start | bytes 221192 | tf_op jit(solution)/shard_map/ppermute | solution.py:361
  32.6 11.5 %collective-permute-start.2 = (f32[16,1152]{1,0:T(8,128)S(1)}, f32[16,1152]{1,0:T(8,128)S(1)}, u32[]{:S(2)}, u32[]{:S(2)}) collective-permute-start(f32[16,1152]{1,0:T(8,128)S(1)} %get-tuple-element.39), channel_id=1, source_target_pairs={{0,96},{1,97},{2,98},{3,99},{4,100},{5,101},{6,102},{7,103},{8,104... | collective-permute-start | bytes 221192 | tf_op jit(solution)/shard_map/ppermute | solution.py:361
  34.4 10.8 %collective-permute-start.3 = (f32[16,1152]{1,0:T(8,128)S(1)}, f32[16,1152]{1,0:T(8,128)S(1)}, u32[]{:S(2)}, u32[]{:S(2)}) collective-permute-start(f32[16,1152]{1,0:T(8,128)S(1)} %get-tuple-element.38), channel_id=1, source_target_pairs={{0,64},{1,65},{2,66},{3,67},{4,68},{5,69},{6,70},{7,71},{8,72},{9,... | collective-permute-start | bytes 221192 | tf_op jit(solution)/shard_map/ppermute | solution.py:361
  45.2 4.9 %collective-permute-start.4 = (f32[16,1152]{1,0:T(8,128)S(1)}, f32[16,1152]{1,0:T(8,128)S(1)}, u32[]{:S(2)}, u32[]{:S(2)}) collective-permute-start(f32[16,1152]{1,0:T(8,128)S(1)} %fusion.1._.refs_1_), channel_id=1, source_target_pairs={{0,16},{1,17},{2,18},{3,19},{4,20},{5,21},{6,22},{7,23},{8,24},{9,... | collective-permute-start | bytes 221192 | tf_op jit(solution)/shard_map/ppermute | solution.py:361
  50.1 21.0 %copy-start.1 = (s32[128]{0:T(128)S(1)}, s32[128]{0:T(128)}, u32[]{:S(2)}) copy-start(s32[128]{0:T(128)} %param.5) | copy-start | bytes 1540
  50.1 8.7 %collective-permute-start.5 = (f32[16,1152]{1,0:T(8,128)S(1)}, f32[16,1152]{1,0:T(8,128)S(1)}, u32[]{:S(2)}, u32[]{:S(2)}) collective-permute-start(f32[16,1152]{1,0:T(8,128)S(1)} %gram_z.1._.refs_0_), channel_id=1, source_target_pairs={{0,32},{1,33},{2,34},{3,35},{4,36},{5,37},{6,38},{7,39},{8,40},{9,... | collective-permute-start | bytes 221192 | tf_op jit(solution)/shard_map/ppermute | solution.py:361
  50.2 8.6 %collective-permute-start.6 = (f32[16,1152]{1,0:T(8,128)S(1)}, f32[16,1152]{1,0:T(8,128)S(1)}, u32[]{:S(2)}, u32[]{:S(2)}) collective-permute-start(f32[16,1152]{1,0:T(8,128)S(1)} %gram_z.1._.refs_0_), channel_id=1, source_target_pairs={{0,64},{1,65},{2,66},{3,67},{4,68},{5,69},{6,70},{7,71},{8,72},{9,... | collective-permute-start | bytes 221192 | tf_op jit(solution)/shard_map/ppermute | solution.py:361
  53.0 5.8 %collective-permute-start.7 = (f32[16,1152]{1,0:T(8,128)S(1)}, f32[16,1152]{1,0:T(8,128)S(1)}, u32[]{:S(2)}, u32[]{:S(2)}) collective-permute-start(f32[16,1152]{1,0:T(8,128)S(1)} %gram_z.1._.refs_0_), channel_id=1, source_target_pairs={{0,96},{1,97},{2,98},{3,99},{4,100},{5,101},{6,102},{7,103},{8,104... | collective-permute-start | bytes 221192 | tf_op jit(solution)/shard_map/ppermute | solution.py:361
  58.8 6.8 %collective-permute-start.9 = (f32[64,1024]{1,0:T(8,128)S(1)}, f32[64,1024]{1,0:T(8,128)S(1)}, u32[]{:S(2)}, u32[]{:S(2)}) collective-permute-start(f32[64,1024]{1,0:T(8,128)S(1)} %sum_split.1), channel_id=1, source_target_pairs={{0,8},{1,9},{2,10},{3,11},{4,12},{5,13},{6,14},{7,15},{8,0},{9,1},... | collective-permute-start | bytes 786440 | tf_op jit(solution)/shard_map/ppermute | solution.py:361
  61.7 8.6 %collective-permute-start.8 = (f32[64,1152]{1,0:T(8,128)S(1)}, f32[64,1152]{1,0:T(8,128)S(1)}, u32[]{:S(2)}, u32[]{:S(2)}) collective-permute-start(f32[64,1152]{1,0:T(8,128)S(1)} %gram_x.1._.refs_0_), channel_id=1, source_target_pairs={{0,1},{1,0},{2,3},{3,2},{4,5},{5,4},{6,7},{7,6},{8,9},{9,8},{10,11... | collective-permute-start | bytes 884744 | tf_op jit(solution)/shard_map/ppermute | solution.py:361
  63.0 17.0 %collective-permute-start.14 = (f32[64,1152]{1,0:T(8,128)S(1)}, f32[64,1152]{1,0:T(8,128)S(1)}, u32[]{:S(2)}, u32[]{:S(2)}) collective-permute-start(f32[64,1152]{1,0:T(8,128)S(1)} %gram_x.1._.refs_0_), channel_id=1, source_target_pairs={{0,2},{1,3},{2,0},{3,1},{4,6},{5,7},{6,4},{7,5},{8,10},{9,11},{10,... | collective-permute-start | bytes 884744 | tf_op jit(solution)/shard_map/ppermute | solution.py:361
  65.6 15.4 %collective-permute-start.15 = (f32[64,1152]{1,0:T(8,128)S(1)}, f32[64,1152]{1,0:T(8,128)S(1)}, u32[]{:S(2)}, u32[]{:S(2)}) collective-permute-start(f32[64,1152]{1,0:T(8,128)S(1)} %gram_x.1._.refs_0_), channel_id=1, source_target_pairs={{0,3},{1,2},{2,1},{3,0},{4,7},{5,6},{6,5},{7,4},{8,11},{9,10},{10,... | collective-permute-start | bytes 884744 | tf_op jit(solution)/shard_map/ppermute | solution.py:361
  65.7 5.4 %collective-permute-start.10 = (f32[16,1024]{1,0:T(8,128)S(1)}, f32[16,1024]{1,0:T(8,128)S(1)}, u32[]{:S(2)}, u32[]{:S(2)}) collective-permute-start(f32[16,1024]{1,0:T(8,128)S(1)} %get-tuple-element.42), channel_id=1, source_target_pairs={{0,32},{1,33},{2,34},{3,35},{4,36},{5,37},{6,38},{7,39},{8,40},{9,... | collective-permute-start | bytes 196616 | tf_op jit(solution)/shard_map/ppermute | solution.py:361
  65.8 5.3 %collective-permute-start.11 = (f32[16,1024]{1,0:T(8,128)S(1)}, f32[16,1024]{1,0:T(8,128)S(1)}, u32[]{:S(2)}, u32[]{:S(2)}) collective-permute-start(f32[16,1024]{1,0:T(8,128)S(1)} %get-tuple-element.41), channel_id=1, source_target_pairs={{0,64},{1,65},{2,66},{3,67},{4,68},{5,69},{6,70},{7,71},{8,72},{9,... | collective-permute-start | bytes 196616 | tf_op jit(solution)/shard_map/ppermute | solution.py:361
  70.3 4.6 %collective-permute-start.12 = (f32[16,1024]{1,0:T(8,128)S(1)}, f32[16,1024]{1,0:T(8,128)S(1)}, u32[]{:S(2)}, u32[]{:S(2)}) collective-permute-start(f32[16,1024]{1,0:T(8,128)S(1)} %get-tuple-element.40), channel_id=1, source_target_pairs={{0,96},{1,97},{2,98},{3,99},{4,100},{5,101},{6,102},{7,103},{8,104... | collective-permute-start | bytes 196616 | tf_op jit(solution)/shard_map/ppermute | solution.py:361
  74.9 5.1 %collective-permute-start.13 = (f32[16,1024]{1,0:T(8,128)S(1)}, f32[16,1024]{1,0:T(8,128)S(1)}, u32[]{:S(2)}, u32[]{:S(2)}) collective-permute-start(f32[16,1024]{1,0:T(8,128)S(1)} %sum_x.1.refs_1_), channel_id=1, source_target_pairs={{0,16},{1,17},{2,18},{3,19},{4,20},{5,21},{6,22},{7,23},{8,24},{9,... | collective-permute-start | bytes 196616 | tf_op jit(solution)/shard_map/ppermute | solution.py:361
  81.2 6.1 %collective-permute-start.16 = (f32[256,1152]{1,0:T(8,128)S(1)}, f32[256,1152]{1,0:T(8,128)S(1)}, u32[]{:S(2)}, u32[]{:S(2)}) collective-permute-start(f32[256,1152]{1,0:T(8,128)S(1)} %gram_y.1.refs_0_), channel_id=1, source_target_pairs={{0,8},{1,9},{2,10},{3,11},{4,12},{5,13},{6,14},{7,15},{8,0},{9,1},... | collective-permute-start | bytes 3538952 | tf_op jit(solution)/shard_map/ppermute | solution.py:361
  83.3 8.2 %collective-permute-start.17 = (f32[16,1024]{1,0:T(8,128)S(1)}, f32[16,1024]{1,0:T(8,128)S(1)}, u32[]{:S(2)}, u32[]{:S(2)}) collective-permute-start(f32[16,1024]{1,0:T(8,128)S(1)} %sum_z.1._.refs_0_), channel_id=1, source_target_pairs={{0,32},{1,33},{2,34},{3,35},{4,36},{5,37},{6,38},{7,39},{8,40},{9,... | collective-permute-start | bytes 196616 | tf_op jit(solution)/shard_map/ppermute | solution.py:361
  83.3 8.3 %collective-permute-start.18 = (f32[16,1024]{1,0:T(8,128)S(1)}, f32[16,1024]{1,0:T(8,128)S(1)}, u32[]{:S(2)}, u32[]{:S(2)}) collective-permute-start(f32[16,1024]{1,0:T(8,128)S(1)} %sum_z.1._.refs_0_), channel_id=1, source_target_pairs={{0,64},{1,65},{2,66},{3,67},{4,68},{5,69},{6,70},{7,71},{8,72},{9,... | collective-permute-start | bytes 196616 | tf_op jit(solution)/shard_map/ppermute | solution.py:361
  85.4 6.2 %collective-permute-start.19 = (f32[16,1024]{1,0:T(8,128)S(1)}, f32[16,1024]{1,0:T(8,128)S(1)}, u32[]{:S(2)}, u32[]{:S(2)}) collective-permute-start(f32[16,1024]{1,0:T(8,128)S(1)} %sum_z.1._.refs_0_), channel_id=1, source_target_pairs={{0,96},{1,97},{2,98},{3,99},{4,100},{5,101},{6,102},{7,103},{8,104... | collective-permute-start | bytes 196616 | tf_op jit(solution)/shard_map/ppermute | solution.py:361
  91.6 2.6 %collective-permute-start.20 = (f32[64,1024]{1,0:T(8,128)S(1)}, f32[64,1024]{1,0:T(8,128)S(1)}, u32[]{:S(2)}, u32[]{:S(2)}) collective-permute-start(f32[64,1024]{1,0:T(8,128)S(1)} %sum_join.1.refs_0_), channel_id=1, source_target_pairs={{0,8},{1,9},{2,10},{3,11},{4,12},{5,13},{6,14},{7,15},{8,0},{9,1},... | collective-permute-start | bytes 786440 | tf_op jit(solution)/shard_map/ppermute | solution.py:361

commit v6 on v5

--- a/solution.py
+++ b/solution.py
@@ -423,7 +423,7 @@
     )(place, lead, pltpu.with_memory_space_constraint(reflectors, pltpu.HBM))
     both = keep + swap(send, CORE)
     part = both[:16]
-    for k, bits in ((1, 32), (3, 96), (2, 64)):
+    for k, bits in ((2, 64), (3, 96), (1, 32)):
         part = part + swap(both[k * 16 : k * 16 + 16], bits)
     near = swap(part, Z_HIGH)
 

time: 103 us -> 103 us (level)
  starting transfers between devices: 36.6 us -> 35.5 us
    ppermute x21, starting transfers between devices: 27.3 us -> 26.3 us  [swap(): return lax.ppermute(x, ('row', 'col'), [(i, i ^ bits) for i in range(128)])]
where the time goes in v6:
time: 103 us
  Pallas kernels  46.3 us (45%)
  starting transfers between devices  35.5 us (34%)
  waiting for transfers between devices  19.9 us (19%)
    ppermute x21, starting transfers between devices, swap(): return lax.ppermute(x, ('row', 'col'), [(i, i ^ bits) for i in range(128)])  26.3 us
    ppermute x21, waiting for transfers between devices, swap(): return lax.ppermute(x, ('row', 'col'), [(i, i ^ bits) for i in range(128)])  19.9 us
    pallas_call x1, Pallas kernels, per_device(): pl.pallas_call(gram_kernel, in_specs=[smem, vmem, hbm], out_specs=[hbm, h...  19.9 us
    all_to_all x1, starting transfers between devices, per_device(): lax.all_to_all(shaped, 'row', 0, 0, tiled=True).reshape(count, rows_dev)  9.26 us
    pallas_call x1, Pallas kernels, per_device(): pl.pallas_call(change_kernel, in_specs=[smem] + [vmem] * 12, out_specs=hb...  8.21 us
    pallas_call x1, Pallas kernels, per_device(): pl.pallas_call(first_product_kernel, in_specs=[after, vmem, hbm, hbm], ou...  4.74 us
    pallas_call x1, Pallas kernels, per_device(): pl.pallas_call(last_product_kernel, in_specs=[after, smem, vmem, vmem, hb...  4.72 us
    pallas_call x1, Pallas kernels, per_device(): pl.pallas_call(blocks_kernel, in_specs=[smem] + [vmem] * 2, out_specs=[vm...  4.36 us
  transfers between devices with their start and end apart: 22, of which 7 were waited for; matrix products, arithmetic and copies ran while one was open for 0% of the time, Pallas kernels for 37%

profile of v6, /device:TPU:1, one launch (start us, length us, event | category | flops | bytes accessed | tf_op | source)
XLA Modules:
  0.0 102.6 jit_solution(6502917184329087782)
XLA Ops:
  0.0 9.3 %all-to-all-start = ((f32[16,8,4608]{2,1,0:T(8,128)}), f32[16,8,4608]{2,1,0:T(8,128)S(1)}, u32[]{:S(2)}, u32[]{:S(2)}) async-start(f32[16,8,4608]{2,1,0:T(8,128)} %bitcast.11), calls=%async_computation | async-start | bytes 4718592 | tf_op jit(solution)/shard_map/all_to_all | solution.py:401
  9.5 19.9 %gram.1 = (bf16[4608,1024]{1,0:T(8,128)(2,1)}, bf16[4608,1024]{1,0:T(8,128)(2,1)}, f32[64,1152]{1,0:T(8,128)S(1)}, f32[64,1152]{1,0:T(8,128)S(1)}) custom-call(s32[4]{0:T(128)S(1)} %pad_add_fusion.place_ref, s32[1,1024]{1,0:T(1,128)S(1)} %add.56.lead_ref, f32[4608,1024]{1,0:T(8,128)} %tiles_ref.1), custom_call_target="tpu_custom_call" | custom-call | flops 7247757312 | bytes 37748736 | tf_op jit(solution)/shard_map/gram/pallas_call | solution.py:406
  29.4 0.2 collective-permute-start
  29.6 1.5 %collective-permute-done = f32[64,1152]{1,0:T(8,128)S(1)} collective-permute-done((f32[64,1152]{1,0:T(8,128)S(1)}, f32[64,1152]{1,0:T(8,128)S(1)}, u32[]{:S(2)}, u32[]{:S(2)}) %collective-permute-start) | collective-permute-done | bytes 294944 | tf_op jit(solution)/shard_map/ppermute | solution.py:361
  31.1 3.0 %collective-permute-start.1 = (f32[16,1152]{1,0:T(8,128)S(1)}, f32[16,1152]{1,0:T(8,128)S(1)}, u32[]{:S(2)}, u32[]{:S(2)}) collective-permute-start(f32[16,1152]{1,0:T(8,128)S(1)} %get-tuple-element.37), channel_id=1, source_target_pairs={{0,64},{1,65},{2,66},{3,67},{4,68},{5,69},{6,70},{7,71},{8,72},{9,... | collective-permute-start | bytes 221192 | tf_op jit(solution)/shard_map/ppermute | solution.py:361
  34.1 0.9 collective-permute-start.2
  35.0 8.6 %collective-permute-done.1 = f32[16,1152]{1,0:T(8,128)S(1)} collective-permute-done((f32[16,1152]{1,0:T(8,128)S(1)}, f32[16,1152]{1,0:T(8,128)S(1)}, u32[]{:S(2)}, u32[]{:S(2)}) %collective-permute-start.1) | collective-permute-done | bytes 73760 | tf_op jit(solution)/shard_map/ppermute | solution.py:361
  43.6 1.9 %collective-permute-done.2 = f32[16,1152]{1,0:T(8,128)S(1)} collective-permute-done((f32[16,1152]{1,0:T(8,128)S(1)}, f32[16,1152]{1,0:T(8,128)S(1)}, u32[]{:S(2)}, u32[]{:S(2)}) %collective-permute-start.2) | collective-permute-done | bytes 73760 | tf_op jit(solution)/shard_map/ppermute | solution.py:361
  45.5 0.1 collective-permute-start.4
  45.6 4.7 %product_first.1 = (bf16[2560,1024]{1,0:T(8,128)(2,1)S(1)}, bf16[2560,1024]{1,0:T(8,128)(2,1)S(1)}, f32[128,1024]{1,0:T(8,128)S(1)}) custom-call(f32[16,1152]{1,0:T(8,128)S(1)} %fusion.1._.refs_1_, f32[128,4608]{1,0:T(8,128)S(1)} %bitcast.8, bf16[4608,1024]{1,0:T(8,128)(2,1)} %get-tuple-element.23.from_high_ref, ...), custom_call_target="tpu_custom_call" | custom-call | flops 1811939328 | bytes 9437184 | tf_op jit(solution)/shard_map/product_first/pallas_call | solution.py:437
  50.4 0.1 collective-permute-start.5
  50.5 1.1 %collective-permute-start.6 = (f32[16,1152]{1,0:T(8,128)S(1)}, f32[16,1152]{1,0:T(8,128)S(1)}, u32[]{:S(2)}, u32[]{:S(2)}) collective-permute-start(f32[16,1152]{1,0:T(8,128)S(1)} %gram_z.1._.refs_0_), channel_id=1, source_target_pairs={{0,64},{1,65},{2,66},{3,67},{4,68},{5,69},{6,70},{7,71},{8,72},{9,... | collective-permute-start | bytes 221192 | tf_op jit(solution)/shard_map/ppermute | solution.py:361
  51.6 2.7 %collective-permute-start.7 = (f32[16,1152]{1,0:T(8,128)S(1)}, f32[16,1152]{1,0:T(8,128)S(1)}, u32[]{:S(2)}, u32[]{:S(2)}) collective-permute-start(f32[16,1152]{1,0:T(8,128)S(1)} %gram_z.1._.refs_0_), channel_id=1, source_target_pairs={{0,96},{1,97},{2,98},{3,99},{4,100},{5,101},{6,102},{7,103},{8,104... | collective-permute-start | bytes 221192 | tf_op jit(solution)/shard_map/ppermute | solution.py:361
  54.4 4.7 %product_last.1 = (bf16[2048,1024]{1,0:T(8,128)(2,1)S(1)}, bf16[2048,1024]{1,0:T(8,128)(2,1)S(1)}, f32[128,1024]{1,0:T(8,128)S(1)}) custom-call(f32[16,1152]{1,0:T(8,128)S(1)} %gram_z.1._.refs_0_, s32[4]{0:T(128)S(1)} %pad_add_fusion.place_ref, f32[128,1024]{1,0:T(8,128)S(1)} %get-tuple-element.25.refs_0_.total_ref, f32[128,4608]{1,0:T(8,128)S(1)} %bitcast.9, ...), custom_call_target="tpu_custom_call" | custom-call | flops 1811939328 | bytes 9437184 | tf_op jit(solution)/shard_map/product_last/pallas_call | solution.py:449
  59.2 2.5 %collective-permute-start.9 = (f32[64,1024]{1,0:T(8,128)S(1)}, f32[64,1024]{1,0:T(8,128)S(1)}, u32[]{:S(2)}, u32[]{:S(2)}) collective-permute-start(f32[64,1024]{1,0:T(8,128)S(1)} %sum_split.1), channel_id=1, source_target_pairs={{0,8},{1,9},{2,10},{3,11},{4,12},{5,13},{6,14},{7,15},{8,0},{9,1},... | collective-permute-start | bytes 786440 | tf_op jit(solution)/shard_map/ppermute | solution.py:361
  61.7 1.3 %collective-permute-start.8 = (f32[64,1152]{1,0:T(8,128)S(1)}, f32[64,1152]{1,0:T(8,128)S(1)}, u32[]{:S(2)}, u32[]{:S(2)}) collective-permute-start(f32[64,1152]{1,0:T(8,128)S(1)} %gram_x.1._.refs_0_), channel_id=1, source_target_pairs={{0,1},{1,0},{2,3},{3,2},{4,5},{5,4},{6,7},{7,6},{8,9},{9,8},{10,11... | collective-permute-start | bytes 884744 | tf_op jit(solution)/shard_map/ppermute | solution.py:361
  63.0 2.6 %collective-permute-start.14 = (f32[64,1152]{1,0:T(8,128)S(1)}, f32[64,1152]{1,0:T(8,128)S(1)}, u32[]{:S(2)}, u32[]{:S(2)}) collective-permute-start(f32[64,1152]{1,0:T(8,128)S(1)} %gram_x.1._.refs_0_), channel_id=1, source_target_pairs={{0,2},{1,3},{2,0},{3,1},{4,6},{5,7},{6,4},{7,5},{8,10},{9,11},{10,... | collective-permute-start | bytes 884744 | tf_op jit(solution)/shard_map/ppermute | solution.py:361
  65.8 1.7 %collective-permute-start.11 = (f32[16,1024]{1,0:T(8,128)S(1)}, f32[16,1024]{1,0:T(8,128)S(1)}, u32[]{:S(2)}, u32[]{:S(2)}) collective-permute-start(f32[16,1024]{1,0:T(8,128)S(1)} %get-tuple-element.41), channel_id=1, source_target_pairs={{0,64},{1,65},{2,66},{3,67},{4,68},{5,69},{6,70},{7,71},{8,72},{9,... | collective-permute-start | bytes 196616 | tf_op jit(solution)/shard_map/ppermute | solution.py:361
  67.4 2.8 %collective-permute-done.8._.refs_1_ = f32[64,1152]{1,0:T(8,128)S(1)} collective-permute-done((f32[64,1152]{1,0:T(8,128)S(1)}, f32[64,1152]{1,0:T(8,128)S(1)}, u32[]{:S(2)}, u32[]{:S(2)}) %collective-permute-start.8) | collective-permute-done | bytes 294944 | tf_op jit(solution)/shard_map/ppermute | solution.py:361
  70.2 0.5 collective-permute-start.12
  70.8 0.3 collective-permute-done.11.refs_2_
  71.1 3.7 %collective-permute-done.12.refs_3_ = f32[16,1024]{1,0:T(8,128)S(1)} collective-permute-done((f32[16,1024]{1,0:T(8,128)S(1)}, f32[16,1024]{1,0:T(8,128)S(1)}, u32[]{:S(2)}, u32[]{:S(2)}) %collective-permute-start.12) | collective-permute-done | bytes 65568 | tf_op jit(solution)/shard_map/ppermute | solution.py:361
  74.9 2.4 %collective-permute-start.13 = (f32[16,1024]{1,0:T(8,128)S(1)}, f32[16,1024]{1,0:T(8,128)S(1)}, u32[]{:S(2)}, u32[]{:S(2)}) collective-permute-start(f32[16,1024]{1,0:T(8,128)S(1)} %sum_x.1.refs_1_), channel_id=1, source_target_pairs={{0,16},{1,17},{2,18},{3,19},{4,20},{5,21},{6,22},{7,23},{8,24},{9,... | collective-permute-start | bytes 196616 | tf_op jit(solution)/shard_map/ppermute | solution.py:361
  77.4 2.6 %reorder.1.refs_0_.refs_6_ = f32[128,4608]{1,0:T(8,128)S(1)} custom-call(bf16[128,128]{1,0:T(8,128)(2,1)S(1)} %fusion.2.order_ref, f32[128,4608]{1,0:T(8,128)S(1)} %bitcast.10), custom_call_target="tpu_custom_call" | custom-call | flops 452984832 | bytes 9437184 | tf_op jit(solution)/shard_map/reorder/pallas_call | solution.py:462
  80.0 1.0 collective-permute-done.15.refs_3_
  81.1 2.2 %collective-permute-start.16 = (f32[256,1152]{1,0:T(8,128)S(1)}, f32[256,1152]{1,0:T(8,128)S(1)}, u32[]{:S(2)}, u32[]{:S(2)}) collective-permute-start(f32[256,1152]{1,0:T(8,128)S(1)} %gram_y.1.refs_0_), channel_id=1, source_target_pairs={{0,8},{1,9},{2,10},{3,11},{4,12},{5,13},{6,14},{7,15},{8,0},{9,1},... | collective-permute-start | bytes 3538952 | tf_op jit(solution)/shard_map/ppermute | solution.py:361
  83.3 1.7 %collective-permute-start.18 = (f32[16,1024]{1,0:T(8,128)S(1)}, f32[16,1024]{1,0:T(8,128)S(1)}, u32[]{:S(2)}, u32[]{:S(2)}) collective-permute-start(f32[16,1024]{1,0:T(8,128)S(1)} %sum_z.1._.refs_0_), channel_id=1, source_target_pairs={{0,64},{1,65},{2,66},{3,67},{4,68},{5,69},{6,70},{7,71},{8,72},{9,... | collective-permute-start | bytes 196616 | tf_op jit(solution)/shard_map/ppermute | solution.py:361
  85.0 2.2 %collective-permute-start.19 = (f32[16,1024]{1,0:T(8,128)S(1)}, f32[16,1024]{1,0:T(8,128)S(1)}, u32[]{:S(2)}, u32[]{:S(2)}) collective-permute-start(f32[16,1024]{1,0:T(8,128)S(1)} %sum_z.1._.refs_0_), channel_id=1, source_target_pairs={{0,96},{1,97},{2,98},{3,99},{4,100},{5,101},{6,102},{7,103},{8,104... | collective-permute-start | bytes 196616 | tf_op jit(solution)/shard_map/ppermute | solution.py:361
  87.2 4.4 %inverse_blocks.1 = (f32[1024,1024]{1,0:T(8,128)S(1)}, f32[8,128,128]{2,1,0:T(8,128)S(1)}) custom-call(s32[4]{0:T(128)S(1)} %pad_add_fusion.place_ref, f32[256,1152]{1,0:T(8,128)S(1)} %gram_y.1.refs_0_, f32[256,1152]{1,0:T(8,128)S(1)} %collective-permute-done.16.refs_1_), custom_call_target="tpu_custom_call" | custom-call | flops 4294967296 | bytes 4194304 | tf_op jit(solution)/shard_map/inverse_blocks/pallas_call | solution.py:480
  91.6 1.0 collective-permute-start.20
  92.6 1.6 %inverse.1 = (bf16[1024,512]{1,0:T(8,128)(2,1)S(1)}, bf16[1024,512]{1,0:T(8,128)(2,1)S(1)}, bf16[512,512]{1,0:T(8,128)(2,1)S(1)}, bf16[512,512]{1,0:T(8,128)(2,1)S(1)}) custom-call(f32[1024,1024]{1,0:T(8,128)S(1)} %get-tuple-element.28.lower_ref, f32[8,128,128]{2,1,0:T(8,128)S(1)} %get-tuple-element.27._.blocks_ref), custom_call_target="tpu_custom_call" | custom-call | flops 4294967296 | bytes 4194304 | tf_op jit(solution)/shard_map/inverse/pallas_call | solution.py:492
  94.2 8.2 %change.1 = f32[128,4608]{1,0:T(8,128)} custom-call(s32[4]{0:T(128)S(1)} %pad_add_fusion.place_ref, bf16[128,128]{1,0:T(8,128)(2,1)S(1)} %fusion.2.order_ref, f32[64,1024]{1,0:T(8,128)S(1)} %sum_join.1.refs_0_, f32[64,1024]{1,0:T(8,128)S(1)} %collective-permute-done.20.refs_1_, bf16[1024,512]{1,0:T(8,128)(2,1)S(1)} %get-tuple-element.29.refs_2_, ...), custom_call_target="tpu_custom_call" | custom-call | flops 3623878656 | bytes 2359296 | tf_op jit(solution)/shard_map/change/pallas_call | solution.py:503
  (40 shorter events, 0.8 us)
Async XLA Ops:
  0.0 9.3 %copy-start = (s32[16]{0:T(128)S(1)}, s32[16]{0:T(128)}, u32[]{:S(2)}) copy-start(s32[16]{0:T(128)} %param.7) | copy-start | bytes 196
  0.0 45.6 %all-to-all-start = ((f32[16,8,4608]{2,1,0:T(8,128)}), f32[16,8,4608]{2,1,0:T(8,128)S(1)}, u32[]{:S(2)}, u32[]{:S(2)}) async-start(f32[16,8,4608]{2,1,0:T(8,128)} %bitcast.11), calls=%async_computation | async-start | bytes 4718592 | tf_op jit(solution)/shard_map/all_to_all | solution.py:401
  29.4 1.7 %collective-permute-start = (f32[64,1152]{1,0:T(8,128)S(1)}, f32[64,1152]{1,0:T(8,128)S(1)}, u32[]{:S(2)}, u32[]{:S(2)}) collective-permute-start(f32[64,1152]{1,0:T(8,128)S(1)} %get-tuple-element.22), channel_id=1, source_target_pairs={{0,8},{1,9},{2,10},{3,11},{4,12},{5,13},{6,14},{7,15},{8,0},{9,1},... | collective-permute-start | bytes 884744 | tf_op jit(solution)/shard_map/ppermute | solution.py:361
  31.1 12.5 %collective-permute-start.1 = (f32[16,1152]{1,0:T(8,128)S(1)}, f32[16,1152]{1,0:T(8,128)S(1)}, u32[]{:S(2)}, u32[]{:S(2)}) collective-permute-start(f32[16,1152]{1,0:T(8,128)S(1)} %get-tuple-element.37), channel_id=1, source_target_pairs={{0,64},{1,65},{2,66},{3,67},{4,68},{5,69},{6,70},{7,71},{8,72},{9,... | collective-permute-start | bytes 221192 | tf_op jit(solution)/shard_map/ppermute | solution.py:361
  34.1 11.4 %collective-permute-start.2 = (f32[16,1152]{1,0:T(8,128)S(1)}, f32[16,1152]{1,0:T(8,128)S(1)}, u32[]{:S(2)}, u32[]{:S(2)}) collective-permute-start(f32[16,1152]{1,0:T(8,128)S(1)} %get-tuple-element.39), channel_id=1, source_target_pairs={{0,96},{1,97},{2,98},{3,99},{4,100},{5,101},{6,102},{7,103},{8,104... | collective-permute-start | bytes 221192 | tf_op jit(solution)/shard_map/ppermute | solution.py:361
  35.0 10.5 %collective-permute-start.3 = (f32[16,1152]{1,0:T(8,128)S(1)}, f32[16,1152]{1,0:T(8,128)S(1)}, u32[]{:S(2)}, u32[]{:S(2)}) collective-permute-start(f32[16,1152]{1,0:T(8,128)S(1)} %get-tuple-element.38), channel_id=1, source_target_pairs={{0,32},{1,33},{2,34},{3,35},{4,36},{5,37},{6,38},{7,39},{8,40},{9,... | collective-permute-start | bytes 221192 | tf_op jit(solution)/shard_map/ppermute | solution.py:361
  45.5 4.9 %collective-permute-start.4 = (f32[16,1152]{1,0:T(8,128)S(1)}, f32[16,1152]{1,0:T(8,128)S(1)}, u32[]{:S(2)}, u32[]{:S(2)}) collective-permute-start(f32[16,1152]{1,0:T(8,128)S(1)} %fusion.1._.refs_1_), channel_id=1, source_target_pairs={{0,16},{1,17},{2,18},{3,19},{4,20},{5,21},{6,22},{7,23},{8,24},{9,... | collective-permute-start | bytes 221192 | tf_op jit(solution)/shard_map/ppermute | solution.py:361
  50.4 20.3 %copy-start.1 = (s32[128]{0:T(128)S(1)}, s32[128]{0:T(128)}, u32[]{:S(2)}) copy-start(s32[128]{0:T(128)} %param.5) | copy-start | bytes 1540
  50.4 8.7 %collective-permute-start.5 = (f32[16,1152]{1,0:T(8,128)S(1)}, f32[16,1152]{1,0:T(8,128)S(1)}, u32[]{:S(2)}, u32[]{:S(2)}) collective-permute-start(f32[16,1152]{1,0:T(8,128)S(1)} %gram_z.1._.refs_0_), channel_id=1, source_target_pairs={{0,32},{1,33},{2,34},{3,35},{4,36},{5,37},{6,38},{7,39},{8,40},{9,... | collective-permute-start | bytes 221192 | tf_op jit(solution)/shard_map/ppermute | solution.py:361
  50.5 8.6 %collective-permute-start.6 = (f32[16,1152]{1,0:T(8,128)S(1)}, f32[16,1152]{1,0:T(8,128)S(1)}, u32[]{:S(2)}, u32[]{:S(2)}) collective-permute-start(f32[16,1152]{1,0:T(8,128)S(1)} %gram_z.1._.refs_0_), channel_id=1, source_target_pairs={{0,64},{1,65},{2,66},{3,67},{4,68},{5,69},{6,70},{7,71},{8,72},{9,... | collective-permute-start | bytes 221192 | tf_op jit(solution)/shard_map/ppermute | solution.py:361
  51.6 7.5 %collective-permute-start.7 = (f32[16,1152]{1,0:T(8,128)S(1)}, f32[16,1152]{1,0:T(8,128)S(1)}, u32[]{:S(2)}, u32[]{:S(2)}) collective-permute-start(f32[16,1152]{1,0:T(8,128)S(1)} %gram_z.1._.refs_0_), channel_id=1, source_target_pairs={{0,96},{1,97},{2,98},{3,99},{4,100},{5,101},{6,102},{7,103},{8,104... | collective-permute-start | bytes 221192 | tf_op jit(solution)/shard_map/ppermute | solution.py:361
  59.2 6.4 %collective-permute-start.9 = (f32[64,1024]{1,0:T(8,128)S(1)}, f32[64,1024]{1,0:T(8,128)S(1)}, u32[]{:S(2)}, u32[]{:S(2)}) collective-permute-start(f32[64,1024]{1,0:T(8,128)S(1)} %sum_split.1), channel_id=1, source_target_pairs={{0,8},{1,9},{2,10},{3,11},{4,12},{5,13},{6,14},{7,15},{8,0},{9,1},... | collective-permute-start | bytes 786440 | tf_op jit(solution)/shard_map/ppermute | solution.py:361
  61.7 8.6 %collective-permute-start.8 = (f32[64,1152]{1,0:T(8,128)S(1)}, f32[64,1152]{1,0:T(8,128)S(1)}, u32[]{:S(2)}, u32[]{:S(2)}) collective-permute-start(f32[64,1152]{1,0:T(8,128)S(1)} %gram_x.1._.refs_0_), channel_id=1, source_target_pairs={{0,1},{1,0},{2,3},{3,2},{4,5},{5,4},{6,7},{7,6},{8,9},{9,8},{10,11... | collective-permute-start | bytes 884744 | tf_op jit(solution)/shard_map/ppermute | solution.py:361
  63.0 17.0 %collective-permute-start.14 = (f32[64,1152]{1,0:T(8,128)S(1)}, f32[64,1152]{1,0:T(8,128)S(1)}, u32[]{:S(2)}, u32[]{:S(2)}) collective-permute-start(f32[64,1152]{1,0:T(8,128)S(1)} %gram_x.1._.refs_0_), channel_id=1, source_target_pairs={{0,2},{1,3},{2,0},{3,1},{4,6},{5,7},{6,4},{7,5},{8,10},{9,11},{10,... | collective-permute-start | bytes 884744 | tf_op jit(solution)/shard_map/ppermute | solution.py:361
  65.6 15.4 %collective-permute-start.15 = (f32[64,1152]{1,0:T(8,128)S(1)}, f32[64,1152]{1,0:T(8,128)S(1)}, u32[]{:S(2)}, u32[]{:S(2)}) collective-permute-start(f32[64,1152]{1,0:T(8,128)S(1)} %gram_x.1._.refs_0_), channel_id=1, source_target_pairs={{0,3},{1,2},{2,1},{3,0},{4,7},{5,6},{6,5},{7,4},{8,11},{9,10},{10,... | collective-permute-start | bytes 884744 | tf_op jit(solution)/shard_map/ppermute | solution.py:361
  65.7 5.1 %collective-permute-start.10 = (f32[16,1024]{1,0:T(8,128)S(1)}, f32[16,1024]{1,0:T(8,128)S(1)}, u32[]{:S(2)}, u32[]{:S(2)}) collective-permute-start(f32[16,1024]{1,0:T(8,128)S(1)} %get-tuple-element.42), channel_id=1, source_target_pairs={{0,32},{1,33},{2,34},{3,35},{4,36},{5,37},{6,38},{7,39},{8,40},{9,... | collective-permute-start | bytes 196616 | tf_op jit(solution)/shard_map/ppermute | solution.py:361
  65.8 5.4 %collective-permute-start.11 = (f32[16,1024]{1,0:T(8,128)S(1)}, f32[16,1024]{1,0:T(8,128)S(1)}, u32[]{:S(2)}, u32[]{:S(2)}) collective-permute-start(f32[16,1024]{1,0:T(8,128)S(1)} %get-tuple-element.41), channel_id=1, source_target_pairs={{0,64},{1,65},{2,66},{3,67},{4,68},{5,69},{6,70},{7,71},{8,72},{9,... | collective-permute-start | bytes 196616 | tf_op jit(solution)/shard_map/ppermute | solution.py:361
  70.2 4.6 %collective-permute-start.12 = (f32[16,1024]{1,0:T(8,128)S(1)}, f32[16,1024]{1,0:T(8,128)S(1)}, u32[]{:S(2)}, u32[]{:S(2)}) collective-permute-start(f32[16,1024]{1,0:T(8,128)S(1)} %get-tuple-element.40), channel_id=1, source_target_pairs={{0,96},{1,97},{2,98},{3,99},{4,100},{5,101},{6,102},{7,103},{8,104... | collective-permute-start | bytes 196616 | tf_op jit(solution)/shard_map/ppermute | solution.py:361
  74.9 5.1 %collective-permute-start.13 = (f32[16,1024]{1,0:T(8,128)S(1)}, f32[16,1024]{1,0:T(8,128)S(1)}, u32[]{:S(2)}, u32[]{:S(2)}) collective-permute-start(f32[16,1024]{1,0:T(8,128)S(1)} %sum_x.1.refs_1_), channel_id=1, source_target_pairs={{0,16},{1,17},{2,18},{3,19},{4,20},{5,21},{6,22},{7,23},{8,24},{9,... | collective-permute-start | bytes 196616 | tf_op jit(solution)/shard_map/ppermute | solution.py:361
  81.1 6.1 %collective-permute-start.16 = (f32[256,1152]{1,0:T(8,128)S(1)}, f32[256,1152]{1,0:T(8,128)S(1)}, u32[]{:S(2)}, u32[]{:S(2)}) collective-permute-start(f32[256,1152]{1,0:T(8,128)S(1)} %gram_y.1.refs_0_), channel_id=1, source_target_pairs={{0,8},{1,9},{2,10},{3,11},{4,12},{5,13},{6,14},{7,15},{8,0},{9,1},... | collective-permute-start | bytes 3538952 | tf_op jit(solution)/shard_map/ppermute | solution.py:361
  83.3 8.2 %collective-permute-start.17 = (f32[16,1024]{1,0:T(8,128)S(1)}, f32[16,1024]{1,0:T(8,128)S(1)}, u32[]{:S(2)}, u32[]{:S(2)}) collective-permute-start(f32[16,1024]{1,0:T(8,128)S(1)} %sum_z.1._.refs_0_), channel_id=1, source_target_pairs={{0,32},{1,33},{2,34},{3,35},{4,36},{5,37},{6,38},{7,39},{8,40},{9,... | collective-permute-start | bytes 196616 | tf_op jit(solution)/shard_map/ppermute | solution.py:361
  83.3 8.3 %collective-permute-start.18 = (f32[16,1024]{1,0:T(8,128)S(1)}, f32[16,1024]{1,0:T(8,128)S(1)}, u32[]{:S(2)}, u32[]{:S(2)}) collective-permute-start(f32[16,1024]{1,0:T(8,128)S(1)} %sum_z.1._.refs_0_), channel_id=1, source_target_pairs={{0,64},{1,65},{2,66},{3,67},{4,68},{5,69},{6,70},{7,71},{8,72},{9,... | collective-permute-start | bytes 196616 | tf_op jit(solution)/shard_map/ppermute | solution.py:361
  85.0 6.6 %collective-permute-start.19 = (f32[16,1024]{1,0:T(8,128)S(1)}, f32[16,1024]{1,0:T(8,128)S(1)}, u32[]{:S(2)}, u32[]{:S(2)}) collective-permute-start(f32[16,1024]{1,0:T(8,128)S(1)} %sum_z.1._.refs_0_), channel_id=1, source_target_pairs={{0,96},{1,97},{2,98},{3,99},{4,100},{5,101},{6,102},{7,103},{8,104... | collective-permute-start | bytes 196616 | tf_op jit(solution)/shard_map/ppermute | solution.py:361
  91.6 2.6 %collective-permute-start.20 = (f32[64,1024]{1,0:T(8,128)S(1)}, f32[64,1024]{1,0:T(8,128)S(1)}, u32[]{:S(2)}, u32[]{:S(2)}) collective-permute-start(f32[64,1024]{1,0:T(8,128)S(1)} %sum_join.1.refs_0_), channel_id=1, source_target_pairs={{0,8},{1,9},{2,10},{3,11},{4,12},{5,13},{6,14},{7,15},{8,0},{9,1},... | collective-permute-start | bytes 786440 | tf_op jit(solution)/shard_map/ppermute | solution.py:361
